TPU v7x, 32 devices: a whole 2x2x4 slice. The times are simulated.
32 devices in a mesh: gx: 8 (over z, y), gy: 4 (over x, core).
Axes of the slice: x: 2, y: 2, z: 4, core: 2. Of those that a mesh axis runs over, the one named last changes fastest.
Arguments:
- mass_per_volume: float32 [64, 512, 32], P('gx', 'gy'), may hold values from 0.5 to 2
- momentum: float32 [3, 64, 512, 32], P(None, 'gx', 'gy'), may hold values from -0.9 to 0.9
- energy: float32 [64, 512, 32], P('gx', 'gy'), may hold values from 3 to 8
Outputs:
- tendency: float32 [5, 64, 512, 32], P(None, 'gx', 'gy')
- advanced: float32 [5, 64, 512, 32], P(None, 'gx', 'gy')
All inputs are finite; a program needn't handle non-finite values.
Results may differ from a plain program's by a relative error of at most 0.00016.
Values sent between devices are 32-bit elements; how exact they have to be, the bound alone decides.
No kernel may reach another device: no remote copies, remote signals or barrier semaphores. Data moves between devices by JAX's collectives and lax.ppermute only.
A program may use at most 64 MiB of HBM per device.

v0:
```python
import functools

import jax
import jax.numpy as jnp
import numpy as np
from jax import lax
from jax.experimental import pallas as pl
from jax.experimental.pallas import tpu as pltpu
from jax.sharding import PartitionSpec as P

CX = 8
CY = 8
NZ = 512
HALO = 4


heat_ratio = 1.4
shear_resistance_reference = 0.08
sutherland_power_law = 0.7
prandtl = 0.72
section_step = 0.05
compact_alpha = 1.0 / 3.0
compact_near = 14.0 / 9.0
compact_far = 1.0 / 9.0

conduction = heat_ratio / ((heat_ratio - 1.0) * prandtl)
enthalpy = heat_ratio / (heat_ratio - 1.0)


def tridiagonal_inverse_product(length, stencil):
    solved = np.array(stencil)
    upper_ratio = np.zeros(length)
    for row_index in range(length):
        if row_index == 0:
            pivot_value = 1.0
            solved[row_index] = solved[row_index] / pivot_value
        else:
            pivot_value = 1.0 - compact_alpha * upper_ratio[row_index - 1]
            solved[row_index] = (
                solved[row_index] - compact_alpha * solved[row_index - 1]
            ) / pivot_value
        upper_ratio[row_index] = compact_alpha / pivot_value
    for row_index in range(length - 2, -1, -1):
        solved[row_index] = solved[row_index] - upper_ratio[row_index] * solved[row_index + 1]
    return solved


def exact_compact_matrix(block_size, margin):
    length = block_size + 2 * margin
    stencil = compact_near / 2.0 * (np.eye(length, k=1) - np.eye(length, k=-1))
    stencil = stencil + compact_far / 4.0 * (np.eye(length, k=2) - np.eye(length, k=-2))
    inverse_product = tridiagonal_inverse_product(length, stencil)
    return inverse_product[margin : margin + block_size]


def compact_matrix(block_size, margin):
    return exact_compact_matrix(block_size, margin).astype(np.float32)


def pitch_matrix(total, block_size):
    matrix = compact_matrix(block_size, HALO)
    result = np.zeros((total, total), np.float32)
    rows_all = np.arange(total)
    block_start = rows_all // block_size * block_size
    for offset in range(block_size + 2 * HALO):
        columns = (block_start - HALO + offset) % total
        result[rows_all, columns] += matrix[rows_all % block_size, offset]
    return result


def span_matrix(total):
    offsets = np.arange(total)[:, None] - np.arange(total)[None, :]
    angles = np.pi * offsets / total
    signs = np.where(offsets % 2 == 0, 1.0, -1.0)
    sines = np.where(offsets == 0, 1.0, np.sin(angles))
    result = np.where(offsets == 0, 0.0, np.pi / total * signs * np.cos(angles) / sines)
    return result.astype(np.float32)


F32 = jnp.float32
BF16 = jnp.bfloat16
U, W, V, T, R = range(5)
PLACES = (0, 2, 1, 3)
HALF = CX // 2


def halves(matrix):
    high = np.asarray(matrix, np.float32).astype(BF16)
    low = (matrix - high.astype(np.float32)).astype(BF16)
    return jnp.asarray(high), jnp.asarray(low)


def span_blocks(length, sources, targets):
    width = length // 4
    matrix = span_matrix(length).T
    both = []
    for core in range(2):
        columns = []
        for target in targets:
            to = core ^ target
            columns.append(
                np.concatenate(
                    [
                        matrix[
                            (core ^ source) * width : (core ^ source) * width + width,
                            to * width : to * width + width,
                        ]
                        for source in sources
                    ],
                    axis=0,
                )
            )
        both.append(np.concatenate(columns, axis=1))
    return halves(np.stack(both))


def halo_basis():
    matrix = exact_compact_matrix(CX, HALO)
    left = matrix[:, :HALO]
    basis = np.linalg.svd(left)[2][:2]
    inner = left @ basis.T
    outer = -inner[::-1]
    return basis, np.concatenate(
        [inner, matrix[:, HALO : HALO + CX], outer[:, ::-1]], axis=1
    )


def split(values):
    high = values.astype(BF16)
    low = (values - high.astype(F32)).astype(BF16)
    return high, low


def dot(a, b):
    return jnp.dot(a, b, preferred_element_type=F32)


def right_product(values, matrix_high, matrix_low):
    high, low = split(values)
    return dot(high, matrix_high) + dot(low, matrix_high) + dot(high, matrix_low)


def left_product(matrix_high, matrix_low, values):
    high, low = split(values)
    return dot(matrix_high, high) + dot(matrix_high, low) + dot(matrix_low, high)


def compact_x(planes):
    matrix = halo_basis()[1]
    length = CX + 4
    half = length // 2
    odd = [planes[l] - planes[length - 1 - l] for l in range(half)]
    even = [planes[l] + planes[length - 1 - l] for l in range(half)]
    result = [None] * CX
    for i in range(HALF):
        first = None
        second = None
        for l in range(half):
            a = float(0.5 * (matrix[i, l] - matrix[i, length - 1 - l]))
            b = float(0.5 * (matrix[i, l] + matrix[i, length - 1 - l]))
            first = a * odd[l] if first is None else first + a * odd[l]
            second = b * even[l] if second is None else second + b * even[l]
        result[i] = first + second
        result[CX - 1 - i] = first - second
    return result


def extended(before, own, after, f, rows):
    return (
        [before[f, 0, rows, :], before[f, 1, rows, :]]
        + [own[f, l, rows, :] for l in range(CX)]
        + [after[f, 1, rows, :], after[f, 0, rows, :]]
    )


def halo_sums(values, f, rows, up, down):
    basis = halo_basis()[0]
    for k in range(2):
        top = None
        bottom = None
        for l in range(HALO):
            a = float(basis[k, l]) * values[f, CX - HALO + l, rows, :]
            b = float(basis[k, l]) * values[f, HALO - 1 - l, rows, :]
            top = a if top is None else top + a
            bottom = b if bottom is None else bottom + b
        up[f, k, rows, :] = top
        down[f, k, rows, :] = bottom


def row_chunks(rows):
    return [slice(start, start + 8) for start in range(0, rows, 8)]


def flat(values):
    return values.reshape(-1, values.shape[-1])


def kernel_primitives(
    rho_in, mom_in, ene_in, conserved, own, first, up, down, arrived
):
    rho = conserved.at[0]
    mom = conserved.at[1:4]
    ene = conserved.at[4]
    copies = [
        pltpu.make_async_copy(source, target, arrived.at[k])
        for k, (source, target) in enumerate(((rho_in, rho), (mom_in, mom), (ene_in, ene)))
    ]
    for copy in copies:
        copy.start()
    for copy in copies:
        copy.wait()

    def plane(x, carry):
        density = rho[x]
        inverse = 1.0 / density
        u = mom[0, x] * inverse
        v = mom[1, x] * inverse
        w = mom[2, x] * inverse
        kinetic = 0.5 * (mom[0, x] * u + mom[1, x] * v + mom[2, x] * w)
        temperature = (heat_ratio - 1.0) * (ene[x] - kinetic) * inverse
        own[U, x] = u
        own[W, x] = w
        own[V, x] = v
        own[T, x] = temperature
        first[0, x] = u
        first[1, x] = w
        return carry

    lax.fori_loop(0, CX, plane, 0)

    def sums(f, carry):
        for rows in row_chunks(rho.shape[1]):
            halo_sums(own, f, rows, up, down)
        return carry

    lax.fori_loop(0, 4, sums, 0)


def kernel_pitch_gradients(
    own, conserved, y_high, y_low, dy, mu, second, mate_a, mate_b
):
    for f in range(4):
        dy[f] = left_product(y_high[...], y_low[...], flat(own[f])).reshape(own.shape[1:])

    def plane(x, carry):
        mu[x] = shear_resistance_reference * jnp.exp(
            sutherland_power_law * jnp.log(own[T, x])
        )
        for f in range(2):
            mate_a[f, x] = own[f, x]
            mate_b[f, x] = own[V + f, x]
        second[0, x] = own[V, x]
        second[1, x] = own[T, x]
        second[2, x] = conserved[0, x]
        return carry

    lax.fori_loop(0, CX, plane, 0)


def kernel_stream_gradients(own, before, after, mu, dx, third):
    def field(f, carry):
        for rows in row_chunks(own.shape[2]):
            derived = compact_x(extended(before, own, after, f, rows))
            for x in range(CX):
                dx[f, x, rows, :] = derived[x]
        return carry

    lax.fori_loop(0, 4, field, 0)

    def plane(x, carry):
        third[0, x] = (2.0 / 3.0) * mu[x] * dx[U, x]
        third[1, x] = mu[x] * dx[W, x]
        return carry

    lax.fori_loop(0, CX, plane, 0)


def kernel_flux_x(
    own, second, peer_first, first_mate, across_first, dx, dy, mu, z_high, z_low,
    dz, flux, up, down,
):
    width = own.shape[-1]
    odd = lax.rem(lax.axis_index("gy"), 2)
    for f in range(2):
        values = jnp.concatenate(
            [flat(own[f]), flat(peer_first[f]), flat(first_mate[f]), flat(across_first[f])], axis=1
        )
        dz[f] = right_product(values, z_high[odd], z_low[odd])

    rows = own.shape[2]

    def plane(x, carry):
        at = pl.ds(pl.multiple_of(x * rows, rows), rows)
        u, w, v, t = (own[f, x] for f in range(4))
        density = second[2, x]
        viscosity = mu[x]
        dil = dx[U, x] + dy[V, x] + dz[1, at, :width]
        s1 = viscosity * (2.0 * dx[U, x] - (2.0 / 3.0) * dil)
        s2 = viscosity * (dx[V, x] + dy[U, x])
        s3 = viscosity * (dx[W, x] + dz[0, at, :width])
        m = density * u
        total = m * (enthalpy * t + 0.5 * (u * u + v * v + w * w))
        flux[0, x] = m
        flux[1, x] = m * u + density * t - s1
        flux[2, x] = m * v - s2
        flux[3, x] = m * w - s3
        flux[4, x] = total - (s1 * u + s2 * v + s3 * w) - conduction * viscosity * dx[T, x]
        return carry

    lax.fori_loop(0, CX, plane, 0)

    def sums(f, carry):
        for chunk in row_chunks(rows):
            halo_sums(flux, f, chunk, up, down)
        return carry

    lax.fori_loop(0, 5, sums, 0)


def kernel_peer(peer_first, peer_second, flux, y_high, y_low, for_v, for_t, dy_peer):
    for_v[...] = peer_second[0]
    for_t[...] = peer_second[1]
    dy_peer[0] = left_product(y_high[...], y_low[...], flat(peer_second[0]))
    dy_peer[1] = left_product(y_high[...], y_low[...], flat(peer_first[1]))


def kernel_flux_yz(
    own, second, peer_first, peer_second, second_mate, across_v, across_t, dy_peer,
    dz, dx, dy, mu, y_high, y_low, z_high, z_low, f_high, f_low, part, part_mate,
    dz_more, flux, flux_y,
):
    rows, width = own.shape[2:]
    odd = lax.rem(lax.axis_index("gy"), 2)
    for f, across in enumerate((across_v, across_t)):
        values = jnp.concatenate(
            [flat(own[V + f]), flat(peer_second[f]), flat(second_mate[f]), flat(across[...])],
            axis=1,
        )
        dz_more[f] = right_product(values, z_high[odd], z_low[odd])

    def span_flux(at, lanes, u, w, v, t, density, viscosity, yv, yw):
        s1 = viscosity * dz[0, at, lanes]
        s2 = viscosity * (dz_more[0, at, lanes] + yw)
        s3 = viscosity * ((4.0 / 3.0) * dz[1, at, lanes] - (2.0 / 3.0) * yv)
        m = density * w
        total = m * (enthalpy * t + 0.5 * (u * u + v * v + w * w))
        flux[0, at, lanes] = m
        flux[1, at, lanes] = m * u - s1
        flux[2, at, lanes] = m * v - s2
        flux[3, at, lanes] = m * w + density * t - s3
        flux[4, at, lanes] = (
            total
            - (s1 * u + s2 * v + s3 * w)
            - conduction * viscosity * dz_more[1, at, lanes]
        )

    def plane(x, carry):
        at = pl.ds(pl.multiple_of(x * rows, rows), rows)
        here = slice(0, width)
        u, w, v, t = (own[f, x] for f in range(4))
        density = second[2, x]
        viscosity = mu[x]
        span_flux(at, here, u, w, v, t, density, viscosity, dy[V, x], dy[W, x])
        dil = dx[U, x] + dy[V, x] + dz[1, at, here]
        s1 = viscosity * (dy[U, x] + dx[V, x])
        s2 = viscosity * (2.0 * dy[V, x] - (2.0 / 3.0) * dil)
        s3 = viscosity * (dy[W, x] + dz_more[0, at, here])
        m = density * v
        total = m * (enthalpy * t + 0.5 * (u * u + v * v + w * w))
        flux_y[0, at, :] = m
        flux_y[1, at, :] = m * u - s1
        flux_y[2, at, :] = m * v + density * t - s2
        flux_y[3, at, :] = m * w - s3
        flux_y[4, at, :] = (
            total - (s1 * u + s2 * v + s3 * w) - conduction * viscosity * dy[T, x]
        )
        t = peer_second[1, x]
        viscosity = shear_resistance_reference * jnp.exp(sutherland_power_law * jnp.log(t))
        span_flux(
            at, slice(width, 2 * width), peer_first[0, x], peer_first[1, x],
            peer_second[0, x], t, peer_second[2, x], viscosity,
            dy_peer[0, at, :], dy_peer[1, at, :],
        )
        return carry

    lax.fori_loop(0, CX, plane, 0)
    shape = own.shape[1:]
    for f in range(5):
        spread = right_product(flux[f], f_high[odd], f_low[odd])
        local = left_product(y_high[...], y_low[...], flux_y[f])
        part[f] = (spread[:, :width] + local).reshape(shape)
        part_mate[f] = spread[:, width:].reshape(shape)


def kernel_corrections(
    own, peer_first, third, peer_third, part, part_mate, f_high, f_low, total, *for_mate
):
    width = own.shape[-1]
    odd = lax.rem(lax.axis_index("gy"), 2)
    shape = own.shape[1:]
    for f in (0, 2):
        total[f] = part[f]
        for_mate[f][...] = part_mate[f]
    pairs = ((own, third), (peer_first, peer_third))
    for f in (1, 3, 4):
        sides = []
        for speeds, shared in pairs:
            if f == 1:
                value = -shared[1]
            elif f == 3:
                value = shared[0]
            else:
                value = shared[0] * speeds[W] - shared[1] * speeds[U]
            sides.append(flat(value))
        spread = right_product(jnp.concatenate(sides, axis=1), f_high[odd], f_low[odd])
        total[f] = part[f] + spread[:, :width].reshape(shape)
        for_mate[f][...] = part_mate[f] + spread[:, width:].reshape(shape)


def kernel_finish(
    conserved, total, mate_0, mate_1, mate_2, mate_3, mate_4, flux, before, after,
    tendency, advanced,
):
    for f, from_mate in enumerate((mate_0, mate_1, mate_2, mate_3, mate_4)):
        for rows in row_chunks(flux.shape[2]):
            derived = compact_x(extended(before, flux, after, f, rows))
            for x in range(CX):
                value = -(total[f, x, rows, :] + from_mate[x, rows, :] + derived[x])
                tendency[f, x, rows, :] = value
                advanced[f, x, rows, :] = conserved[f, x, rows, :] + section_step * value


def call(kernel, outputs, operands, scratch=(), outside=False):
    space = pltpu.HBM if outside else pltpu.VMEM
    in_specs = [pl.BlockSpec(memory_space=space) for _ in operands]
    if outside:
        operands = [pltpu.with_memory_space_constraint(value, pltpu.HBM) for value in operands]
    touched = sum(value.size * value.dtype.itemsize for value in operands)
    touched += 4 * sum(int(np.prod(shape)) for shape in outputs)
    return pl.pallas_call(
        kernel,
        out_shape=[jax.ShapeDtypeStruct(shape, F32) for shape in outputs],
        in_specs=in_specs,
        out_specs=[pl.BlockSpec(memory_space=pltpu.VMEM) for _ in outputs],
        scratch_shapes=list(scratch),
        cost_estimate=pl.CostEstimate(flops=0, bytes_accessed=touched, transcendentals=0),
        compiler_params=pltpu.CompilerParams(vmem_limit_bytes=24 * 1024 * 1024),
    )(*operands)


def fast_device(mass_per_volume, momentum, energy):
    rho = jnp.transpose(mass_per_volume, (0, 2, 1))
    mom = jnp.transpose(momentum, (0, 1, 3, 2))
    ene = jnp.transpose(energy, (0, 2, 1))
    _, rows, width = rho.shape
    length = 4 * width
    z_high, z_low = span_blocks(length, PLACES, PLACES[:2])
    f_high, f_low = span_blocks(length, PLACES[:2], (0, 1))
    y_high, y_low = halves(np.kron(np.eye(CX, dtype=np.float32), pitch_matrix(rows, CY)))
    block = (CX, rows, width)
    sums = (2, rows, width)
    points = CX * rows
    devices = lax.axis_size("gx")
    ring_up = [(i, (i + 1) % devices) for i in range(devices)]
    ring_down = [(j, i) for i, j in ring_up]
    to_mate = [(i, i ^ 1) for i in range(4)]
    to_peer = [(i, i ^ 2) for i in range(4)]

    conserved, own, first, up, down = call(
        kernel_primitives,
        [(5,) + block, (4,) + block, (2,) + block, (4,) + sums, (4,) + sums],
        (rho, mom, ene),
        scratch=(pltpu.SemaphoreType.DMA((3,)),),
        outside=True,
    )
    peer_first = lax.ppermute(first, "gy", to_peer)
    before = lax.ppermute(up, "gx", ring_up)
    after = lax.ppermute(down, "gx", ring_down)
    dy, mu, second, mate_a, mate_b = call(
        kernel_pitch_gradients,
        [(4,) + block, block, (3,) + block, (2,) + block, (2,) + block],
        (own, conserved, y_high, y_low),
    )
    first_mate = lax.ppermute(mate_a, "gy", to_mate)
    second_mate = lax.ppermute(mate_b, "gy", to_mate)
    peer_second = lax.ppermute(second, "gy", to_peer)
    peer_first, before, after = lax.optimization_barrier((peer_first, before, after))
    across_first = lax.ppermute(peer_first, "gy", to_mate)
    dx, third = call(
        kernel_stream_gradients, [(4,) + block, (2,) + block], (own, before, after, mu)
    )
    peer_third = lax.ppermute(third, "gy", to_peer)
    dz, flux, flux_up, flux_down = call(
        kernel_flux_x,
        [(2, points, 2 * width), (5,) + block, (5,) + sums, (5,) + sums],
        (own, second, peer_first, first_mate, across_first, dx, dy, mu, z_high, z_low),
    )
    flux_before = lax.ppermute(flux_up, "gx", ring_up)
    flux_after = lax.ppermute(flux_down, "gx", ring_down)
    for_v, for_t, dy_peer = call(
        kernel_peer,
        [block, block, (2, points, width)],
        (peer_first, peer_second, flux, y_high, y_low),
    )
    across_v = lax.ppermute(for_v, "gy", to_mate)
    across_t = lax.ppermute(for_t, "gy", to_mate)
    part, part_mate = call(
        kernel_flux_yz,
        [(5,) + block, (5,) + block],
        (
            own, second, peer_first, peer_second, second_mate, across_v, across_t, dy_peer,
            dz, dx, dy, mu, y_high, y_low, z_high, z_low, f_high, f_low,
        ),
        scratch=(
            pltpu.VMEM((2, points, 2 * width), F32),
            pltpu.VMEM((5, points, 2 * width), F32),
            pltpu.VMEM((5, points, width), F32),
        ),
    )
    total, *for_mate = call(
        kernel_corrections,
        [(5,) + block] + 5 * [block],
        (own, peer_first, third, peer_third, part, part_mate, f_high, f_low),
    )
    from_mate = [lax.ppermute(value, "gy", to_mate) for value in for_mate]
    tendency, advanced = call(
        kernel_finish,
        [(5,) + block, (5,) + block],
        (conserved, total, *from_mate, flux, flux_before, flux_after),
    )
    return (
        jnp.transpose(tendency, (0, 1, 3, 2)),
        jnp.transpose(advanced, (0, 1, 3, 2)),
    )


def padded(array, sides, width):
    for axis, dim in sides:
        devices, length = (lax.axis_size(axis), array.shape[dim])
        up = [(i, (i + 1) % devices) for i in range(devices)]
        down = [(j, i) for i, j in up]
        last = lax.slice_in_dim(array, length - width, length, axis=dim)
        initial = lax.slice_in_dim(array, 0, width, axis=dim)
        before = lax.ppermute(last, axis, up)
        after = lax.ppermute(initial, axis, down)
        array = jnp.concatenate([before, array, after], axis=dim)
    return array


def right_side(conserved, gradients_of, derive_x, derive_y, derive_z):
    mass_per_volume = conserved[0]
    momentum = conserved[1:4]
    energy = conserved[4]
    local_speed_vector = momentum / mass_per_volume
    kinetic = 0.5 * jnp.sum(momentum * local_speed_vector, axis=0)
    normal_force_per_area = (heat_ratio - 1.0) * (energy - kinetic)
    thermal_state = normal_force_per_area / mass_per_volume
    basic_quantities = jnp.concatenate([local_speed_vector, thermal_state[None]], 0)
    gradients = gradients_of(basic_quantities)
    shear_resistance = shear_resistance_reference * jnp.power(thermal_state, sutherland_power_law)
    conductivity = shear_resistance * heat_ratio / ((heat_ratio - 1.0) * prandtl)
    dilatation = gradients[0][0] + gradients[1][1] + gradients[2][2]
    derivers = (derive_x, derive_y, derive_z)
    accumulated = None
    for direction in range(3):
        stress_column = [
            shear_resistance * (gradients[direction][component] + gradients[component][direction])
            for component in range(3)
        ]
        stress_column[direction] = (
            stress_column[direction] - 2.0 / 3.0 * shear_resistance * dilatation
        )
        fluxes = [momentum[direction]]
        for component in range(3):
            moment_flux = (
                momentum[component] * local_speed_vector[direction] - stress_column[component]
            )
            if component == direction:
                moment_flux = moment_flux + normal_force_per_area
            fluxes.append(moment_flux)
        work_term = (
            stress_column[0] * local_speed_vector[0]
            + stress_column[1] * local_speed_vector[1]
            + stress_column[2] * local_speed_vector[2]
        )
        fluxes.append(
            (energy + normal_force_per_area) * local_speed_vector[direction]
            - work_term
            - conductivity * gradients[direction][3]
        )
        divergence_part = derivers[direction](jnp.stack(fluxes))
        accumulated = divergence_part if accumulated is None else accumulated + divergence_part
    return -accumulated


def plain_device(mass_per_volume, momentum, energy):
    conserved = jnp.concatenate([mass_per_volume[None], momentum, energy[None]], 0)
    highest = lax.Precision.HIGHEST
    x_matrix = jnp.asarray(compact_matrix(CX, HALO))
    z_matrix = jnp.asarray(span_matrix(NZ))

    def apply_x(extended):
        return jnp.einsum("il,flab->fiab", x_matrix, extended, precision=highest)

    def flux_x(values):
        return apply_x(padded(values, (("gx", 1),), HALO))

    y_matrix = jnp.asarray(pitch_matrix(conserved.shape[3], CY))

    def apply_y(values):
        return jnp.einsum("fabk,jk->fabj", values, y_matrix, precision=highest)

    def derive_span(values):
        lines = jnp.transpose(
            lax.all_to_all(values, "gy", split_axis=3, concat_axis=2, tiled=True), (0, 1, 3, 2)
        )
        derived = jnp.einsum("fack,jk->facj", lines, z_matrix, precision=highest)
        returned = lax.all_to_all(derived, "gy", split_axis=3, concat_axis=2, tiled=True)
        return jnp.transpose(returned, (0, 1, 3, 2))

    def gradients_of(basic_quantities):
        extended = padded(basic_quantities, (("gx", 1),), HALO)
        return (apply_x(extended), apply_y(basic_quantities), derive_span(basic_quantities))

    tendency = right_side(conserved, gradients_of, flux_x, apply_y, derive_span)
    advanced = conserved + section_step * tendency
    return (tendency, advanced)


def per_device(mass_per_volume, momentum, energy):
    planes, width, rows = mass_per_volume.shape
    fits = planes == CX and width % 128 == 0 and rows <= 32 and rows % CY == 0
    if fits and lax.axis_size("gy") == 4:
        return fast_device(mass_per_volume, momentum, energy)
    return plain_device(mass_per_volume, momentum, energy)


def solution(mesh):
    in_specs = (P("gx", "gy", None), P(None, "gx", "gy", None), P("gx", "gy", None))
    out_specs = (P(None, "gx", "gy", None), P(None, "gx", "gy", None))
    return jax.shard_map(
        per_device, mesh=mesh, in_specs=in_specs, out_specs=out_specs, check_vma=False
    )
```

profile of v0, /device:TPU:0, one launch (start us, length us, event | category | flops | bytes accessed | tf_op | source)
XLA Modules:
  0.0 31.4 jit_solution(17884349495261324224)
XLA Ops:
  0.7 1.4 %shard_map.104 = (f32[5,8,32,128]{3,2,1,0:T(8,128)S(1)}, f32[4,8,32,128]{3,2,1,0:T(8,128)S(1)}, f32[2,8,32,128]{3,2,1,0:T(8,128)S(1)}, f32[4,2,32,128]{3,2,1,0:T(8,128)S(1)}, f32[4,2,32,128]{3,2,1,0:T(8,128)S(1)}) custom-call(f32[8,32,128]{2,1,0:T(8,128)} %bitcast.6, f32[3,8,32,128]{3,2,1,0:T(8,128)} %bitcast.5, f32[8,32,128]{2,1,0:T(8,128)} %bitcast.7), custom_call_target="tpu_custom_call" | custom-call | bytes 2359296 | tf_op jit(solution)/shard_map/pallas_call | solution.py:440
  2.1 3.0 %collective-permute-start = (f32[2,8,32,128]{3,2,1,0:T(8,128)S(1)}, f32[2,8,32,128]{3,2,1,0:T(8,128)S(1)}, u32[]{:S(2)}, u32[]{:S(2)}) collective-permute-start(f32[2,8,32,128]{3,2,1,0:T(8,128)S(1)} %get-tuple-element.36), channel_id=1, source_target_pairs={{0,2},{1,3},{2,0},{3,1},{4,6},{5,7},{6,4},{7,5},{8,10},{9,11},{10,... | collective-permute-start | bytes 786440 | tf_op jit(solution)/shard_map/ppermute | solution.py:476
  5.1 1.5 %collective-permute-start.1 = (f32[4,2,32,128]{3,2,1,0:T(8,128)S(1)}, f32[4,2,32,128]{3,2,1,0:T(8,128)S(1)}, u32[]{:S(2)}, u32[]{:S(2)}) collective-permute-start(f32[4,2,32,128]{3,2,1,0:T(8,128)S(1)} %get-tuple-element.37), channel_id=1, source_target_pairs={{0,4},{4,8},{8,12},{12,16},{16,20},{20,24},{24,28},{28,0},{1,5},{5... | collective-permute-start | bytes 393224 | tf_op jit(solution)/shard_map/ppermute | solution.py:477
  6.6 3.2 %collective-permute-start.2 = (f32[4,2,32,128]{3,2,1,0:T(8,128)S(1)}, f32[4,2,32,128]{3,2,1,0:T(8,128)S(1)}, u32[]{:S(2)}, u32[]{:S(2)}) collective-permute-start(f32[4,2,32,128]{3,2,1,0:T(8,128)S(1)} %get-tuple-element.38), channel_id=1, source_target_pairs={{4,0},{8,4},{12,8},{16,12},{20,16},{24,20},{28,24},{0,28},{5,1},{9... | collective-permute-start | bytes 393224 | tf_op jit(solution)/shard_map/ppermute | solution.py:478
  9.8 0.7 %shard_map.105 = (f32[4,8,32,128]{3,2,1,0:T(8,128)S(1)}, f32[8,32,128]{2,1,0:T(8,128)S(1)}, f32[3,8,32,128]{3,2,1,0:T(8,128)S(1)}, f32[2,8,32,128]{3,2,1,0:T(8,128)S(1)}, f32[2,8,32,128]{3,2,1,0:T(8,128)S(1)}) custom-call(f32[4,8,32,128]{3,2,1,0:T(8,128)S(1)} %get-tuple-element.35.own, f32[5,8,32,128]{3,2,1,0:T(8,128)S(1)} %get-tuple-element.34.conserved, ...), custom_call_target="tpu_custom_call" | custom-call | bytes 3014656 | tf_op jit(solution)/shard_map/pallas_call | solution.py:440
  10.5 0.4 %collective-permute-start.4 = (f32[3,8,32,128]{3,2,1,0:T(8,128)S(1)}, f32[3,8,32,128]{3,2,1,0:T(8,128)S(1)}, u32[]{:S(2)}, u32[]{:S(2)}) collective-permute-start(f32[3,8,32,128]{3,2,1,0:T(8,128)S(1)} %get-tuple-element.44.second), channel_id=1, source_target_pairs={{0,2},{1,3},{2,0},{3,1},{4,6},{5,7},{6,4},{7,5},{8,10},{9,11},{10,... | collective-permute-start | bytes 1179656 | tf_op jit(solution)/shard_map/ppermute | solution.py:486
  11.0 2.0 %collective-permute-done.1.before = f32[4,2,32,128]{3,2,1,0:T(8,128)S(1)} collective-permute-done((f32[4,2,32,128]{3,2,1,0:T(8,128)S(1)}, f32[4,2,32,128]{3,2,1,0:T(8,128)S(1)}, u32[]{:S(2)}, u32[]{:S(2)}) %collective-permute-start.1) | collective-permute-done | bytes 131104 | tf_op jit(solution)/shard_map/ppermute | solution.py:477
  12.9 1.3 %collective-permute-done.2.after = f32[4,2,32,128]{3,2,1,0:T(8,128)S(1)} collective-permute-done((f32[4,2,32,128]{3,2,1,0:T(8,128)S(1)}, f32[4,2,32,128]{3,2,1,0:T(8,128)S(1)}, u32[]{:S(2)}, u32[]{:S(2)}) %collective-permute-start.2) | collective-permute-done | bytes 131104 | tf_op jit(solution)/shard_map/ppermute | solution.py:478
  14.2 0.5 %collective-permute-start.5 = (f32[2,8,32,128]{3,2,1,0:T(8,128)S(1)}, f32[2,8,32,128]{3,2,1,0:T(8,128)S(1)}, u32[]{:S(2)}, u32[]{:S(2)}) collective-permute-start(f32[2,8,32,128]{3,2,1,0:T(8,128)S(1)} %get-tuple-element.45), channel_id=1, source_target_pairs={{0,1},{1,0},{2,3},{3,2},{4,5},{5,4},{6,7},{7,6},{8,9},{9,8},{10,11... | collective-permute-start | bytes 786440 | tf_op jit(solution)/shard_map/ppermute | solution.py:485
  14.7 0.3 %shard_map.106 = (f32[4,8,32,128]{3,2,1,0:T(8,128)S(1)}, f32[2,8,32,128]{3,2,1,0:T(8,128)S(1)}) custom-call(f32[4,8,32,128]{3,2,1,0:T(8,128)S(1)} %get-tuple-element.35.own, f32[4,2,32,128]{3,2,1,0:T(8,128)S(1)} %collective-permute-done.1.before, f32[4,2,32,128]{3,2,1,0:T(8,128)S(1)} %collective-permute-done.2.after, f32[8,32,128]{2,1,0:T(8,128)S(1)} %get-tuple-element.42.mu), custom_call_target="tpu_custom_call" | custom-call | bytes 1703936 | tf_op jit(solution)/shard_map/pallas_call | solution.py:440
  15.1 0.6 %collective-permute-start.3 = (f32[2,8,32,128]{3,2,1,0:T(8,128)S(1)}, f32[2,8,32,128]{3,2,1,0:T(8,128)S(1)}, u32[]{:S(2)}, u32[]{:S(2)}) collective-permute-start(f32[2,8,32,128]{3,2,1,0:T(8,128)S(1)} %get-tuple-element.43.third), channel_id=1, source_target_pairs={{0,2},{1,3},{2,0},{3,1},{4,6},{5,7},{6,4},{7,5},{8,10},{9,11},{10,... | collective-permute-start | bytes 786440 | tf_op jit(solution)/shard_map/ppermute | solution.py:492
  15.7 0.1 collective-permute-done.7.across_first
  15.8 0.9 %shard_map.107 = (f32[2,256,256]{2,1,0:T(8,128)S(1)}, f32[5,8,32,128]{3,2,1,0:T(8,128)S(1)}, f32[5,2,32,128]{3,2,1,0:T(8,128)S(1)}, f32[5,2,32,128]{3,2,1,0:T(8,128)S(1)}) custom-call(f32[4,8,32,128]{3,2,1,0:T(8,128)S(1)} %get-tuple-element.35.own, f32[3,8,32,128]{3,2,1,0:T(8,128)S(1)} %get-tuple-element.44.second, ...), custom_call_target="tpu_custom_call" | custom-call | bytes 5439488 | tf_op jit(solution)/shard_map/pallas_call | solution.py:440
  16.7 1.0 %collective-permute-start.15 = (f32[5,2,32,128]{3,2,1,0:T(8,128)S(1)}, f32[5,2,32,128]{3,2,1,0:T(8,128)S(1)}, u32[]{:S(2)}, u32[]{:S(2)}) collective-permute-start(f32[5,2,32,128]{3,2,1,0:T(8,128)S(1)} %get-tuple-element.62), channel_id=1, source_target_pairs={{0,4},{4,8},{8,12},{12,16},{16,20},{20,24},{24,28},{28,0},{1,5},{5... | collective-permute-start | bytes 491528 | tf_op jit(solution)/shard_map/ppermute | solution.py:498
  17.7 3.8 %collective-permute-start.16 = (f32[5,2,32,128]{3,2,1,0:T(8,128)S(1)}, f32[5,2,32,128]{3,2,1,0:T(8,128)S(1)}, u32[]{:S(2)}, u32[]{:S(2)}) collective-permute-start(f32[5,2,32,128]{3,2,1,0:T(8,128)S(1)} %get-tuple-element.63), channel_id=1, source_target_pairs={{4,0},{8,4},{12,8},{16,12},{20,16},{24,20},{28,24},{0,28},{5,1},{9... | collective-permute-start | bytes 491528 | tf_op jit(solution)/shard_map/ppermute | solution.py:499
  21.5 1.2 %collective-permute-done.4.peer_second = f32[3,8,32,128]{3,2,1,0:T(8,128)S(1)} collective-permute-done((f32[3,8,32,128]{3,2,1,0:T(8,128)S(1)}, f32[3,8,32,128]{3,2,1,0:T(8,128)S(1)}, u32[]{:S(2)}, u32[]{:S(2)}) %collective-permute-start.4) | collective-permute-done | bytes 393248 | tf_op jit(solution)/shard_map/ppermute | solution.py:486
  22.6 0.4 %shard_map.108 = (f32[8,32,128]{2,1,0:T(8,128)S(1)}, f32[8,32,128]{2,1,0:T(8,128)S(1)}, f32[2,256,128]{2,1,0:T(8,128)S(1)}) custom-call(f32[2,8,32,128]{3,2,1,0:T(8,128)S(1)} %collective-permute-done.peer_first, f32[3,8,32,128]{3,2,1,0:T(8,128)S(1)} %collective-permute-done.4.peer_second, f32[5,8,32,128]{3,2,1,0:T(8,128)S(1)} %get-tuple-element.49.flux, ...), custom_call_target="tpu_custom_call" | custom-call | bytes 2097152 | tf_op jit(solution)/shard_map/pallas_call | solution.py:440
  23.1 0.5 %collective-permute-start.9 = (f32[8,32,128]{2,1,0:T(8,128)S(1)}, f32[8,32,128]{2,1,0:T(8,128)S(1)}, u32[]{:S(2)}, u32[]{:S(2)}) collective-permute-start(f32[8,32,128]{2,1,0:T(8,128)S(1)} %get-tuple-element.51), channel_id=1, source_target_pairs={{0,1},{1,0},{2,3},{3,2},{4,5},{5,4},{6,7},{7,6},{8,9},{9,8},{10,11... | collective-permute-start | bytes 393224 | tf_op jit(solution)/shard_map/ppermute | solution.py:506
  23.6 0.8 %collective-permute-done.8.across_v = f32[8,32,128]{2,1,0:T(8,128)S(1)} collective-permute-done((f32[8,32,128]{2,1,0:T(8,128)S(1)}, f32[8,32,128]{2,1,0:T(8,128)S(1)}, u32[]{:S(2)}, u32[]{:S(2)}) %collective-permute-start.8) | collective-permute-done | bytes 131104 | tf_op jit(solution)/shard_map/ppermute | solution.py:505
  24.4 0.2 collective-permute-done.9.across_t
  24.6 2.3 %shard_map.109 = (f32[5,8,32,128]{3,2,1,0:T(8,128)S(1)}, f32[5,8,32,128]{3,2,1,0:T(8,128)S(1)}) custom-call(f32[4,8,32,128]{3,2,1,0:T(8,128)S(1)} %get-tuple-element.35.own, f32[3,8,32,128]{3,2,1,0:T(8,128)S(1)} %get-tuple-element.44.second, f32[2,8,32,128]{3,2,1,0:T(8,128)S(1)} %collective-permute-done.peer_first, ...), custom_call_target="tpu_custom_call" | custom-call | bytes 7208960 | tf_op jit(solution)/shard_map/pallas_call | solution.py:440
  26.9 0.5 %shard_map.110 = (f32[5,8,32,128]{3,2,1,0:T(8,128)S(1)}, f32[8,32,128]{2,1,0:T(8,128)S(1)}, f32[8,32,128]{2,1,0:T(8,128)S(1)}, f32[8,32,128]{2,1,0:T(8,128)S(1)}...) custom-call(f32[4,8,32,128]{3,2,1,0:T(8,128)S(1)} %get-tuple-element.35.own, ...), custom_call_target="tpu_custom_call" | custom-call | bytes 4456448 | tf_op jit(solution)/shard_map/pallas_call | solution.py:440
  27.4 0.4 %collective-permute-start.10 = (f32[8,32,128]{2,1,0:T(8,128)S(1)}, f32[8,32,128]{2,1,0:T(8,128)S(1)}, u32[]{:S(2)}, u32[]{:S(2)}) collective-permute-start(f32[8,32,128]{2,1,0:T(8,128)S(1)} %get-tuple-element.57), channel_id=1, source_target_pairs={{0,1},{1,0},{2,3},{3,2},{4,5},{5,4},{6,7},{7,6},{8,9},{9,8},{10,11... | collective-permute-start | bytes 393224 | tf_op jit(solution)/shard_map/ppermute | solution.py:525
  27.8 0.2 collective-permute-start.11
  28.0 0.3 %collective-permute-start.12 = (f32[8,32,128]{2,1,0:T(8,128)S(1)}, f32[8,32,128]{2,1,0:T(8,128)S(1)}, u32[]{:S(2)}, u32[]{:S(2)}) collective-permute-start(f32[8,32,128]{2,1,0:T(8,128)S(1)} %get-tuple-element.59), channel_id=1, source_target_pairs={{0,1},{1,0},{2,3},{3,2},{4,5},{5,4},{6,7},{7,6},{8,9},{9,8},{10,11... | collective-permute-start | bytes 393224 | tf_op jit(solution)/shard_map/ppermute | solution.py:525
  28.3 0.2 collective-permute-start.13
  28.5 0.3 %collective-permute-start.14 = (f32[8,32,128]{2,1,0:T(8,128)S(1)}, f32[8,32,128]{2,1,0:T(8,128)S(1)}, u32[]{:S(2)}, u32[]{:S(2)}) collective-permute-start(f32[8,32,128]{2,1,0:T(8,128)S(1)} %get-tuple-element.61), channel_id=1, source_target_pairs={{0,1},{1,0},{2,3},{3,2},{4,5},{5,4},{6,7},{7,6},{8,9},{9,8},{10,11... | collective-permute-start | bytes 393224 | tf_op jit(solution)/shard_map/ppermute | solution.py:525
  28.9 0.3 %collective-permute-done.11.mate_1 = f32[8,32,128]{2,1,0:T(8,128)S(1)} collective-permute-done((f32[8,32,128]{2,1,0:T(8,128)S(1)}, f32[8,32,128]{2,1,0:T(8,128)S(1)}, u32[]{:S(2)}, u32[]{:S(2)}) %collective-permute-start.11) | collective-permute-done | bytes 131104 | tf_op jit(solution)/shard_map/ppermute | solution.py:525
  29.2 0.2 collective-permute-done.12.mate_2
  29.4 0.3 %collective-permute-done.13.mate_3 = f32[8,32,128]{2,1,0:T(8,128)S(1)} collective-permute-done((f32[8,32,128]{2,1,0:T(8,128)S(1)}, f32[8,32,128]{2,1,0:T(8,128)S(1)}, u32[]{:S(2)}, u32[]{:S(2)}) %collective-permute-start.13) | collective-permute-done | bytes 131104 | tf_op jit(solution)/shard_map/ppermute | solution.py:525
  29.7 0.2 collective-permute-done.14.mate_4
  29.9 1.5 %shard_map.111 = (f32[5,8,32,128]{3,2,1,0:T(8,128)}, f32[5,8,32,128]{3,2,1,0:T(8,128)}) custom-call(f32[5,8,32,128]{3,2,1,0:T(8,128)S(1)} %get-tuple-element.34.conserved, f32[5,8,32,128]{3,2,1,0:T(8,128)S(1)} %get-tuple-element.56.total, f32[8,32,128]{2,1,0:T(8,128)S(1)} %collective-permute-done.10.mate_0, ...), custom_call_target="tpu_custom_call" | custom-call | bytes 4259840 | tf_op jit(solution)/shard_map/pallas_call | solution.py:440
  (22 shorter events, 0.1 us)
Async XLA Ops:
  0.6 9.2 %copy-start.2 = (bf16[256,256]{1,0:T(8,128)(2,1)S(1)}, bf16[256,256]{1,0:T(8,128)(2,1)}, u32[]{:S(2)}) copy-start(bf16[256,256]{1,0:T(8,128)(2,1)} %constant.16.clone.y_high) | copy-start | bytes 393220
  0.6 9.1 %copy-start.3 = (bf16[256,256]{1,0:T(8,128)(2,1)S(1)}, bf16[256,256]{1,0:T(8,128)(2,1)}, u32[]{:S(2)}) copy-start(bf16[256,256]{1,0:T(8,128)(2,1)} %constant.17.clone.y_low) | copy-start | bytes 393220
  2.1 12.2 %collective-permute-start = (f32[2,8,32,128]{3,2,1,0:T(8,128)S(1)}, f32[2,8,32,128]{3,2,1,0:T(8,128)S(1)}, u32[]{:S(2)}, u32[]{:S(2)}) collective-permute-start(f32[2,8,32,128]{3,2,1,0:T(8,128)S(1)} %get-tuple-element.36), channel_id=1, source_target_pairs={{0,2},{1,3},{2,0},{3,1},{4,6},{5,7},{6,4},{7,5},{8,10},{9,11},{10,... | collective-permute-start | bytes 786440 | tf_op jit(solution)/shard_map/ppermute | solution.py:476
  5.1 7.9 %collective-permute-start.1 = (f32[4,2,32,128]{3,2,1,0:T(8,128)S(1)}, f32[4,2,32,128]{3,2,1,0:T(8,128)S(1)}, u32[]{:S(2)}, u32[]{:S(2)}) collective-permute-start(f32[4,2,32,128]{3,2,1,0:T(8,128)S(1)} %get-tuple-element.37), channel_id=1, source_target_pairs={{0,4},{4,8},{8,12},{12,16},{16,20},{20,24},{24,28},{28,0},{1,5},{5... | collective-permute-start | bytes 393224 | tf_op jit(solution)/shard_map/ppermute | solution.py:477
  6.6 7.7 %collective-permute-start.2 = (f32[4,2,32,128]{3,2,1,0:T(8,128)S(1)}, f32[4,2,32,128]{3,2,1,0:T(8,128)S(1)}, u32[]{:S(2)}, u32[]{:S(2)}) collective-permute-start(f32[4,2,32,128]{3,2,1,0:T(8,128)S(1)} %get-tuple-element.38), channel_id=1, source_target_pairs={{4,0},{8,4},{12,8},{16,12},{20,16},{24,20},{28,24},{0,28},{5,1},{9... | collective-permute-start | bytes 393224 | tf_op jit(solution)/shard_map/ppermute | solution.py:478
  9.8 6.0 %copy-start.1 = (bf16[2,512,256]{2,1,0:T(8,128)(2,1)S(1)}, bf16[2,512,256]{2,1,0:T(8,128)(2,1)}, u32[]{:S(2)}) copy-start(bf16[2,512,256]{2,1,0:T(8,128)(2,1)} %constant.13.clone.z_low) | copy-start | bytes 1572868
  10.5 5.3 %copy-start = (bf16[2,512,256]{2,1,0:T(8,128)(2,1)S(1)}, bf16[2,512,256]{2,1,0:T(8,128)(2,1)}, u32[]{:S(2)}) copy-start(bf16[2,512,256]{2,1,0:T(8,128)(2,1)} %constant.12.clone.z_high) | copy-start | bytes 1572868
  10.5 12.1 %collective-permute-start.4 = (f32[3,8,32,128]{3,2,1,0:T(8,128)S(1)}, f32[3,8,32,128]{3,2,1,0:T(8,128)S(1)}, u32[]{:S(2)}, u32[]{:S(2)}) collective-permute-start(f32[3,8,32,128]{3,2,1,0:T(8,128)S(1)} %get-tuple-element.44.second), channel_id=1, source_target_pairs={{0,2},{1,3},{2,0},{3,1},{4,6},{5,7},{6,4},{7,5},{8,10},{9,11},{10,... | collective-permute-start | bytes 1179656 | tf_op jit(solution)/shard_map/ppermute | solution.py:486
  11.0 4.7 %collective-permute-start.6 = (f32[2,8,32,128]{3,2,1,0:T(8,128)S(1)}, f32[2,8,32,128]{3,2,1,0:T(8,128)S(1)}, u32[]{:S(2)}, u32[]{:S(2)}) collective-permute-start(f32[2,8,32,128]{3,2,1,0:T(8,128)S(1)} %get-tuple-element.46), channel_id=1, source_target_pairs={{0,1},{1,0},{2,3},{3,2},{4,5},{5,4},{6,7},{7,6},{8,9},{9,8},{10,11... | collective-permute-start | bytes 786440 | tf_op jit(solution)/shard_map/ppermute | solution.py:484
  14.2 1.5 %collective-permute-start.7 = (f32[2,8,32,128]{3,2,1,0:T(8,128)S(1)}, f32[2,8,32,128]{3,2,1,0:T(8,128)S(1)}, u32[]{:S(2)}, u32[]{:S(2)}) collective-permute-start(f32[2,8,32,128]{3,2,1,0:T(8,128)S(1)} %collective-permute-done.peer_first), channel_id=1, source_target_pairs={{0,1},{1,0},{2,3},{3,2},{4,5},{5,4},{6,7},{7,6},{8,9},{9,8},{10,11... | collective-permute-start | bytes 786440 | tf_op jit(solution)/shard_map/ppermute | solution.py:488
  14.2 8.8 %collective-permute-start.5 = (f32[2,8,32,128]{3,2,1,0:T(8,128)S(1)}, f32[2,8,32,128]{3,2,1,0:T(8,128)S(1)}, u32[]{:S(2)}, u32[]{:S(2)}) collective-permute-start(f32[2,8,32,128]{3,2,1,0:T(8,128)S(1)} %get-tuple-element.45), channel_id=1, source_target_pairs={{0,1},{1,0},{2,3},{3,2},{4,5},{5,4},{6,7},{7,6},{8,9},{9,8},{10,11... | collective-permute-start | bytes 786440 | tf_op jit(solution)/shard_map/ppermute | solution.py:485
  15.1 11.8 %collective-permute-start.3 = (f32[2,8,32,128]{3,2,1,0:T(8,128)S(1)}, f32[2,8,32,128]{3,2,1,0:T(8,128)S(1)}, u32[]{:S(2)}, u32[]{:S(2)}) collective-permute-start(f32[2,8,32,128]{3,2,1,0:T(8,128)S(1)} %get-tuple-element.43.third), channel_id=1, source_target_pairs={{0,2},{1,3},{2,0},{3,1},{4,6},{5,7},{6,4},{7,5},{8,10},{9,11},{10,... | collective-permute-start | bytes 786440 | tf_op jit(solution)/shard_map/ppermute | solution.py:492
  16.7 11.6 %collective-permute-start.15 = (f32[5,2,32,128]{3,2,1,0:T(8,128)S(1)}, f32[5,2,32,128]{3,2,1,0:T(8,128)S(1)}, u32[]{:S(2)}, u32[]{:S(2)}) collective-permute-start(f32[5,2,32,128]{3,2,1,0:T(8,128)S(1)} %get-tuple-element.62), channel_id=1, source_target_pairs={{0,4},{4,8},{8,12},{12,16},{16,20},{20,24},{24,28},{28,0},{1,5},{5... | collective-permute-start | bytes 491528 | tf_op jit(solution)/shard_map/ppermute | solution.py:498
  17.7 10.9 %collective-permute-start.16 = (f32[5,2,32,128]{3,2,1,0:T(8,128)S(1)}, f32[5,2,32,128]{3,2,1,0:T(8,128)S(1)}, u32[]{:S(2)}, u32[]{:S(2)}) collective-permute-start(f32[5,2,32,128]{3,2,1,0:T(8,128)S(1)} %get-tuple-element.63), channel_id=1, source_target_pairs={{4,0},{8,4},{12,8},{16,12},{20,16},{24,20},{28,24},{0,28},{5,1},{9... | collective-permute-start | bytes 491528 | tf_op jit(solution)/shard_map/ppermute | solution.py:499
  22.6 2.0 %copy-start.4 = (bf16[2,256,256]{2,1,0:T(8,128)(2,1)S(1)}, bf16[2,256,256]{2,1,0:T(8,128)(2,1)}, u32[]{:S(2)}) copy-start(bf16[2,256,256]{2,1,0:T(8,128)(2,1)} %constant.14.clone.f_high) | copy-start | bytes 786436
  22.6 2.0 %copy-start.5 = (bf16[2,256,256]{2,1,0:T(8,128)(2,1)S(1)}, bf16[2,256,256]{2,1,0:T(8,128)(2,1)}, u32[]{:S(2)}) copy-start(bf16[2,256,256]{2,1,0:T(8,128)(2,1)} %constant.15.clone.f_low) | copy-start | bytes 786436
  23.0 1.4 %collective-permute-start.8 = (f32[8,32,128]{2,1,0:T(8,128)S(1)}, f32[8,32,128]{2,1,0:T(8,128)S(1)}, u32[]{:S(2)}, u32[]{:S(2)}) collective-permute-start(f32[8,32,128]{2,1,0:T(8,128)S(1)} %get-tuple-element.50), channel_id=1, source_target_pairs={{0,1},{1,0},{2,3},{3,2},{4,5},{5,4},{6,7},{7,6},{8,9},{9,8},{10,11... | collective-permute-start | bytes 393224 | tf_op jit(solution)/shard_map/ppermute | solution.py:505
  23.1 1.5 %collective-permute-start.9 = (f32[8,32,128]{2,1,0:T(8,128)S(1)}, f32[8,32,128]{2,1,0:T(8,128)S(1)}, u32[]{:S(2)}, u32[]{:S(2)}) collective-permute-start(f32[8,32,128]{2,1,0:T(8,128)S(1)} %get-tuple-element.51), channel_id=1, source_target_pairs={{0,1},{1,0},{2,3},{3,2},{4,5},{5,4},{6,7},{7,6},{8,9},{9,8},{10,11... | collective-permute-start | bytes 393224 | tf_op jit(solution)/shard_map/ppermute | solution.py:506
  27.4 1.4 %collective-permute-start.10 = (f32[8,32,128]{2,1,0:T(8,128)S(1)}, f32[8,32,128]{2,1,0:T(8,128)S(1)}, u32[]{:S(2)}, u32[]{:S(2)}) collective-permute-start(f32[8,32,128]{2,1,0:T(8,128)S(1)} %get-tuple-element.57), channel_id=1, source_target_pairs={{0,1},{1,0},{2,3},{3,2},{4,5},{5,4},{6,7},{7,6},{8,9},{9,8},{10,11... | collective-permute-start | bytes 393224 | tf_op jit(solution)/shard_map/ppermute | solution.py:525
  27.8 1.3 %collective-permute-start.11 = (f32[8,32,128]{2,1,0:T(8,128)S(1)}, f32[8,32,128]{2,1,0:T(8,128)S(1)}, u32[]{:S(2)}, u32[]{:S(2)}) collective-permute-start(f32[8,32,128]{2,1,0:T(8,128)S(1)} %get-tuple-element.58), channel_id=1, source_target_pairs={{0,1},{1,0},{2,3},{3,2},{4,5},{5,4},{6,7},{7,6},{8,9},{9,8},{10,11... | collective-permute-start | bytes 393224 | tf_op jit(solution)/shard_map/ppermute | solution.py:525
  28.0 1.3 %collective-permute-start.12 = (f32[8,32,128]{2,1,0:T(8,128)S(1)}, f32[8,32,128]{2,1,0:T(8,128)S(1)}, u32[]{:S(2)}, u32[]{:S(2)}) collective-permute-start(f32[8,32,128]{2,1,0:T(8,128)S(1)} %get-tuple-element.59), channel_id=1, source_target_pairs={{0,1},{1,0},{2,3},{3,2},{4,5},{5,4},{6,7},{7,6},{8,9},{9,8},{10,11... | collective-permute-start | bytes 393224 | tf_op jit(solution)/shard_map/ppermute | solution.py:525
  28.3 1.3 %collective-permute-start.13 = (f32[8,32,128]{2,1,0:T(8,128)S(1)}, f32[8,32,128]{2,1,0:T(8,128)S(1)}, u32[]{:S(2)}, u32[]{:S(2)}) collective-permute-start(f32[8,32,128]{2,1,0:T(8,128)S(1)} %get-tuple-element.60), channel_id=1, source_target_pairs={{0,1},{1,0},{2,3},{3,2},{4,5},{5,4},{6,7},{7,6},{8,9},{9,8},{10,11... | collective-permute-start | bytes 393224 | tf_op jit(solution)/shard_map/ppermute | solution.py:525
  28.5 1.3 %collective-permute-start.14 = (f32[8,32,128]{2,1,0:T(8,128)S(1)}, f32[8,32,128]{2,1,0:T(8,128)S(1)}, u32[]{:S(2)}, u32[]{:S(2)}) collective-permute-start(f32[8,32,128]{2,1,0:T(8,128)S(1)} %get-tuple-element.61), channel_id=1, source_target_pairs={{0,1},{1,0},{2,3},{3,2},{4,5},{5,4},{6,7},{7,6},{8,9},{9,8},{10,11... | collective-permute-start | bytes 393224 | tf_op jit(solution)/shard_map/ppermute | solution.py:525
where the time goes:
time: 31.5 us; the launch traced here: 31.4 us
  starting transfers between devices  16 us (51%)
  Pallas kernels  7.96 us (25%)
  waiting for transfers between devices  6.6 us (21%)
  between operations  0.75 us (2%)
    pallas_call x8, Pallas kernels, call(): pl.pallas_call(kernel, out_shape=[jax.ShapeDtypeStruct(shape, F32) for sh...  7.96 us
    ppermute x1, starting transfers between devices, fast_device(): flux_after = lax.ppermute(flux_down, 'gx', ring_down)  3.8 us
    ppermute x1, starting transfers between devices, fast_device(): after = lax.ppermute(down, 'gx', ring_down)  3.2 us
    ppermute x1, starting transfers between devices, fast_device(): peer_first = lax.ppermute(first, 'gy', to_peer)  3 us
    ppermute x1, waiting for transfers between devices, fast_device(): before = lax.ppermute(up, 'gx', ring_up)  1.98 us
    ppermute x1, starting transfers between devices, fast_device(): before = lax.ppermute(up, 'gx', ring_up)  1.52 us
    ppermute x5, starting transfers between devices, fast_device(): from_mate = [lax.ppermute(value, 'gy', to_mate) for value in for_mate]  1.41 us
    ppermute x1, waiting for transfers between devices, fast_device(): after = lax.ppermute(down, 'gx', ring_down)  1.3 us
  transfers between devices with their start and end apart: 17, of which 10 were waited for; matrix products, arithmetic and copies ran while one was open for 0% of the time, Pallas kernels for 16%

commit v1 on v0

--- a/solution.py
+++ b/solution.py
@@ -196,7 +196,7 @@
 
 
 def kernel_primitives(
-    rho_in, mom_in, ene_in, conserved, own, first, up, down, arrived
+    rho_in, mom_in, ene_in, conserved, own, first, second, up, down, arrived
 ):
     rho = conserved.at[0]
     mom = conserved.at[1:4]
@@ -224,6 +224,9 @@
         own[T, x] = temperature
         first[0, x] = u
         first[1, x] = w
+        second[0, x] = v
+        second[1, x] = temperature
+        second[2, x] = density
         return carry
 
     lax.fori_loop(0, CX, plane, 0)
@@ -237,7 +240,7 @@
 
 
 def kernel_pitch_gradients(
-    own, conserved, y_high, y_low, dy, mu, second, mate_a, mate_b
+    own, y_high, y_low, dy, mu, mate_u, mate_w, mate_b
 ):
     for f in range(4):
         dy[f] = left_product(y_high[...], y_low[...], flat(own[f])).reshape(own.shape[1:])
@@ -246,18 +249,19 @@
         mu[x] = shear_resistance_reference * jnp.exp(
             sutherland_power_law * jnp.log(own[T, x])
         )
+        mate_u[x] = own[U, x]
+        mate_w[x] = own[W, x]
         for f in range(2):
-            mate_a[f, x] = own[f, x]
             mate_b[f, x] = own[V + f, x]
-        second[0, x] = own[V, x]
-        second[1, x] = own[T, x]
-        second[2, x] = conserved[0, x]
         return carry
 
     lax.fori_loop(0, CX, plane, 0)
 
 
-def kernel_stream_gradients(own, before, after, mu, dx, third):
+def kernel_stream_gradients(own, before, after, mu, peer_first, dx, third, for_u, for_w):
+    for_u[...] = peer_first[0]
+    for_w[...] = peer_first[1]
+
     def field(f, carry):
         for rows in row_chunks(own.shape[2]):
             derived = compact_x(extended(before, own, after, f, rows))
@@ -276,14 +280,14 @@
 
 
 def kernel_flux_x(
-    own, second, peer_first, first_mate, across_first, dx, dy, mu, z_high, z_low,
-    dz, flux, up, down,
+    own, second, peer_first, mate_u, mate_w, across_u, across_w, dx, dy, mu,
+    z_high, z_low, dz, flux, up, down,
 ):
     width = own.shape[-1]
     odd = lax.rem(lax.axis_index("gy"), 2)
-    for f in range(2):
+    for f, (mate, across) in enumerate(((mate_u, across_u), (mate_w, across_w))):
         values = jnp.concatenate(
-            [flat(own[f]), flat(peer_first[f]), flat(first_mate[f]), flat(across_first[f])], axis=1
+            [flat(own[f]), flat(peer_first[f]), flat(mate[...]), flat(across[...])], axis=1
         )
         dz[f] = right_product(values, z_high[odd], z_low[odd])
 
@@ -417,17 +421,29 @@
         for_mate[f][...] = part_mate[f] + spread[:, width:].reshape(shape)
 
 
-def kernel_finish(
-    conserved, total, mate_0, mate_1, mate_2, mate_3, mate_4, flux, before, after,
-    tendency, advanced,
-):
-    for f, from_mate in enumerate((mate_0, mate_1, mate_2, mate_3, mate_4)):
+def kernel_add_stream(total, flux, before, after, result):
+    def field(f, carry):
         for rows in row_chunks(flux.shape[2]):
             derived = compact_x(extended(before, flux, after, f, rows))
             for x in range(CX):
-                value = -(total[f, x, rows, :] + from_mate[x, rows, :] + derived[x])
-                tendency[f, x, rows, :] = value
-                advanced[f, x, rows, :] = conserved[f, x, rows, :] + section_step * value
+                result[f, x, rows, :] = total[f, x, rows, :] + derived[x]
+        return carry
+
+    lax.fori_loop(0, 5, field, 0)
+
+
+def kernel_finish(
+    conserved, total, mate_0, mate_1, mate_2, mate_3, mate_4, tendency, advanced
+):
+    for f, from_mate in enumerate((mate_0, mate_1, mate_2, mate_3, mate_4)):
+
+        def plane(x, carry):
+            value = -(total[f, x] + from_mate[x])
+            tendency[f, x] = value
+            advanced[f, x] = conserved[f, x] + section_step * value
+            return carry
+
+        lax.fori_loop(0, CX, plane, 0, unroll=2)
 
 
 def call(kernel, outputs, operands, scratch=(), outside=False):
@@ -466,9 +482,9 @@
     to_mate = [(i, i ^ 1) for i in range(4)]
     to_peer = [(i, i ^ 2) for i in range(4)]
 
-    conserved, own, first, up, down = call(
+    conserved, own, first, second, up, down = call(
         kernel_primitives,
-        [(5,) + block, (4,) + block, (2,) + block, (4,) + sums, (4,) + sums],
+        [(5,) + block, (4,) + block, (2,) + block, (3,) + block, (4,) + sums, (4,) + sums],
         (rho, mom, ene),
         scratch=(pltpu.SemaphoreType.DMA((3,)),),
         outside=True,
@@ -476,24 +492,28 @@
     peer_first = lax.ppermute(first, "gy", to_peer)
     before = lax.ppermute(up, "gx", ring_up)
     after = lax.ppermute(down, "gx", ring_down)
-    dy, mu, second, mate_a, mate_b = call(
+    dy, mu, for_u, for_w, mate_b = call(
         kernel_pitch_gradients,
-        [(4,) + block, block, (3,) + block, (2,) + block, (2,) + block],
-        (own, conserved, y_high, y_low),
-    )
-    first_mate = lax.ppermute(mate_a, "gy", to_mate)
+        [(4,) + block, block, block, block, (2,) + block],
+        (own, y_high, y_low),
+    )
+    mate_u, mate_w = (lax.ppermute(value, "gy", to_mate) for value in (for_u, for_w))
     second_mate = lax.ppermute(mate_b, "gy", to_mate)
     peer_second = lax.ppermute(second, "gy", to_peer)
-    peer_first, before, after = lax.optimization_barrier((peer_first, before, after))
-    across_first = lax.ppermute(peer_first, "gy", to_mate)
-    dx, third = call(
-        kernel_stream_gradients, [(4,) + block, (2,) + block], (own, before, after, mu)
-    )
+    dx, third, for_u, for_w = call(
+        kernel_stream_gradients,
+        [(4,) + block, (2,) + block, block, block],
+        (own, before, after, mu, peer_first),
+    )
+    across_u, across_w = (lax.ppermute(value, "gy", to_mate) for value in (for_u, for_w))
     peer_third = lax.ppermute(third, "gy", to_peer)
     dz, flux, flux_up, flux_down = call(
         kernel_flux_x,
         [(2, points, 2 * width), (5,) + block, (5,) + sums, (5,) + sums],
-        (own, second, peer_first, first_mate, across_first, dx, dy, mu, z_high, z_low),
+        (
+            own, second, peer_first, mate_u, mate_w, across_u, across_w, dx, dy, mu,
+            z_high, z_low,
+        ),
     )
     flux_before = lax.ppermute(flux_up, "gx", ring_up)
     flux_after = lax.ppermute(flux_down, "gx", ring_down)
@@ -523,10 +543,11 @@
         (own, peer_first, third, peer_third, part, part_mate, f_high, f_low),
     )
     from_mate = [lax.ppermute(value, "gy", to_mate) for value in for_mate]
+    (total,) = call(
+        kernel_add_stream, [(5,) + block], (total, flux, flux_before, flux_after)
+    )
     tendency, advanced = call(
-        kernel_finish,
-        [(5,) + block, (5,) + block],
-        (conserved, total, *from_mate, flux, flux_before, flux_after),
+        kernel_finish, [(5,) + block, (5,) + block], (conserved, total, *from_mate)
     )
     return (
         jnp.transpose(tendency, (0, 1, 3, 2)),

time: 31.5 us -> 31.7 us (level)
  starting transfers between devices: 16 us -> 17.1 us
  waiting for transfers between devices: 6.6 us -> 5.55 us
    ppermute x1, waiting for transfers between devices: 1.16 us -> 0.01 us  [fast_device(): peer_second = lax.ppermute(second, 'gy', to_peer)]
    ppermute x1, starting transfers between devices: 0.6 us -> 1.49 us  [fast_device(): peer_third = lax.ppermute(third, 'gy', to_peer)]
    ppermute x2 -> x4, starting transfers between devices: 0.01 us -> 0.71 us  [fast_device(): lax.ppermute(value, 'gy', to_mate)]
    ppermute x1, starting transfers between devices: 0.51 us -> 0.01 us  [fast_device(): second_mate = lax.ppermute(mate_b, 'gy', to_mate)]
    ppermute x1, starting transfers between devices: 1.52 us -> 1.98 us  [fast_device(): before = lax.ppermute(up, 'gx', ring_up)]
    ppermute x5, waiting for transfers between devices: 1.03 us -> 0.64 us  [fast_device(): from_mate = [lax.ppermute(value, 'gy', to_mate) for value in for_mate]]
    ppermute x1, starting transfers between devices: 0.44 us -> 0.08 us  [fast_device(): peer_second = lax.ppermute(second, 'gy', to_peer)]
    pallas_call x8 -> x9, Pallas kernels: 7.96 us -> 8.14 us  [call(): pl.pallas_call(kernel, out_shape=[jax.ShapeDtypeStruct(shape, F32) for sh...]
  transfers between devices with their start and end apart: 17 -> 19, of which waited for: 10 -> 8; matrix products, arithmetic and copies ran while one was open for 0% -> 0% of each run, Pallas kernels for 16% -> 17%
where the time goes in v1:
time: 31.7 us; the launch traced here: 31.6 us
  starting transfers between devices  17.1 us (54%)
  Pallas kernels  8.14 us (26%)
  waiting for transfers between devices  5.55 us (18%)
  between operations  0.79 us (2%)
    pallas_call x9, Pallas kernels, call(): pl.pallas_call(kernel, out_shape=[jax.ShapeDtypeStruct(shape, F32) for sh...  8.14 us
    ppermute x1, starting transfers between devices, fast_device(): flux_after = lax.ppermute(flux_down, 'gx', ring_down)  3.95 us
    ppermute x1, starting transfers between devices, fast_device(): after = lax.ppermute(down, 'gx', ring_down)  3.04 us
    ppermute x1, starting transfers between devices, fast_device(): peer_first = lax.ppermute(first, 'gy', to_peer)  3 us
    ppermute x1, waiting for transfers between devices, fast_device(): before = lax.ppermute(up, 'gx', ring_up)  2.24 us
    ppermute x1, starting transfers between devices, fast_device(): before = lax.ppermute(up, 'gx', ring_up)  1.98 us
    ppermute x1, starting transfers between devices, fast_device(): peer_third = lax.ppermute(third, 'gy', to_peer)  1.49 us
    ppermute x5, starting transfers between devices, fast_device(): from_mate = [lax.ppermute(value, 'gy', to_mate) for value in for_mate]  1.42 us
  transfers between devices with their start and end apart: 19, of which 8 were waited for; matrix products, arithmetic and copies ran while one was open for 0% of the time, Pallas kernels for 17%

profile of v1, /device:TPU:0, one launch (start us, length us, event | category | flops | bytes accessed | tf_op | source)
XLA Modules:
  0.0 31.6 jit_solution(5727154756520491987)
XLA Ops:
  0.7 1.4 %shard_map.104 = (f32[5,8,32,128]{3,2,1,0:T(8,128)S(1)}, f32[4,8,32,128]{3,2,1,0:T(8,128)S(1)}, f32[2,8,32,128]{3,2,1,0:T(8,128)S(1)}, f32[3,8,32,128]{3,2,1,0:T...) custom-call(f32[8,32,128]{2,1,0:T(8,128)} %bitcast.6, f32[3,8,32,128]{3,2,1,0:T(8,128)} %bitcast.5, ...), custom_call_target="tpu_custom_call" | custom-call | bytes 2752512 | tf_op jit(solution)/shard_map/pallas_call | solution.py:456
  2.1 3.0 %collective-permute-start = (f32[2,8,32,128]{3,2,1,0:T(8,128)S(1)}, f32[2,8,32,128]{3,2,1,0:T(8,128)S(1)}, u32[]{:S(2)}, u32[]{:S(2)}) collective-permute-start(f32[2,8,32,128]{3,2,1,0:T(8,128)S(1)} %get-tuple-element.36), channel_id=1, source_target_pairs={{0,2},{1,3},{2,0},{3,1},{4,6},{5,7},{6,4},{7,5},{8,10},{9,11},{10,... | collective-permute-start | bytes 786440 | tf_op jit(solution)/shard_map/ppermute | solution.py:492
  5.1 0.1 collective-permute-start.4
  5.1 2.0 %collective-permute-start.1 = (f32[4,2,32,128]{3,2,1,0:T(8,128)S(1)}, f32[4,2,32,128]{3,2,1,0:T(8,128)S(1)}, u32[]{:S(2)}, u32[]{:S(2)}) collective-permute-start(f32[4,2,32,128]{3,2,1,0:T(8,128)S(1)} %get-tuple-element.37), channel_id=1, source_target_pairs={{0,4},{4,8},{8,12},{12,16},{16,20},{20,24},{24,28},{28,0},{1,5},{5... | collective-permute-start | bytes 393224 | tf_op jit(solution)/shard_map/ppermute | solution.py:493
  7.1 3.0 %collective-permute-start.2 = (f32[4,2,32,128]{3,2,1,0:T(8,128)S(1)}, f32[4,2,32,128]{3,2,1,0:T(8,128)S(1)}, u32[]{:S(2)}, u32[]{:S(2)}) collective-permute-start(f32[4,2,32,128]{3,2,1,0:T(8,128)S(1)} %get-tuple-element.38), channel_id=1, source_target_pairs={{4,0},{8,4},{12,8},{16,12},{20,16},{24,20},{28,24},{0,28},{5,1},{9... | collective-permute-start | bytes 393224 | tf_op jit(solution)/shard_map/ppermute | solution.py:494
  10.2 0.7 %shard_map.105 = (f32[4,8,32,128]{3,2,1,0:T(8,128)S(1)}, f32[8,32,128]{2,1,0:T(8,128)S(1)}, f32[8,32,128]{2,1,0:T(8,128)S(1)}, f32[8,32,128]{2,1,0:T(8,128)S(1)}, f32[2,8,32,128]{3,2,1,0:T(8,128)S(1)}) custom-call(f32[4,8,32,128]{3,2,1,0:T(8,128)S(1)} %get-tuple-element.35.own, bf16[256,256]{1,0:T(8,128)(2,1)S(1)} %copy-done.2, bf16[256,256]{1,0:T(8,128)(2,1)S(1)} %copy-done.3), custom_call_target="tpu_custom_call" | custom-call | bytes 1966080 | tf_op jit(solution)/shard_map/pallas_call | solution.py:456
  11.0 2.2 %collective-permute-done.1.before = f32[4,2,32,128]{3,2,1,0:T(8,128)S(1)} collective-permute-done((f32[4,2,32,128]{3,2,1,0:T(8,128)S(1)}, f32[4,2,32,128]{3,2,1,0:T(8,128)S(1)}, u32[]{:S(2)}, u32[]{:S(2)}) %collective-permute-start.1) | collective-permute-done | bytes 131104 | tf_op jit(solution)/shard_map/ppermute | solution.py:493
  13.2 1.3 %collective-permute-done.2.after = f32[4,2,32,128]{3,2,1,0:T(8,128)S(1)} collective-permute-done((f32[4,2,32,128]{3,2,1,0:T(8,128)S(1)}, f32[4,2,32,128]{3,2,1,0:T(8,128)S(1)}, u32[]{:S(2)}, u32[]{:S(2)}) %collective-permute-start.2) | collective-permute-done | bytes 131104 | tf_op jit(solution)/shard_map/ppermute | solution.py:494
  14.5 0.3 %shard_map.106 = (f32[4,8,32,128]{3,2,1,0:T(8,128)S(1)}, f32[2,8,32,128]{3,2,1,0:T(8,128)S(1)}, f32[8,32,128]{2,1,0:T(8,128)S(1)}, f32[8,32,128]{2,1,0:T(8,128)S(1)}) custom-call(f32[4,8,32,128]{3,2,1,0:T(8,128)S(1)} %get-tuple-element.35.own, f32[4,2,32,128]{3,2,1,0:T(8,128)S(1)} %collective-permute-done.1.before, ...), custom_call_target="tpu_custom_call" | custom-call | bytes 2228224 | tf_op jit(solution)/shard_map/pallas_call | solution.py:456
  14.9 0.6 %collective-permute-start.8 = (f32[8,32,128]{2,1,0:T(8,128)S(1)}, f32[8,32,128]{2,1,0:T(8,128)S(1)}, u32[]{:S(2)}, u32[]{:S(2)}) collective-permute-start(f32[8,32,128]{2,1,0:T(8,128)S(1)} %get-tuple-element.45), channel_id=1, source_target_pairs={{0,1},{1,0},{2,3},{3,2},{4,5},{5,4},{6,7},{7,6},{8,9},{9,8},{10,11... | collective-permute-start | bytes 393224 | tf_op jit(solution)/shard_map/ppermute | solution.py:508
  15.4 0.1 collective-permute-start.9
  15.5 0.3 %collective-permute-done.7.mate_w = f32[8,32,128]{2,1,0:T(8,128)S(1)} collective-permute-done((f32[8,32,128]{2,1,0:T(8,128)S(1)}, f32[8,32,128]{2,1,0:T(8,128)S(1)}, u32[]{:S(2)}, u32[]{:S(2)}) %collective-permute-start.7) | collective-permute-done | bytes 131104 | tf_op jit(solution)/shard_map/ppermute | solution.py:500
  15.8 1.5 %collective-permute-start.3 = (f32[2,8,32,128]{3,2,1,0:T(8,128)S(1)}, f32[2,8,32,128]{3,2,1,0:T(8,128)S(1)}, u32[]{:S(2)}, u32[]{:S(2)}) collective-permute-start(f32[2,8,32,128]{3,2,1,0:T(8,128)S(1)} %get-tuple-element.40.third), channel_id=1, source_target_pairs={{0,2},{1,3},{2,0},{3,1},{4,6},{5,7},{6,4},{7,5},{8,10},{9,11},{10,... | collective-permute-start | bytes 786440 | tf_op jit(solution)/shard_map/ppermute | solution.py:509
  17.4 0.9 %shard_map.107 = (f32[2,256,256]{2,1,0:T(8,128)S(1)}, f32[5,8,32,128]{3,2,1,0:T(8,128)S(1)}, f32[5,2,32,128]{3,2,1,0:T(8,128)S(1)}, f32[5,2,32,128]{3,2,1,0:T(8,128)S(1)}) custom-call(f32[4,8,32,128]{3,2,1,0:T(8,128)S(1)} %get-tuple-element.35.own, f32[3,8,32,128]{3,2,1,0:T(8,128)S(1)} %get-tuple-element.41.second, ...), custom_call_target="tpu_custom_call" | custom-call | bytes 5439488 | tf_op jit(solution)/shard_map/pallas_call | solution.py:456
  18.3 0.8 %collective-permute-start.12 = (f32[5,2,32,128]{3,2,1,0:T(8,128)S(1)}, f32[5,2,32,128]{3,2,1,0:T(8,128)S(1)}, u32[]{:S(2)}, u32[]{:S(2)}) collective-permute-start(f32[5,2,32,128]{3,2,1,0:T(8,128)S(1)} %get-tuple-element.57), channel_id=1, source_target_pairs={{0,4},{4,8},{8,12},{12,16},{16,20},{20,24},{24,28},{28,0},{1,5},{5... | collective-permute-start | bytes 491528 | tf_op jit(solution)/shard_map/ppermute | solution.py:518
  19.1 4.0 %collective-permute-start.13 = (f32[5,2,32,128]{3,2,1,0:T(8,128)S(1)}, f32[5,2,32,128]{3,2,1,0:T(8,128)S(1)}, u32[]{:S(2)}, u32[]{:S(2)}) collective-permute-start(f32[5,2,32,128]{3,2,1,0:T(8,128)S(1)} %get-tuple-element.58), channel_id=1, source_target_pairs={{4,0},{8,4},{12,8},{16,12},{20,16},{24,20},{28,24},{0,28},{5,1},{9... | collective-permute-start | bytes 491528 | tf_op jit(solution)/shard_map/ppermute | solution.py:519
  23.1 0.4 %shard_map.108 = (f32[8,32,128]{2,1,0:T(8,128)S(1)}, f32[8,32,128]{2,1,0:T(8,128)S(1)}, f32[2,256,128]{2,1,0:T(8,128)S(1)}) custom-call(f32[2,8,32,128]{3,2,1,0:T(8,128)S(1)} %collective-permute-done.peer_first, f32[3,8,32,128]{3,2,1,0:T(8,128)S(1)} %collective-permute-done.4.peer_second, f32[5,8,32,128]{3,2,1,0:T(8,128)S(1)} %get-tuple-element.49.flux, ...), custom_call_target="tpu_custom_call" | custom-call | bytes 2097152 | tf_op jit(solution)/shard_map/pallas_call | solution.py:456
  23.5 0.5 %collective-permute-start.11 = (f32[8,32,128]{2,1,0:T(8,128)S(1)}, f32[8,32,128]{2,1,0:T(8,128)S(1)}, u32[]{:S(2)}, u32[]{:S(2)}) collective-permute-start(f32[8,32,128]{2,1,0:T(8,128)S(1)} %get-tuple-element.51), channel_id=1, source_target_pairs={{0,1},{1,0},{2,3},{3,2},{4,5},{5,4},{6,7},{7,6},{8,9},{9,8},{10,11... | collective-permute-start | bytes 393224 | tf_op jit(solution)/shard_map/ppermute | solution.py:526
  24.0 0.8 %collective-permute-done.10.across_v = f32[8,32,128]{2,1,0:T(8,128)S(1)} collective-permute-done((f32[8,32,128]{2,1,0:T(8,128)S(1)}, f32[8,32,128]{2,1,0:T(8,128)S(1)}, u32[]{:S(2)}, u32[]{:S(2)}) %collective-permute-start.10) | collective-permute-done | bytes 131104 | tf_op jit(solution)/shard_map/ppermute | solution.py:525
  24.8 0.2 collective-permute-done.11.across_t
  25.0 2.3 %shard_map.109 = (f32[5,8,32,128]{3,2,1,0:T(8,128)S(1)}, f32[5,8,32,128]{3,2,1,0:T(8,128)S(1)}) custom-call(f32[4,8,32,128]{3,2,1,0:T(8,128)S(1)} %get-tuple-element.35.own, f32[3,8,32,128]{3,2,1,0:T(8,128)S(1)} %get-tuple-element.41.second, f32[2,8,32,128]{3,2,1,0:T(8,128)S(1)} %collective-permute-done.peer_first, ...), custom_call_target="tpu_custom_call" | custom-call | bytes 7208960 | tf_op jit(solution)/shard_map/pallas_call | solution.py:456
  27.3 0.5 %shard_map.110 = (f32[5,8,32,128]{3,2,1,0:T(8,128)S(1)}, f32[8,32,128]{2,1,0:T(8,128)S(1)}, f32[8,32,128]{2,1,0:T(8,128)S(1)}, f32[8,32,128]{2,1,0:T(8,128)S(1)}...) custom-call(f32[4,8,32,128]{3,2,1,0:T(8,128)S(1)} %get-tuple-element.35.own, ...), custom_call_target="tpu_custom_call" | custom-call | bytes 4456448 | tf_op jit(solution)/shard_map/pallas_call | solution.py:456
  27.9 0.4 %collective-permute-start.14 = (f32[8,32,128]{2,1,0:T(8,128)S(1)}, f32[8,32,128]{2,1,0:T(8,128)S(1)}, u32[]{:S(2)}, u32[]{:S(2)}) collective-permute-start(f32[8,32,128]{2,1,0:T(8,128)S(1)} %get-tuple-element.59), channel_id=1, source_target_pairs={{0,1},{1,0},{2,3},{3,2},{4,5},{5,4},{6,7},{7,6},{8,9},{9,8},{10,11... | collective-permute-start | bytes 393224 | tf_op jit(solution)/shard_map/ppermute | solution.py:545
  28.3 0.2 collective-permute-start.15
  28.4 0.3 %collective-permute-start.16 = (f32[8,32,128]{2,1,0:T(8,128)S(1)}, f32[8,32,128]{2,1,0:T(8,128)S(1)}, u32[]{:S(2)}, u32[]{:S(2)}) collective-permute-start(f32[8,32,128]{2,1,0:T(8,128)S(1)} %get-tuple-element.61), channel_id=1, source_target_pairs={{0,1},{1,0},{2,3},{3,2},{4,5},{5,4},{6,7},{7,6},{8,9},{9,8},{10,11... | collective-permute-start | bytes 393224 | tf_op jit(solution)/shard_map/ppermute | solution.py:545
  28.8 0.2 collective-permute-start.17
  29.0 0.3 %collective-permute-start.18 = (f32[8,32,128]{2,1,0:T(8,128)S(1)}, f32[8,32,128]{2,1,0:T(8,128)S(1)}, u32[]{:S(2)}, u32[]{:S(2)}) collective-permute-start(f32[8,32,128]{2,1,0:T(8,128)S(1)} %get-tuple-element.63), channel_id=1, source_target_pairs={{0,1},{1,0},{2,3},{3,2},{4,5},{5,4},{6,7},{7,6},{8,9},{9,8},{10,11... | collective-permute-start | bytes 393224 | tf_op jit(solution)/shard_map/ppermute | solution.py:545
  29.3 0.4 %shard_map.111.total = f32[5,8,32,128]{3,2,1,0:T(8,128)S(1)} custom-call(f32[5,8,32,128]{3,2,1,0:T(8,128)S(1)} %get-tuple-element.56.total, f32[5,8,32,128]{3,2,1,0:T(8,128)S(1)} %get-tuple-element.49.flux, f32[5,2,32,128]{3,2,1,0:T(8,128)S(1)} %collective-permute-done.12.before, f32[5,2,32,128]{3,2,1,0:T(8,128)S(1)} %collective-permute-done.13.after), custom_call_target="tpu_custom_call" | custom-call | bytes 2293760 | tf_op jit(solution)/shard_map/pallas_call | solution.py:456
  29.7 0.1 collective-permute-done.16.mate_2
  29.8 0.3 %collective-permute-done.17.mate_3 = f32[8,32,128]{2,1,0:T(8,128)S(1)} collective-permute-done((f32[8,32,128]{2,1,0:T(8,128)S(1)}, f32[8,32,128]{2,1,0:T(8,128)S(1)}, u32[]{:S(2)}, u32[]{:S(2)}) %collective-permute-start.17) | collective-permute-done | bytes 131104 | tf_op jit(solution)/shard_map/ppermute | solution.py:545
  30.1 0.2 collective-permute-done.18.mate_4
  30.3 1.3 %shard_map.112 = (f32[5,8,32,128]{3,2,1,0:T(8,128)}, f32[5,8,32,128]{3,2,1,0:T(8,128)}) custom-call(f32[5,8,32,128]{3,2,1,0:T(8,128)S(1)} %get-tuple-element.34.conserved, f32[5,8,32,128]{3,2,1,0:T(8,128)S(1)} %shard_map.111.total, f32[8,32,128]{2,1,0:T(8,128)S(1)} %collective-permute-done.14.mate_0, f32[8,32,128]{2,1,0:T(8,128)S(1)} %collective-permute-done.15.mate_1, ...), custom_call_target="tpu_custom_call" | custom-call | bytes 3276800 | tf_op jit(solution)/shard_map/pallas_call | solution.py:456
  (27 shorter events, 0.2 us)
Async XLA Ops:
  0.6 9.5 %copy-start.2 = (bf16[256,256]{1,0:T(8,128)(2,1)S(1)}, bf16[256,256]{1,0:T(8,128)(2,1)}, u32[]{:S(2)}) copy-start(bf16[256,256]{1,0:T(8,128)(2,1)} %constant.16.clone.y_high) | copy-start | bytes 393220
  0.6 9.5 %copy-start.3 = (bf16[256,256]{1,0:T(8,128)(2,1)S(1)}, bf16[256,256]{1,0:T(8,128)(2,1)}, u32[]{:S(2)}) copy-start(bf16[256,256]{1,0:T(8,128)(2,1)} %constant.17.clone.y_low) | copy-start | bytes 393220
  2.1 12.4 %collective-permute-start = (f32[2,8,32,128]{3,2,1,0:T(8,128)S(1)}, f32[2,8,32,128]{3,2,1,0:T(8,128)S(1)}, u32[]{:S(2)}, u32[]{:S(2)}) collective-permute-start(f32[2,8,32,128]{3,2,1,0:T(8,128)S(1)} %get-tuple-element.36), channel_id=1, source_target_pairs={{0,2},{1,3},{2,0},{3,1},{4,6},{5,7},{6,4},{7,5},{8,10},{9,11},{10,... | collective-permute-start | bytes 786440 | tf_op jit(solution)/shard_map/ppermute | solution.py:492
  5.1 18.0 %collective-permute-start.4 = (f32[3,8,32,128]{3,2,1,0:T(8,128)S(1)}, f32[3,8,32,128]{3,2,1,0:T(8,128)S(1)}, u32[]{:S(2)}, u32[]{:S(2)}) collective-permute-start(f32[3,8,32,128]{3,2,1,0:T(8,128)S(1)} %get-tuple-element.41.second), channel_id=1, source_target_pairs={{0,2},{1,3},{2,0},{3,1},{4,6},{5,7},{6,4},{7,5},{8,10},{9,11},{10,... | collective-permute-start | bytes 1179656 | tf_op jit(solution)/shard_map/ppermute | solution.py:502
  5.1 8.1 %collective-permute-start.1 = (f32[4,2,32,128]{3,2,1,0:T(8,128)S(1)}, f32[4,2,32,128]{3,2,1,0:T(8,128)S(1)}, u32[]{:S(2)}, u32[]{:S(2)}) collective-permute-start(f32[4,2,32,128]{3,2,1,0:T(8,128)S(1)} %get-tuple-element.37), channel_id=1, source_target_pairs={{0,4},{4,8},{8,12},{12,16},{16,20},{20,24},{24,28},{28,0},{1,5},{5... | collective-permute-start | bytes 393224 | tf_op jit(solution)/shard_map/ppermute | solution.py:493
  7.1 7.4 %collective-permute-start.2 = (f32[4,2,32,128]{3,2,1,0:T(8,128)S(1)}, f32[4,2,32,128]{3,2,1,0:T(8,128)S(1)}, u32[]{:S(2)}, u32[]{:S(2)}) collective-permute-start(f32[4,2,32,128]{3,2,1,0:T(8,128)S(1)} %get-tuple-element.38), channel_id=1, source_target_pairs={{4,0},{8,4},{12,8},{16,12},{20,16},{24,20},{28,24},{0,28},{5,1},{9... | collective-permute-start | bytes 393224 | tf_op jit(solution)/shard_map/ppermute | solution.py:494
  10.9 4.5 %collective-permute-start.6 = (f32[8,32,128]{2,1,0:T(8,128)S(1)}, f32[8,32,128]{2,1,0:T(8,128)S(1)}, u32[]{:S(2)}, u32[]{:S(2)}) collective-permute-start(f32[8,32,128]{2,1,0:T(8,128)S(1)} %get-tuple-element.43), channel_id=1, source_target_pairs={{0,1},{1,0},{2,3},{3,2},{4,5},{5,4},{6,7},{7,6},{8,9},{9,8},{10,11... | collective-permute-start | bytes 393224 | tf_op jit(solution)/shard_map/ppermute | solution.py:500
  13.2 10.3 %collective-permute-start.5 = (f32[2,8,32,128]{3,2,1,0:T(8,128)S(1)}, f32[2,8,32,128]{3,2,1,0:T(8,128)S(1)}, u32[]{:S(2)}, u32[]{:S(2)}) collective-permute-start(f32[2,8,32,128]{3,2,1,0:T(8,128)S(1)} %get-tuple-element.42), channel_id=1, source_target_pairs={{0,1},{1,0},{2,3},{3,2},{4,5},{5,4},{6,7},{7,6},{8,9},{9,8},{10,11... | collective-permute-start | bytes 786440 | tf_op jit(solution)/shard_map/ppermute | solution.py:501
  14.5 1.3 %collective-permute-start.7 = (f32[8,32,128]{2,1,0:T(8,128)S(1)}, f32[8,32,128]{2,1,0:T(8,128)S(1)}, u32[]{:S(2)}, u32[]{:S(2)}) collective-permute-start(f32[8,32,128]{2,1,0:T(8,128)S(1)} %get-tuple-element.44), channel_id=1, source_target_pairs={{0,1},{1,0},{2,3},{3,2},{4,5},{5,4},{6,7},{7,6},{8,9},{9,8},{10,11... | collective-permute-start | bytes 393224 | tf_op jit(solution)/shard_map/ppermute | solution.py:500
  14.5 2.8 %copy-start = (bf16[2,512,256]{2,1,0:T(8,128)(2,1)S(1)}, bf16[2,512,256]{2,1,0:T(8,128)(2,1)}, u32[]{:S(2)}) copy-start(bf16[2,512,256]{2,1,0:T(8,128)(2,1)} %constant.12.clone.z_high) | copy-start | bytes 1572868
  14.5 2.8 %copy-start.1 = (bf16[2,512,256]{2,1,0:T(8,128)(2,1)S(1)}, bf16[2,512,256]{2,1,0:T(8,128)(2,1)}, u32[]{:S(2)}) copy-start(bf16[2,512,256]{2,1,0:T(8,128)(2,1)} %constant.13.clone.z_low) | copy-start | bytes 1572868
  14.9 2.5 %collective-permute-start.8 = (f32[8,32,128]{2,1,0:T(8,128)S(1)}, f32[8,32,128]{2,1,0:T(8,128)S(1)}, u32[]{:S(2)}, u32[]{:S(2)}) collective-permute-start(f32[8,32,128]{2,1,0:T(8,128)S(1)} %get-tuple-element.45), channel_id=1, source_target_pairs={{0,1},{1,0},{2,3},{3,2},{4,5},{5,4},{6,7},{7,6},{8,9},{9,8},{10,11... | collective-permute-start | bytes 393224 | tf_op jit(solution)/shard_map/ppermute | solution.py:508
  15.4 1.9 %collective-permute-start.9 = (f32[8,32,128]{2,1,0:T(8,128)S(1)}, f32[8,32,128]{2,1,0:T(8,128)S(1)}, u32[]{:S(2)}, u32[]{:S(2)}) collective-permute-start(f32[8,32,128]{2,1,0:T(8,128)S(1)} %get-tuple-element.46), channel_id=1, source_target_pairs={{0,1},{1,0},{2,3},{3,2},{4,5},{5,4},{6,7},{7,6},{8,9},{9,8},{10,11... | collective-permute-start | bytes 393224 | tf_op jit(solution)/shard_map/ppermute | solution.py:508
  15.8 11.5 %collective-permute-start.3 = (f32[2,8,32,128]{3,2,1,0:T(8,128)S(1)}, f32[2,8,32,128]{3,2,1,0:T(8,128)S(1)}, u32[]{:S(2)}, u32[]{:S(2)}) collective-permute-start(f32[2,8,32,128]{3,2,1,0:T(8,128)S(1)} %get-tuple-element.40.third), channel_id=1, source_target_pairs={{0,2},{1,3},{2,0},{3,1},{4,6},{5,7},{6,4},{7,5},{8,10},{9,11},{10,... | collective-permute-start | bytes 786440 | tf_op jit(solution)/shard_map/ppermute | solution.py:509
  18.3 10.5 %collective-permute-start.12 = (f32[5,2,32,128]{3,2,1,0:T(8,128)S(1)}, f32[5,2,32,128]{3,2,1,0:T(8,128)S(1)}, u32[]{:S(2)}, u32[]{:S(2)}) collective-permute-start(f32[5,2,32,128]{3,2,1,0:T(8,128)S(1)} %get-tuple-element.57), channel_id=1, source_target_pairs={{0,4},{4,8},{8,12},{12,16},{16,20},{20,24},{24,28},{28,0},{1,5},{5... | collective-permute-start | bytes 491528 | tf_op jit(solution)/shard_map/ppermute | solution.py:518
  19.1 9.9 %collective-permute-start.13 = (f32[5,2,32,128]{3,2,1,0:T(8,128)S(1)}, f32[5,2,32,128]{3,2,1,0:T(8,128)S(1)}, u32[]{:S(2)}, u32[]{:S(2)}) collective-permute-start(f32[5,2,32,128]{3,2,1,0:T(8,128)S(1)} %get-tuple-element.58), channel_id=1, source_target_pairs={{4,0},{8,4},{12,8},{16,12},{20,16},{24,20},{28,24},{0,28},{5,1},{9... | collective-permute-start | bytes 491528 | tf_op jit(solution)/shard_map/ppermute | solution.py:519
  23.1 2.0 %copy-start.4 = (bf16[2,256,256]{2,1,0:T(8,128)(2,1)S(1)}, bf16[2,256,256]{2,1,0:T(8,128)(2,1)}, u32[]{:S(2)}) copy-start(bf16[2,256,256]{2,1,0:T(8,128)(2,1)} %constant.14.clone.f_high) | copy-start | bytes 786436
  23.1 2.0 %copy-start.5 = (bf16[2,256,256]{2,1,0:T(8,128)(2,1)S(1)}, bf16[2,256,256]{2,1,0:T(8,128)(2,1)}, u32[]{:S(2)}) copy-start(bf16[2,256,256]{2,1,0:T(8,128)(2,1)} %constant.15.clone.f_low) | copy-start | bytes 786436
  23.4 1.4 %collective-permute-start.10 = (f32[8,32,128]{2,1,0:T(8,128)S(1)}, f32[8,32,128]{2,1,0:T(8,128)S(1)}, u32[]{:S(2)}, u32[]{:S(2)}) collective-permute-start(f32[8,32,128]{2,1,0:T(8,128)S(1)} %get-tuple-element.50), channel_id=1, source_target_pairs={{0,1},{1,0},{2,3},{3,2},{4,5},{5,4},{6,7},{7,6},{8,9},{9,8},{10,11... | collective-permute-start | bytes 393224 | tf_op jit(solution)/shard_map/ppermute | solution.py:525
  23.5 1.5 %collective-permute-start.11 = (f32[8,32,128]{2,1,0:T(8,128)S(1)}, f32[8,32,128]{2,1,0:T(8,128)S(1)}, u32[]{:S(2)}, u32[]{:S(2)}) collective-permute-start(f32[8,32,128]{2,1,0:T(8,128)S(1)} %get-tuple-element.51), channel_id=1, source_target_pairs={{0,1},{1,0},{2,3},{3,2},{4,5},{5,4},{6,7},{7,6},{8,9},{9,8},{10,11... | collective-permute-start | bytes 393224 | tf_op jit(solution)/shard_map/ppermute | solution.py:526
  27.9 1.8 %collective-permute-start.14 = (f32[8,32,128]{2,1,0:T(8,128)S(1)}, f32[8,32,128]{2,1,0:T(8,128)S(1)}, u32[]{:S(2)}, u32[]{:S(2)}) collective-permute-start(f32[8,32,128]{2,1,0:T(8,128)S(1)} %get-tuple-element.59), channel_id=1, source_target_pairs={{0,1},{1,0},{2,3},{3,2},{4,5},{5,4},{6,7},{7,6},{8,9},{9,8},{10,11... | collective-permute-start | bytes 393224 | tf_op jit(solution)/shard_map/ppermute | solution.py:545
  28.3 1.4 %collective-permute-start.15 = (f32[8,32,128]{2,1,0:T(8,128)S(1)}, f32[8,32,128]{2,1,0:T(8,128)S(1)}, u32[]{:S(2)}, u32[]{:S(2)}) collective-permute-start(f32[8,32,128]{2,1,0:T(8,128)S(1)} %get-tuple-element.60), channel_id=1, source_target_pairs={{0,1},{1,0},{2,3},{3,2},{4,5},{5,4},{6,7},{7,6},{8,9},{9,8},{10,11... | collective-permute-start | bytes 393224 | tf_op jit(solution)/shard_map/ppermute | solution.py:545
  28.4 1.4 %collective-permute-start.16 = (f32[8,32,128]{2,1,0:T(8,128)S(1)}, f32[8,32,128]{2,1,0:T(8,128)S(1)}, u32[]{:S(2)}, u32[]{:S(2)}) collective-permute-start(f32[8,32,128]{2,1,0:T(8,128)S(1)} %get-tuple-element.61), channel_id=1, source_target_pairs={{0,1},{1,0},{2,3},{3,2},{4,5},{5,4},{6,7},{7,6},{8,9},{9,8},{10,11... | collective-permute-start | bytes 393224 | tf_op jit(solution)/shard_map/ppermute | solution.py:545
  28.8 1.3 %collective-permute-start.17 = (f32[8,32,128]{2,1,0:T(8,128)S(1)}, f32[8,32,128]{2,1,0:T(8,128)S(1)}, u32[]{:S(2)}, u32[]{:S(2)}) collective-permute-start(f32[8,32,128]{2,1,0:T(8,128)S(1)} %get-tuple-element.62), channel_id=1, source_target_pairs={{0,1},{1,0},{2,3},{3,2},{4,5},{5,4},{6,7},{7,6},{8,9},{9,8},{10,11... | collective-permute-start | bytes 393224 | tf_op jit(solution)/shard_map/ppermute | solution.py:545
  29.0 1.4 %collective-permute-start.18 = (f32[8,32,128]{2,1,0:T(8,128)S(1)}, f32[8,32,128]{2,1,0:T(8,128)S(1)}, u32[]{:S(2)}, u32[]{:S(2)}) collective-permute-start(f32[8,32,128]{2,1,0:T(8,128)S(1)} %get-tuple-element.63), channel_id=1, source_target_pairs={{0,1},{1,0},{2,3},{3,2},{4,5},{5,4},{6,7},{7,6},{8,9},{9,8},{10,11... | collective-permute-start | bytes 393224 | tf_op jit(solution)/shard_map/ppermute | solution.py:545

commit v2 on v1

--- a/solution.py
+++ b/solution.py
@@ -195,15 +195,12 @@
     return values.reshape(-1, values.shape[-1])
 
 
-def kernel_primitives(
-    rho_in, mom_in, ene_in, conserved, own, first, second, up, down, arrived
-):
-    rho = conserved.at[0]
-    mom = conserved.at[1:4]
-    ene = conserved.at[4]
+def kernel_inputs(rho_in, mom_in, ene_in, conserved, first, arrived):
     copies = [
-        pltpu.make_async_copy(source, target, arrived.at[k])
-        for k, (source, target) in enumerate(((rho_in, rho), (mom_in, mom), (ene_in, ene)))
+        pltpu.make_async_copy(source, conserved.at[part], arrived.at[k])
+        for k, (source, part) in enumerate(
+            ((rho_in, 0), (mom_in, slice(1, 4)), (ene_in, 4))
+        )
     ]
     for copy in copies:
         copy.start()
@@ -211,28 +208,36 @@
         copy.wait()
 
     def plane(x, carry):
-        density = rho[x]
+        inverse = 1.0 / conserved[0, x]
+        first[0, x] = conserved[1, x] * inverse
+        first[1, x] = conserved[3, x] * inverse
+        return carry
+
+    lax.fori_loop(0, CX, plane, 0, unroll=2)
+
+
+def kernel_primitives(conserved, first, own, second, up, down):
+    def plane(x, carry):
+        density = conserved[0, x]
         inverse = 1.0 / density
-        u = mom[0, x] * inverse
-        v = mom[1, x] * inverse
-        w = mom[2, x] * inverse
-        kinetic = 0.5 * (mom[0, x] * u + mom[1, x] * v + mom[2, x] * w)
-        temperature = (heat_ratio - 1.0) * (ene[x] - kinetic) * inverse
+        u = first[0, x]
+        w = first[1, x]
+        v = conserved[2, x] * inverse
+        kinetic = 0.5 * (conserved[1, x] * u + conserved[2, x] * v + conserved[3, x] * w)
+        temperature = (heat_ratio - 1.0) * (conserved[4, x] - kinetic) * inverse
         own[U, x] = u
         own[W, x] = w
         own[V, x] = v
         own[T, x] = temperature
-        first[0, x] = u
-        first[1, x] = w
         second[0, x] = v
         second[1, x] = temperature
         second[2, x] = density
         return carry
 
-    lax.fori_loop(0, CX, plane, 0)
+    lax.fori_loop(0, CX, plane, 0, unroll=2)
 
     def sums(f, carry):
-        for rows in row_chunks(rho.shape[1]):
+        for rows in row_chunks(own.shape[2]):
             halo_sums(own, f, rows, up, down)
         return carry
 
@@ -433,21 +438,25 @@
 
 
 def kernel_finish(
-    conserved, total, mate_0, mate_1, mate_2, mate_3, mate_4, tendency, advanced
+    conserved, total, mate_0, mate_1, mate_2, mate_3, mate_4, tendency, advanced,
+    rate, state, sent,
 ):
+    copies = []
     for f, from_mate in enumerate((mate_0, mate_1, mate_2, mate_3, mate_4)):
-
-        def plane(x, carry):
-            value = -(total[f, x] + from_mate[x])
-            tendency[f, x] = value
-            advanced[f, x] = conserved[f, x] + section_step * value
-            return carry
-
-        lax.fori_loop(0, CX, plane, 0, unroll=2)
-
-
-def call(kernel, outputs, operands, scratch=(), outside=False):
+        value = -(total[f] + from_mate[...])
+        rate[f] = value
+        state[f] = conserved[f] + section_step * value
+        for k, (source, target) in enumerate(((rate, tendency), (state, advanced))):
+            copy = pltpu.make_async_copy(source.at[f], target.at[f], sent.at[2 * f + k])
+            copy.start()
+            copies.append(copy)
+    for copy in copies:
+        copy.wait()
+
+
+def call(kernel, outputs, operands, scratch=(), outside=False, written=False):
     space = pltpu.HBM if outside else pltpu.VMEM
+    target = pltpu.HBM if written else pltpu.VMEM
     in_specs = [pl.BlockSpec(memory_space=space) for _ in operands]
     if outside:
         operands = [pltpu.with_memory_space_constraint(value, pltpu.HBM) for value in operands]
@@ -457,7 +466,7 @@
         kernel,
         out_shape=[jax.ShapeDtypeStruct(shape, F32) for shape in outputs],
         in_specs=in_specs,
-        out_specs=[pl.BlockSpec(memory_space=pltpu.VMEM) for _ in outputs],
+        out_specs=[pl.BlockSpec(memory_space=target) for _ in outputs],
         scratch_shapes=list(scratch),
         cost_estimate=pl.CostEstimate(flops=0, bytes_accessed=touched, transcendentals=0),
         compiler_params=pltpu.CompilerParams(vmem_limit_bytes=24 * 1024 * 1024),
@@ -482,12 +491,17 @@
     to_mate = [(i, i ^ 1) for i in range(4)]
     to_peer = [(i, i ^ 2) for i in range(4)]
 
-    conserved, own, first, second, up, down = call(
-        kernel_primitives,
-        [(5,) + block, (4,) + block, (2,) + block, (3,) + block, (4,) + sums, (4,) + sums],
+    conserved, first = call(
+        kernel_inputs,
+        [(5,) + block, (2,) + block],
         (rho, mom, ene),
         scratch=(pltpu.SemaphoreType.DMA((3,)),),
         outside=True,
+    )
+    own, second, up, down = call(
+        kernel_primitives,
+        [(4,) + block, (3,) + block, (4,) + sums, (4,) + sums],
+        (conserved, first),
     )
     peer_first = lax.ppermute(first, "gy", to_peer)
     before = lax.ppermute(up, "gx", ring_up)
@@ -547,7 +561,15 @@
         kernel_add_stream, [(5,) + block], (total, flux, flux_before, flux_after)
     )
     tendency, advanced = call(
-        kernel_finish, [(5,) + block, (5,) + block], (conserved, total, *from_mate)
+        kernel_finish,
+        [(5,) + block, (5,) + block],
+        (conserved, total, *from_mate),
+        scratch=(
+            pltpu.VMEM((5,) + block, F32),
+            pltpu.VMEM((5,) + block, F32),
+            pltpu.SemaphoreType.DMA((10,)),
+        ),
+        written=True,
     )
     return (
         jnp.transpose(tendency, (0, 1, 3, 2)),

time: 31.7 us -> 31.6 us (level)
    pallas_call x9 -> x10, Pallas kernels: 8.14 us -> 7.99 us  [call(): pl.pallas_call(kernel, out_shape=[jax.ShapeDtypeStruct(shape, F32) for sh...]
  transfers between devices with their start and end apart: 19 -> 19, of which waited for: 8 -> 8; matrix products, arithmetic and copies ran while one was open for 0% -> 0% of each run, Pallas kernels for 17% -> 18%
where the time goes in v2:
time: 31.6 us; the launch traced here: 31.5 us
  starting transfers between devices  17.1 us (54%)
  Pallas kernels  7.99 us (25%)
  waiting for transfers between devices  5.56 us (18%)
  between operations  0.79 us (2%)
    pallas_call x10, Pallas kernels, call(): pl.pallas_call(kernel, out_shape=[jax.ShapeDtypeStruct(shape, F32) for sh...  7.99 us
    ppermute x1, starting transfers between devices, fast_device(): flux_after = lax.ppermute(flux_down, 'gx', ring_down)  3.94 us
    ppermute x1, starting transfers between devices, fast_device(): after = lax.ppermute(down, 'gx', ring_down)  3.04 us
    ppermute x1, starting transfers between devices, fast_device(): peer_first = lax.ppermute(first, 'gy', to_peer)  3 us
    ppermute x1, waiting for transfers between devices, fast_device(): before = lax.ppermute(up, 'gx', ring_up)  2.24 us
    ppermute x1, starting transfers between devices, fast_device(): before = lax.ppermute(up, 'gx', ring_up)  2.01 us
    ppermute x1, starting transfers between devices, fast_device(): peer_third = lax.ppermute(third, 'gy', to_peer)  1.49 us
    ppermute x5, starting transfers between devices, fast_device(): from_mate = [lax.ppermute(value, 'gy', to_mate) for value in for_mate]  1.41 us
  transfers between devices with their start and end apart: 19, of which 8 were waited for; matrix products, arithmetic and copies ran while one was open for 0% of the time, Pallas kernels for 18%

profile of v2, /device:TPU:0, one launch (start us, length us, event | category | flops | bytes accessed | tf_op | source)
XLA Modules:
  0.0 31.5 jit_solution(1970382908984773618)
XLA Ops:
  0.6 1.2 %shard_map.104 = (f32[5,8,32,128]{3,2,1,0:T(8,128)S(1)}, f32[2,8,32,128]{3,2,1,0:T(8,128)S(1)}) custom-call(f32[8,32,128]{2,1,0:T(8,128)} %bitcast.6, f32[3,8,32,128]{3,2,1,0:T(8,128)} %bitcast.5, f32[8,32,128]{2,1,0:T(8,128)} %bitcast.7), custom_call_target="tpu_custom_call" | custom-call | bytes 1572864 | tf_op jit(solution)/shard_map/pallas_call | solution.py:465
  1.8 3.0 %collective-permute-start = (f32[2,8,32,128]{3,2,1,0:T(8,128)S(1)}, f32[2,8,32,128]{3,2,1,0:T(8,128)S(1)}, u32[]{:S(2)}, u32[]{:S(2)}) collective-permute-start(f32[2,8,32,128]{3,2,1,0:T(8,128)S(1)} %get-tuple-element.35.first), channel_id=1, source_target_pairs={{0,2},{1,3},{2,0},{3,1},{4,6},{5,7},{6,4},{7,5},{8,10},{9,11},{10,... | collective-permute-start | bytes 786440 | tf_op jit(solution)/shard_map/ppermute | solution.py:506
  4.8 0.2 shard_map.105
  5.0 0.1 collective-permute-start.4
  5.1 2.0 %collective-permute-start.1 = (f32[4,2,32,128]{3,2,1,0:T(8,128)S(1)}, f32[4,2,32,128]{3,2,1,0:T(8,128)S(1)}, u32[]{:S(2)}, u32[]{:S(2)}) collective-permute-start(f32[4,2,32,128]{3,2,1,0:T(8,128)S(1)} %get-tuple-element.37), channel_id=1, source_target_pairs={{0,4},{4,8},{8,12},{12,16},{16,20},{20,24},{24,28},{28,0},{1,5},{5... | collective-permute-start | bytes 393224 | tf_op jit(solution)/shard_map/ppermute | solution.py:507
  7.1 3.0 %collective-permute-start.2 = (f32[4,2,32,128]{3,2,1,0:T(8,128)S(1)}, f32[4,2,32,128]{3,2,1,0:T(8,128)S(1)}, u32[]{:S(2)}, u32[]{:S(2)}) collective-permute-start(f32[4,2,32,128]{3,2,1,0:T(8,128)S(1)} %get-tuple-element.38), channel_id=1, source_target_pairs={{4,0},{8,4},{12,8},{16,12},{20,16},{24,20},{28,24},{0,28},{5,1},{9... | collective-permute-start | bytes 393224 | tf_op jit(solution)/shard_map/ppermute | solution.py:508
  10.2 0.7 %shard_map.106 = (f32[4,8,32,128]{3,2,1,0:T(8,128)S(1)}, f32[8,32,128]{2,1,0:T(8,128)S(1)}, f32[8,32,128]{2,1,0:T(8,128)S(1)}, f32[8,32,128]{2,1,0:T(8,128)S(1)}, f32[2,8,32,128]{3,2,1,0:T(8,128)S(1)}) custom-call(f32[4,8,32,128]{3,2,1,0:T(8,128)S(1)} %get-tuple-element.36.own, bf16[256,256]{1,0:T(8,128)(2,1)S(1)} %copy-done.2, bf16[256,256]{1,0:T(8,128)(2,1)S(1)} %copy-done.3), custom_call_target="tpu_custom_call" | custom-call | bytes 1966080 | tf_op jit(solution)/shard_map/pallas_call | solution.py:465
  11.0 2.2 %collective-permute-done.1.before = f32[4,2,32,128]{3,2,1,0:T(8,128)S(1)} collective-permute-done((f32[4,2,32,128]{3,2,1,0:T(8,128)S(1)}, f32[4,2,32,128]{3,2,1,0:T(8,128)S(1)}, u32[]{:S(2)}, u32[]{:S(2)}) %collective-permute-start.1) | collective-permute-done | bytes 131104 | tf_op jit(solution)/shard_map/ppermute | solution.py:507
  13.2 1.3 %collective-permute-done.2.after = f32[4,2,32,128]{3,2,1,0:T(8,128)S(1)} collective-permute-done((f32[4,2,32,128]{3,2,1,0:T(8,128)S(1)}, f32[4,2,32,128]{3,2,1,0:T(8,128)S(1)}, u32[]{:S(2)}, u32[]{:S(2)}) %collective-permute-start.2) | collective-permute-done | bytes 131104 | tf_op jit(solution)/shard_map/ppermute | solution.py:508
  14.5 0.3 %shard_map.107 = (f32[4,8,32,128]{3,2,1,0:T(8,128)S(1)}, f32[2,8,32,128]{3,2,1,0:T(8,128)S(1)}, f32[8,32,128]{2,1,0:T(8,128)S(1)}, f32[8,32,128]{2,1,0:T(8,128)S(1)}) custom-call(f32[4,8,32,128]{3,2,1,0:T(8,128)S(1)} %get-tuple-element.36.own, f32[4,2,32,128]{3,2,1,0:T(8,128)S(1)} %collective-permute-done.1.before, ...), custom_call_target="tpu_custom_call" | custom-call | bytes 2228224 | tf_op jit(solution)/shard_map/pallas_call | solution.py:465
  14.9 0.6 %collective-permute-start.8 = (f32[8,32,128]{2,1,0:T(8,128)S(1)}, f32[8,32,128]{2,1,0:T(8,128)S(1)}, u32[]{:S(2)}, u32[]{:S(2)}) collective-permute-start(f32[8,32,128]{2,1,0:T(8,128)S(1)} %get-tuple-element.45), channel_id=1, source_target_pairs={{0,1},{1,0},{2,3},{3,2},{4,5},{5,4},{6,7},{7,6},{8,9},{9,8},{10,11... | collective-permute-start | bytes 393224 | tf_op jit(solution)/shard_map/ppermute | solution.py:522
  15.5 0.3 %collective-permute-done.7.mate_w = f32[8,32,128]{2,1,0:T(8,128)S(1)} collective-permute-done((f32[8,32,128]{2,1,0:T(8,128)S(1)}, f32[8,32,128]{2,1,0:T(8,128)S(1)}, u32[]{:S(2)}, u32[]{:S(2)}) %collective-permute-start.7) | collective-permute-done | bytes 131104 | tf_op jit(solution)/shard_map/ppermute | solution.py:514
  15.8 1.5 %collective-permute-start.3 = (f32[2,8,32,128]{3,2,1,0:T(8,128)S(1)}, f32[2,8,32,128]{3,2,1,0:T(8,128)S(1)}, u32[]{:S(2)}, u32[]{:S(2)}) collective-permute-start(f32[2,8,32,128]{3,2,1,0:T(8,128)S(1)} %get-tuple-element.40.third), channel_id=1, source_target_pairs={{0,2},{1,3},{2,0},{3,1},{4,6},{5,7},{6,4},{7,5},{8,10},{9,11},{10,... | collective-permute-start | bytes 786440 | tf_op jit(solution)/shard_map/ppermute | solution.py:523
  17.4 0.9 %shard_map.108 = (f32[2,256,256]{2,1,0:T(8,128)S(1)}, f32[5,8,32,128]{3,2,1,0:T(8,128)S(1)}, f32[5,2,32,128]{3,2,1,0:T(8,128)S(1)}, f32[5,2,32,128]{3,2,1,0:T(8,128)S(1)}) custom-call(f32[4,8,32,128]{3,2,1,0:T(8,128)S(1)} %get-tuple-element.36.own, f32[3,8,32,128]{3,2,1,0:T(8,128)S(1)} %get-tuple-element.41.second, ...), custom_call_target="tpu_custom_call" | custom-call | bytes 5439488 | tf_op jit(solution)/shard_map/pallas_call | solution.py:465
  18.3 0.8 %collective-permute-start.12 = (f32[5,2,32,128]{3,2,1,0:T(8,128)S(1)}, f32[5,2,32,128]{3,2,1,0:T(8,128)S(1)}, u32[]{:S(2)}, u32[]{:S(2)}) collective-permute-start(f32[5,2,32,128]{3,2,1,0:T(8,128)S(1)} %get-tuple-element.57), channel_id=1, source_target_pairs={{0,4},{4,8},{8,12},{12,16},{16,20},{20,24},{24,28},{28,0},{1,5},{5... | collective-permute-start | bytes 491528 | tf_op jit(solution)/shard_map/ppermute | solution.py:532
  19.1 3.9 %collective-permute-start.13 = (f32[5,2,32,128]{3,2,1,0:T(8,128)S(1)}, f32[5,2,32,128]{3,2,1,0:T(8,128)S(1)}, u32[]{:S(2)}, u32[]{:S(2)}) collective-permute-start(f32[5,2,32,128]{3,2,1,0:T(8,128)S(1)} %get-tuple-element.58), channel_id=1, source_target_pairs={{4,0},{8,4},{12,8},{16,12},{20,16},{24,20},{28,24},{0,28},{5,1},{9... | collective-permute-start | bytes 491528 | tf_op jit(solution)/shard_map/ppermute | solution.py:533
  23.1 0.4 %shard_map.109 = (f32[8,32,128]{2,1,0:T(8,128)S(1)}, f32[8,32,128]{2,1,0:T(8,128)S(1)}, f32[2,256,128]{2,1,0:T(8,128)S(1)}) custom-call(f32[2,8,32,128]{3,2,1,0:T(8,128)S(1)} %collective-permute-done.peer_first, f32[3,8,32,128]{3,2,1,0:T(8,128)S(1)} %collective-permute-done.4.peer_second, f32[5,8,32,128]{3,2,1,0:T(8,128)S(1)} %get-tuple-element.49.flux, ...), custom_call_target="tpu_custom_call" | custom-call | bytes 2097152 | tf_op jit(solution)/shard_map/pallas_call | solution.py:465
  23.5 0.5 %collective-permute-start.11 = (f32[8,32,128]{2,1,0:T(8,128)S(1)}, f32[8,32,128]{2,1,0:T(8,128)S(1)}, u32[]{:S(2)}, u32[]{:S(2)}) collective-permute-start(f32[8,32,128]{2,1,0:T(8,128)S(1)} %get-tuple-element.51), channel_id=1, source_target_pairs={{0,1},{1,0},{2,3},{3,2},{4,5},{5,4},{6,7},{7,6},{8,9},{9,8},{10,11... | collective-permute-start | bytes 393224 | tf_op jit(solution)/shard_map/ppermute | solution.py:540
  24.0 0.8 %collective-permute-done.10.across_v = f32[8,32,128]{2,1,0:T(8,128)S(1)} collective-permute-done((f32[8,32,128]{2,1,0:T(8,128)S(1)}, f32[8,32,128]{2,1,0:T(8,128)S(1)}, u32[]{:S(2)}, u32[]{:S(2)}) %collective-permute-start.10) | collective-permute-done | bytes 131104 | tf_op jit(solution)/shard_map/ppermute | solution.py:539
  24.8 0.2 collective-permute-done.11.across_t
  25.0 2.3 %shard_map.110 = (f32[5,8,32,128]{3,2,1,0:T(8,128)S(1)}, f32[5,8,32,128]{3,2,1,0:T(8,128)S(1)}) custom-call(f32[4,8,32,128]{3,2,1,0:T(8,128)S(1)} %get-tuple-element.36.own, f32[3,8,32,128]{3,2,1,0:T(8,128)S(1)} %get-tuple-element.41.second, f32[2,8,32,128]{3,2,1,0:T(8,128)S(1)} %collective-permute-done.peer_first, ...), custom_call_target="tpu_custom_call" | custom-call | bytes 7208960 | tf_op jit(solution)/shard_map/pallas_call | solution.py:465
  27.3 0.5 %shard_map.111 = (f32[5,8,32,128]{3,2,1,0:T(8,128)S(1)}, f32[8,32,128]{2,1,0:T(8,128)S(1)}, f32[8,32,128]{2,1,0:T(8,128)S(1)}, f32[8,32,128]{2,1,0:T(8,128)S(1)}...) custom-call(f32[4,8,32,128]{3,2,1,0:T(8,128)S(1)} %get-tuple-element.36.own, ...), custom_call_target="tpu_custom_call" | custom-call | bytes 4456448 | tf_op jit(solution)/shard_map/pallas_call | solution.py:465
  27.9 0.4 %collective-permute-start.14 = (f32[8,32,128]{2,1,0:T(8,128)S(1)}, f32[8,32,128]{2,1,0:T(8,128)S(1)}, u32[]{:S(2)}, u32[]{:S(2)}) collective-permute-start(f32[8,32,128]{2,1,0:T(8,128)S(1)} %get-tuple-element.59), channel_id=1, source_target_pairs={{0,1},{1,0},{2,3},{3,2},{4,5},{5,4},{6,7},{7,6},{8,9},{9,8},{10,11... | collective-permute-start | bytes 393224 | tf_op jit(solution)/shard_map/ppermute | solution.py:559
  28.3 0.2 collective-permute-start.15
  28.4 0.3 %collective-permute-start.16 = (f32[8,32,128]{2,1,0:T(8,128)S(1)}, f32[8,32,128]{2,1,0:T(8,128)S(1)}, u32[]{:S(2)}, u32[]{:S(2)}) collective-permute-start(f32[8,32,128]{2,1,0:T(8,128)S(1)} %get-tuple-element.61), channel_id=1, source_target_pairs={{0,1},{1,0},{2,3},{3,2},{4,5},{5,4},{6,7},{7,6},{8,9},{9,8},{10,11... | collective-permute-start | bytes 393224 | tf_op jit(solution)/shard_map/ppermute | solution.py:559
  28.8 0.2 collective-permute-start.17
  29.0 0.3 %collective-permute-start.18 = (f32[8,32,128]{2,1,0:T(8,128)S(1)}, f32[8,32,128]{2,1,0:T(8,128)S(1)}, u32[]{:S(2)}, u32[]{:S(2)}) collective-permute-start(f32[8,32,128]{2,1,0:T(8,128)S(1)} %get-tuple-element.63), channel_id=1, source_target_pairs={{0,1},{1,0},{2,3},{3,2},{4,5},{5,4},{6,7},{7,6},{8,9},{9,8},{10,11... | collective-permute-start | bytes 393224 | tf_op jit(solution)/shard_map/ppermute | solution.py:559
  29.3 0.4 %shard_map.112.total = f32[5,8,32,128]{3,2,1,0:T(8,128)S(1)} custom-call(f32[5,8,32,128]{3,2,1,0:T(8,128)S(1)} %get-tuple-element.56.total, f32[5,8,32,128]{3,2,1,0:T(8,128)S(1)} %get-tuple-element.49.flux, f32[5,2,32,128]{3,2,1,0:T(8,128)S(1)} %collective-permute-done.12.before, f32[5,2,32,128]{3,2,1,0:T(8,128)S(1)} %collective-permute-done.13.after), custom_call_target="tpu_custom_call" | custom-call | bytes 2293760 | tf_op jit(solution)/shard_map/pallas_call | solution.py:465
  29.7 0.1 collective-permute-done.16.mate_2
  29.8 0.3 %collective-permute-done.17.mate_3 = f32[8,32,128]{2,1,0:T(8,128)S(1)} collective-permute-done((f32[8,32,128]{2,1,0:T(8,128)S(1)}, f32[8,32,128]{2,1,0:T(8,128)S(1)}, u32[]{:S(2)}, u32[]{:S(2)}) %collective-permute-start.17) | collective-permute-done | bytes 131104 | tf_op jit(solution)/shard_map/ppermute | solution.py:559
  30.1 0.2 collective-permute-done.18.mate_4
  30.3 1.2 %shard_map.113 = (f32[5,8,32,128]{3,2,1,0:T(8,128)}, f32[5,8,32,128]{3,2,1,0:T(8,128)}) custom-call(f32[5,8,32,128]{3,2,1,0:T(8,128)S(1)} %get-tuple-element.34.conserved, f32[5,8,32,128]{3,2,1,0:T(8,128)S(1)} %shard_map.112.total, f32[8,32,128]{2,1,0:T(8,128)S(1)} %collective-permute-done.14.mate_0, f32[8,32,128]{2,1,0:T(8,128)S(1)} %collective-permute-done.15.mate_1, ...), custom_call_target="tpu_custom_call" | custom-call | bytes 3276800 | tf_op jit(solution)/shard_map/pallas_call | solution.py:465
  (28 shorter events, 0.3 us)
Async XLA Ops:
  1.8 12.7 %collective-permute-start = (f32[2,8,32,128]{3,2,1,0:T(8,128)S(1)}, f32[2,8,32,128]{3,2,1,0:T(8,128)S(1)}, u32[]{:S(2)}, u32[]{:S(2)}) collective-permute-start(f32[2,8,32,128]{3,2,1,0:T(8,128)S(1)} %get-tuple-element.35.first), channel_id=1, source_target_pairs={{0,2},{1,3},{2,0},{3,1},{4,6},{5,7},{6,4},{7,5},{8,10},{9,11},{10,... | collective-permute-start | bytes 786440 | tf_op jit(solution)/shard_map/ppermute | solution.py:506
  4.8 5.4 %copy-start.2 = (bf16[256,256]{1,0:T(8,128)(2,1)S(1)}, bf16[256,256]{1,0:T(8,128)(2,1)}, u32[]{:S(2)}) copy-start(bf16[256,256]{1,0:T(8,128)(2,1)} %constant.16.clone.y_high) | copy-start | bytes 393220
  4.8 5.4 %copy-start.3 = (bf16[256,256]{1,0:T(8,128)(2,1)S(1)}, bf16[256,256]{1,0:T(8,128)(2,1)}, u32[]{:S(2)}) copy-start(bf16[256,256]{1,0:T(8,128)(2,1)} %constant.17.clone.y_low) | copy-start | bytes 393220
  5.0 18.1 %collective-permute-start.4 = (f32[3,8,32,128]{3,2,1,0:T(8,128)S(1)}, f32[3,8,32,128]{3,2,1,0:T(8,128)S(1)}, u32[]{:S(2)}, u32[]{:S(2)}) collective-permute-start(f32[3,8,32,128]{3,2,1,0:T(8,128)S(1)} %get-tuple-element.41.second), channel_id=1, source_target_pairs={{0,2},{1,3},{2,0},{3,1},{4,6},{5,7},{6,4},{7,5},{8,10},{9,11},{10,... | collective-permute-start | bytes 1179656 | tf_op jit(solution)/shard_map/ppermute | solution.py:516
  5.1 8.1 %collective-permute-start.1 = (f32[4,2,32,128]{3,2,1,0:T(8,128)S(1)}, f32[4,2,32,128]{3,2,1,0:T(8,128)S(1)}, u32[]{:S(2)}, u32[]{:S(2)}) collective-permute-start(f32[4,2,32,128]{3,2,1,0:T(8,128)S(1)} %get-tuple-element.37), channel_id=1, source_target_pairs={{0,4},{4,8},{8,12},{12,16},{16,20},{20,24},{24,28},{28,0},{1,5},{5... | collective-permute-start | bytes 393224 | tf_op jit(solution)/shard_map/ppermute | solution.py:507
  7.1 7.4 %collective-permute-start.2 = (f32[4,2,32,128]{3,2,1,0:T(8,128)S(1)}, f32[4,2,32,128]{3,2,1,0:T(8,128)S(1)}, u32[]{:S(2)}, u32[]{:S(2)}) collective-permute-start(f32[4,2,32,128]{3,2,1,0:T(8,128)S(1)} %get-tuple-element.38), channel_id=1, source_target_pairs={{4,0},{8,4},{12,8},{16,12},{20,16},{24,20},{28,24},{0,28},{5,1},{9... | collective-permute-start | bytes 393224 | tf_op jit(solution)/shard_map/ppermute | solution.py:508
  10.9 4.5 %collective-permute-start.6 = (f32[8,32,128]{2,1,0:T(8,128)S(1)}, f32[8,32,128]{2,1,0:T(8,128)S(1)}, u32[]{:S(2)}, u32[]{:S(2)}) collective-permute-start(f32[8,32,128]{2,1,0:T(8,128)S(1)} %get-tuple-element.43), channel_id=1, source_target_pairs={{0,1},{1,0},{2,3},{3,2},{4,5},{5,4},{6,7},{7,6},{8,9},{9,8},{10,11... | collective-permute-start | bytes 393224 | tf_op jit(solution)/shard_map/ppermute | solution.py:514
  13.2 10.3 %collective-permute-start.5 = (f32[2,8,32,128]{3,2,1,0:T(8,128)S(1)}, f32[2,8,32,128]{3,2,1,0:T(8,128)S(1)}, u32[]{:S(2)}, u32[]{:S(2)}) collective-permute-start(f32[2,8,32,128]{3,2,1,0:T(8,128)S(1)} %get-tuple-element.42), channel_id=1, source_target_pairs={{0,1},{1,0},{2,3},{3,2},{4,5},{5,4},{6,7},{7,6},{8,9},{9,8},{10,11... | collective-permute-start | bytes 786440 | tf_op jit(solution)/shard_map/ppermute | solution.py:515
  14.5 1.3 %collective-permute-start.7 = (f32[8,32,128]{2,1,0:T(8,128)S(1)}, f32[8,32,128]{2,1,0:T(8,128)S(1)}, u32[]{:S(2)}, u32[]{:S(2)}) collective-permute-start(f32[8,32,128]{2,1,0:T(8,128)S(1)} %get-tuple-element.44), channel_id=1, source_target_pairs={{0,1},{1,0},{2,3},{3,2},{4,5},{5,4},{6,7},{7,6},{8,9},{9,8},{10,11... | collective-permute-start | bytes 393224 | tf_op jit(solution)/shard_map/ppermute | solution.py:514
  14.5 2.8 %copy-start = (bf16[2,512,256]{2,1,0:T(8,128)(2,1)S(1)}, bf16[2,512,256]{2,1,0:T(8,128)(2,1)}, u32[]{:S(2)}) copy-start(bf16[2,512,256]{2,1,0:T(8,128)(2,1)} %constant.12.clone.z_high) | copy-start | bytes 1572868
  14.5 2.8 %copy-start.1 = (bf16[2,512,256]{2,1,0:T(8,128)(2,1)S(1)}, bf16[2,512,256]{2,1,0:T(8,128)(2,1)}, u32[]{:S(2)}) copy-start(bf16[2,512,256]{2,1,0:T(8,128)(2,1)} %constant.13.clone.z_low) | copy-start | bytes 1572868
  14.9 2.5 %collective-permute-start.8 = (f32[8,32,128]{2,1,0:T(8,128)S(1)}, f32[8,32,128]{2,1,0:T(8,128)S(1)}, u32[]{:S(2)}, u32[]{:S(2)}) collective-permute-start(f32[8,32,128]{2,1,0:T(8,128)S(1)} %get-tuple-element.45), channel_id=1, source_target_pairs={{0,1},{1,0},{2,3},{3,2},{4,5},{5,4},{6,7},{7,6},{8,9},{9,8},{10,11... | collective-permute-start | bytes 393224 | tf_op jit(solution)/shard_map/ppermute | solution.py:522
  15.4 1.9 %collective-permute-start.9 = (f32[8,32,128]{2,1,0:T(8,128)S(1)}, f32[8,32,128]{2,1,0:T(8,128)S(1)}, u32[]{:S(2)}, u32[]{:S(2)}) collective-permute-start(f32[8,32,128]{2,1,0:T(8,128)S(1)} %get-tuple-element.46), channel_id=1, source_target_pairs={{0,1},{1,0},{2,3},{3,2},{4,5},{5,4},{6,7},{7,6},{8,9},{9,8},{10,11... | collective-permute-start | bytes 393224 | tf_op jit(solution)/shard_map/ppermute | solution.py:522
  15.8 11.5 %collective-permute-start.3 = (f32[2,8,32,128]{3,2,1,0:T(8,128)S(1)}, f32[2,8,32,128]{3,2,1,0:T(8,128)S(1)}, u32[]{:S(2)}, u32[]{:S(2)}) collective-permute-start(f32[2,8,32,128]{3,2,1,0:T(8,128)S(1)} %get-tuple-element.40.third), channel_id=1, source_target_pairs={{0,2},{1,3},{2,0},{3,1},{4,6},{5,7},{6,4},{7,5},{8,10},{9,11},{10,... | collective-permute-start | bytes 786440 | tf_op jit(solution)/shard_map/ppermute | solution.py:523
  18.3 10.5 %collective-permute-start.12 = (f32[5,2,32,128]{3,2,1,0:T(8,128)S(1)}, f32[5,2,32,128]{3,2,1,0:T(8,128)S(1)}, u32[]{:S(2)}, u32[]{:S(2)}) collective-permute-start(f32[5,2,32,128]{3,2,1,0:T(8,128)S(1)} %get-tuple-element.57), channel_id=1, source_target_pairs={{0,4},{4,8},{8,12},{12,16},{16,20},{20,24},{24,28},{28,0},{1,5},{5... | collective-permute-start | bytes 491528 | tf_op jit(solution)/shard_map/ppermute | solution.py:532
  19.1 9.8 %collective-permute-start.13 = (f32[5,2,32,128]{3,2,1,0:T(8,128)S(1)}, f32[5,2,32,128]{3,2,1,0:T(8,128)S(1)}, u32[]{:S(2)}, u32[]{:S(2)}) collective-permute-start(f32[5,2,32,128]{3,2,1,0:T(8,128)S(1)} %get-tuple-element.58), channel_id=1, source_target_pairs={{4,0},{8,4},{12,8},{16,12},{20,16},{24,20},{28,24},{0,28},{5,1},{9... | collective-permute-start | bytes 491528 | tf_op jit(solution)/shard_map/ppermute | solution.py:533
  23.1 2.0 %copy-start.4 = (bf16[2,256,256]{2,1,0:T(8,128)(2,1)S(1)}, bf16[2,256,256]{2,1,0:T(8,128)(2,1)}, u32[]{:S(2)}) copy-start(bf16[2,256,256]{2,1,0:T(8,128)(2,1)} %constant.14.clone.f_high) | copy-start | bytes 786436
  23.1 2.0 %copy-start.5 = (bf16[2,256,256]{2,1,0:T(8,128)(2,1)S(1)}, bf16[2,256,256]{2,1,0:T(8,128)(2,1)}, u32[]{:S(2)}) copy-start(bf16[2,256,256]{2,1,0:T(8,128)(2,1)} %constant.15.clone.f_low) | copy-start | bytes 786436
  23.4 1.4 %collective-permute-start.10 = (f32[8,32,128]{2,1,0:T(8,128)S(1)}, f32[8,32,128]{2,1,0:T(8,128)S(1)}, u32[]{:S(2)}, u32[]{:S(2)}) collective-permute-start(f32[8,32,128]{2,1,0:T(8,128)S(1)} %get-tuple-element.50), channel_id=1, source_target_pairs={{0,1},{1,0},{2,3},{3,2},{4,5},{5,4},{6,7},{7,6},{8,9},{9,8},{10,11... | collective-permute-start | bytes 393224 | tf_op jit(solution)/shard_map/ppermute | solution.py:539
  23.5 1.5 %collective-permute-start.11 = (f32[8,32,128]{2,1,0:T(8,128)S(1)}, f32[8,32,128]{2,1,0:T(8,128)S(1)}, u32[]{:S(2)}, u32[]{:S(2)}) collective-permute-start(f32[8,32,128]{2,1,0:T(8,128)S(1)} %get-tuple-element.51), channel_id=1, source_target_pairs={{0,1},{1,0},{2,3},{3,2},{4,5},{5,4},{6,7},{7,6},{8,9},{9,8},{10,11... | collective-permute-start | bytes 393224 | tf_op jit(solution)/shard_map/ppermute | solution.py:540
  27.9 1.8 %collective-permute-start.14 = (f32[8,32,128]{2,1,0:T(8,128)S(1)}, f32[8,32,128]{2,1,0:T(8,128)S(1)}, u32[]{:S(2)}, u32[]{:S(2)}) collective-permute-start(f32[8,32,128]{2,1,0:T(8,128)S(1)} %get-tuple-element.59), channel_id=1, source_target_pairs={{0,1},{1,0},{2,3},{3,2},{4,5},{5,4},{6,7},{7,6},{8,9},{9,8},{10,11... | collective-permute-start | bytes 393224 | tf_op jit(solution)/shard_map/ppermute | solution.py:559
  28.3 1.4 %collective-permute-start.15 = (f32[8,32,128]{2,1,0:T(8,128)S(1)}, f32[8,32,128]{2,1,0:T(8,128)S(1)}, u32[]{:S(2)}, u32[]{:S(2)}) collective-permute-start(f32[8,32,128]{2,1,0:T(8,128)S(1)} %get-tuple-element.60), channel_id=1, source_target_pairs={{0,1},{1,0},{2,3},{3,2},{4,5},{5,4},{6,7},{7,6},{8,9},{9,8},{10,11... | collective-permute-start | bytes 393224 | tf_op jit(solution)/shard_map/ppermute | solution.py:559
  28.4 1.3 %collective-permute-start.16 = (f32[8,32,128]{2,1,0:T(8,128)S(1)}, f32[8,32,128]{2,1,0:T(8,128)S(1)}, u32[]{:S(2)}, u32[]{:S(2)}) collective-permute-start(f32[8,32,128]{2,1,0:T(8,128)S(1)} %get-tuple-element.61), channel_id=1, source_target_pairs={{0,1},{1,0},{2,3},{3,2},{4,5},{5,4},{6,7},{7,6},{8,9},{9,8},{10,11... | collective-permute-start | bytes 393224 | tf_op jit(solution)/shard_map/ppermute | solution.py:559
  28.8 1.3 %collective-permute-start.17 = (f32[8,32,128]{2,1,0:T(8,128)S(1)}, f32[8,32,128]{2,1,0:T(8,128)S(1)}, u32[]{:S(2)}, u32[]{:S(2)}) collective-permute-start(f32[8,32,128]{2,1,0:T(8,128)S(1)} %get-tuple-element.62), channel_id=1, source_target_pairs={{0,1},{1,0},{2,3},{3,2},{4,5},{5,4},{6,7},{7,6},{8,9},{9,8},{10,11... | collective-permute-start | bytes 393224 | tf_op jit(solution)/shard_map/ppermute | solution.py:559
  29.0 1.3 %collective-permute-start.18 = (f32[8,32,128]{2,1,0:T(8,128)S(1)}, f32[8,32,128]{2,1,0:T(8,128)S(1)}, u32[]{:S(2)}, u32[]{:S(2)}) collective-permute-start(f32[8,32,128]{2,1,0:T(8,128)S(1)} %get-tuple-element.63), channel_id=1, source_target_pairs={{0,1},{1,0},{2,3},{3,2},{4,5},{5,4},{6,7},{7,6},{8,9},{9,8},{10,11... | collective-permute-start | bytes 393224 | tf_op jit(solution)/shard_map/ppermute | solution.py:559

commit v3 on v2

--- a/solution.py
+++ b/solution.py
@@ -286,7 +286,7 @@
 
 def kernel_flux_x(
     own, second, peer_first, mate_u, mate_w, across_u, across_w, dx, dy, mu,
-    z_high, z_low, dz, flux, up, down,
+    z_high, z_low, dz, flux, down, up,
 ):
     width = own.shape[-1]
     odd = lax.rem(lax.axis_index("gy"), 2)
@@ -426,7 +426,7 @@
         for_mate[f][...] = part_mate[f] + spread[:, width:].reshape(shape)
 
 
-def kernel_add_stream(total, flux, before, after, result):
+def kernel_add_stream(total, flux, after, before, result):
     def field(f, carry):
         for rows in row_chunks(flux.shape[2]):
             derived = compact_x(extended(before, flux, after, f, rows))
@@ -521,7 +521,7 @@
     )
     across_u, across_w = (lax.ppermute(value, "gy", to_mate) for value in (for_u, for_w))
     peer_third = lax.ppermute(third, "gy", to_peer)
-    dz, flux, flux_up, flux_down = call(
+    dz, flux, flux_down, flux_up = call(
         kernel_flux_x,
         [(2, points, 2 * width), (5,) + block, (5,) + sums, (5,) + sums],
         (
@@ -529,8 +529,8 @@
             z_high, z_low,
         ),
     )
+    flux_after = lax.ppermute(flux_down, "gx", ring_down)
     flux_before = lax.ppermute(flux_up, "gx", ring_up)
-    flux_after = lax.ppermute(flux_down, "gx", ring_down)
     for_v, for_t, dy_peer = call(
         kernel_peer,
         [block, block, (2, points, width)],
@@ -558,7 +558,7 @@
     )
     from_mate = [lax.ppermute(value, "gy", to_mate) for value in for_mate]
     (total,) = call(
-        kernel_add_stream, [(5,) + block], (total, flux, flux_before, flux_after)
+        kernel_add_stream, [(5,) + block], (total, flux, flux_after, flux_before)
     )
     tendency, advanced = call(
         kernel_finish,

time: 31.6 us -> 32.9 us (1.041)
  waiting for transfers between devices: 5.56 us -> 8.34 us
  starting transfers between devices: 17.1 us -> 15.6 us
    ppermute x1, waiting for transfers between devices: 0.01 us -> 2.48 us  [fast_device(): flux_before = lax.ppermute(flux_up, 'gx', ring_up)]
    ppermute x1, starting transfers between devices: 0.83 us -> 0.01 us  [fast_device(): flux_before = lax.ppermute(flux_up, 'gx', ring_up)]
    ppermute x1, starting transfers between devices: 3.94 us -> 3.55 us  [fast_device(): flux_after = lax.ppermute(flux_down, 'gx', ring_down)]
  transfers between devices with their start and end apart: 19 -> 19, of which waited for: 8 -> 7; matrix products, arithmetic and copies ran while one was open for 0% -> 0% of each run, Pallas kernels for 18% -> 17%
where the time goes in v3:
time: 32.9 us; the launch traced here: 32.7 us
  starting transfers between devices  15.6 us (47%)
  waiting for transfers between devices  8.34 us (25%)
  Pallas kernels  7.99 us (24%)
  between operations  0.81 us (2%)
    pallas_call x10, Pallas kernels, call(): pl.pallas_call(kernel, out_shape=[jax.ShapeDtypeStruct(shape, F32) for sh...  7.99 us
    ppermute x1, starting transfers between devices, fast_device(): flux_after = lax.ppermute(flux_down, 'gx', ring_down)  3.55 us
    ppermute x1, starting transfers between devices, fast_device(): after = lax.ppermute(down, 'gx', ring_down)  3.04 us
    ppermute x1, starting transfers between devices, fast_device(): peer_first = lax.ppermute(first, 'gy', to_peer)  3 us
    ppermute x1, waiting for transfers between devices, fast_device(): flux_before = lax.ppermute(flux_up, 'gx', ring_up)  2.48 us
    ppermute x1, waiting for transfers between devices, fast_device(): before = lax.ppermute(up, 'gx', ring_up)  2.24 us
    ppermute x1, starting transfers between devices, fast_device(): before = lax.ppermute(up, 'gx', ring_up)  2.01 us
    ppermute x1, starting transfers between devices, fast_device(): peer_third = lax.ppermute(third, 'gy', to_peer)  1.49 us
  transfers between devices with their start and end apart: 19, of which 7 were waited for; matrix products, arithmetic and copies ran while one was open for 0% of the time, Pallas kernels for 17%

profile of v3, /device:TPU:0, one launch (start us, length us, event | category | flops | bytes accessed | tf_op | source)
XLA Modules:
  0.0 32.7 jit_solution(15656584217918933124)
XLA Ops:
  0.6 1.2 %shard_map.104 = (f32[5,8,32,128]{3,2,1,0:T(8,128)S(1)}, f32[2,8,32,128]{3,2,1,0:T(8,128)S(1)}) custom-call(f32[8,32,128]{2,1,0:T(8,128)} %bitcast.6, f32[3,8,32,128]{3,2,1,0:T(8,128)} %bitcast.5, f32[8,32,128]{2,1,0:T(8,128)} %bitcast.7), custom_call_target="tpu_custom_call" | custom-call | bytes 1572864 | tf_op jit(solution)/shard_map/pallas_call | solution.py:465
  1.8 3.0 %collective-permute-start = (f32[2,8,32,128]{3,2,1,0:T(8,128)S(1)}, f32[2,8,32,128]{3,2,1,0:T(8,128)S(1)}, u32[]{:S(2)}, u32[]{:S(2)}) collective-permute-start(f32[2,8,32,128]{3,2,1,0:T(8,128)S(1)} %get-tuple-element.35.first), channel_id=1, source_target_pairs={{0,2},{1,3},{2,0},{3,1},{4,6},{5,7},{6,4},{7,5},{8,10},{9,11},{10,... | collective-permute-start | bytes 786440 | tf_op jit(solution)/shard_map/ppermute | solution.py:506
  4.8 0.2 shard_map.105
  5.0 0.1 collective-permute-start.4
  5.1 2.0 %collective-permute-start.1 = (f32[4,2,32,128]{3,2,1,0:T(8,128)S(1)}, f32[4,2,32,128]{3,2,1,0:T(8,128)S(1)}, u32[]{:S(2)}, u32[]{:S(2)}) collective-permute-start(f32[4,2,32,128]{3,2,1,0:T(8,128)S(1)} %get-tuple-element.37), channel_id=1, source_target_pairs={{0,4},{4,8},{8,12},{12,16},{16,20},{20,24},{24,28},{28,0},{1,5},{5... | collective-permute-start | bytes 393224 | tf_op jit(solution)/shard_map/ppermute | solution.py:507
  7.1 3.0 %collective-permute-start.2 = (f32[4,2,32,128]{3,2,1,0:T(8,128)S(1)}, f32[4,2,32,128]{3,2,1,0:T(8,128)S(1)}, u32[]{:S(2)}, u32[]{:S(2)}) collective-permute-start(f32[4,2,32,128]{3,2,1,0:T(8,128)S(1)} %get-tuple-element.38), channel_id=1, source_target_pairs={{4,0},{8,4},{12,8},{16,12},{20,16},{24,20},{28,24},{0,28},{5,1},{9... | collective-permute-start | bytes 393224 | tf_op jit(solution)/shard_map/ppermute | solution.py:508
  10.2 0.7 %shard_map.106 = (f32[4,8,32,128]{3,2,1,0:T(8,128)S(1)}, f32[8,32,128]{2,1,0:T(8,128)S(1)}, f32[8,32,128]{2,1,0:T(8,128)S(1)}, f32[8,32,128]{2,1,0:T(8,128)S(1)}, f32[2,8,32,128]{3,2,1,0:T(8,128)S(1)}) custom-call(f32[4,8,32,128]{3,2,1,0:T(8,128)S(1)} %get-tuple-element.36.own, bf16[256,256]{1,0:T(8,128)(2,1)S(1)} %copy-done.2, bf16[256,256]{1,0:T(8,128)(2,1)S(1)} %copy-done.3), custom_call_target="tpu_custom_call" | custom-call | bytes 1966080 | tf_op jit(solution)/shard_map/pallas_call | solution.py:465
  10.9 0.1 collective-permute-start.6
  11.0 2.2 %collective-permute-done.1.before = f32[4,2,32,128]{3,2,1,0:T(8,128)S(1)} collective-permute-done((f32[4,2,32,128]{3,2,1,0:T(8,128)S(1)}, f32[4,2,32,128]{3,2,1,0:T(8,128)S(1)}, u32[]{:S(2)}, u32[]{:S(2)}) %collective-permute-start.1) | collective-permute-done | bytes 131104 | tf_op jit(solution)/shard_map/ppermute | solution.py:507
  13.2 1.3 %collective-permute-done.2.after = f32[4,2,32,128]{3,2,1,0:T(8,128)S(1)} collective-permute-done((f32[4,2,32,128]{3,2,1,0:T(8,128)S(1)}, f32[4,2,32,128]{3,2,1,0:T(8,128)S(1)}, u32[]{:S(2)}, u32[]{:S(2)}) %collective-permute-start.2) | collective-permute-done | bytes 131104 | tf_op jit(solution)/shard_map/ppermute | solution.py:508
  14.5 0.3 %shard_map.107 = (f32[4,8,32,128]{3,2,1,0:T(8,128)S(1)}, f32[2,8,32,128]{3,2,1,0:T(8,128)S(1)}, f32[8,32,128]{2,1,0:T(8,128)S(1)}, f32[8,32,128]{2,1,0:T(8,128)S(1)}) custom-call(f32[4,8,32,128]{3,2,1,0:T(8,128)S(1)} %get-tuple-element.36.own, f32[4,2,32,128]{3,2,1,0:T(8,128)S(1)} %collective-permute-done.1.before, ...), custom_call_target="tpu_custom_call" | custom-call | bytes 2228224 | tf_op jit(solution)/shard_map/pallas_call | solution.py:465
  14.9 0.6 %collective-permute-start.8 = (f32[8,32,128]{2,1,0:T(8,128)S(1)}, f32[8,32,128]{2,1,0:T(8,128)S(1)}, u32[]{:S(2)}, u32[]{:S(2)}) collective-permute-start(f32[8,32,128]{2,1,0:T(8,128)S(1)} %get-tuple-element.45), channel_id=1, source_target_pairs={{0,1},{1,0},{2,3},{3,2},{4,5},{5,4},{6,7},{7,6},{8,9},{9,8},{10,11... | collective-permute-start | bytes 393224 | tf_op jit(solution)/shard_map/ppermute | solution.py:522
  15.4 0.1 collective-permute-start.9
  15.5 0.3 %collective-permute-done.7.mate_w = f32[8,32,128]{2,1,0:T(8,128)S(1)} collective-permute-done((f32[8,32,128]{2,1,0:T(8,128)S(1)}, f32[8,32,128]{2,1,0:T(8,128)S(1)}, u32[]{:S(2)}, u32[]{:S(2)}) %collective-permute-start.7) | collective-permute-done | bytes 131104 | tf_op jit(solution)/shard_map/ppermute | solution.py:514
  15.8 1.5 %collective-permute-start.3 = (f32[2,8,32,128]{3,2,1,0:T(8,128)S(1)}, f32[2,8,32,128]{3,2,1,0:T(8,128)S(1)}, u32[]{:S(2)}, u32[]{:S(2)}) collective-permute-start(f32[2,8,32,128]{3,2,1,0:T(8,128)S(1)} %get-tuple-element.40.third), channel_id=1, source_target_pairs={{0,2},{1,3},{2,0},{3,1},{4,6},{5,7},{6,4},{7,5},{8,10},{9,11},{10,... | collective-permute-start | bytes 786440 | tf_op jit(solution)/shard_map/ppermute | solution.py:523
  17.4 0.9 %shard_map.108 = (f32[2,256,256]{2,1,0:T(8,128)S(1)}, f32[5,8,32,128]{3,2,1,0:T(8,128)S(1)}, f32[5,2,32,128]{3,2,1,0:T(8,128)S(1)}, f32[5,2,32,128]{3,2,1,0:T(8,128)S(1)}) custom-call(f32[4,8,32,128]{3,2,1,0:T(8,128)S(1)} %get-tuple-element.36.own, f32[3,8,32,128]{3,2,1,0:T(8,128)S(1)} %get-tuple-element.41.second, ...), custom_call_target="tpu_custom_call" | custom-call | bytes 5439488 | tf_op jit(solution)/shard_map/pallas_call | solution.py:465
  18.3 3.5 %collective-permute-start.12 = (f32[5,2,32,128]{3,2,1,0:T(8,128)S(1)}, f32[5,2,32,128]{3,2,1,0:T(8,128)S(1)}, u32[]{:S(2)}, u32[]{:S(2)}) collective-permute-start(f32[5,2,32,128]{3,2,1,0:T(8,128)S(1)} %get-tuple-element.57), channel_id=1, source_target_pairs={{4,0},{8,4},{12,8},{16,12},{20,16},{24,20},{28,24},{0,28},{5,1},{9... | collective-permute-start | bytes 491528 | tf_op jit(solution)/shard_map/ppermute | solution.py:532
  21.9 0.4 %shard_map.109 = (f32[8,32,128]{2,1,0:T(8,128)S(1)}, f32[8,32,128]{2,1,0:T(8,128)S(1)}, f32[2,256,128]{2,1,0:T(8,128)S(1)}) custom-call(f32[2,8,32,128]{3,2,1,0:T(8,128)S(1)} %collective-permute-done.peer_first, f32[3,8,32,128]{3,2,1,0:T(8,128)S(1)} %collective-permute-done.4.peer_second, f32[5,8,32,128]{3,2,1,0:T(8,128)S(1)} %get-tuple-element.49.flux, ...), custom_call_target="tpu_custom_call" | custom-call | bytes 2097152 | tf_op jit(solution)/shard_map/pallas_call | solution.py:465
  22.2 0.1 collective-permute-start.10
  22.3 0.5 %collective-permute-start.11 = (f32[8,32,128]{2,1,0:T(8,128)S(1)}, f32[8,32,128]{2,1,0:T(8,128)S(1)}, u32[]{:S(2)}, u32[]{:S(2)}) collective-permute-start(f32[8,32,128]{2,1,0:T(8,128)S(1)} %get-tuple-element.51), channel_id=1, source_target_pairs={{0,1},{1,0},{2,3},{3,2},{4,5},{5,4},{6,7},{7,6},{8,9},{9,8},{10,11... | collective-permute-start | bytes 393224 | tf_op jit(solution)/shard_map/ppermute | solution.py:540
  22.8 0.8 %collective-permute-done.10.across_v = f32[8,32,128]{2,1,0:T(8,128)S(1)} collective-permute-done((f32[8,32,128]{2,1,0:T(8,128)S(1)}, f32[8,32,128]{2,1,0:T(8,128)S(1)}, u32[]{:S(2)}, u32[]{:S(2)}) %collective-permute-start.10) | collective-permute-done | bytes 131104 | tf_op jit(solution)/shard_map/ppermute | solution.py:539
  23.6 0.2 collective-permute-done.11.across_t
  23.8 2.3 %shard_map.110 = (f32[5,8,32,128]{3,2,1,0:T(8,128)S(1)}, f32[5,8,32,128]{3,2,1,0:T(8,128)S(1)}) custom-call(f32[4,8,32,128]{3,2,1,0:T(8,128)S(1)} %get-tuple-element.36.own, f32[3,8,32,128]{3,2,1,0:T(8,128)S(1)} %get-tuple-element.41.second, f32[2,8,32,128]{3,2,1,0:T(8,128)S(1)} %collective-permute-done.peer_first, ...), custom_call_target="tpu_custom_call" | custom-call | bytes 7208960 | tf_op jit(solution)/shard_map/pallas_call | solution.py:465
  26.1 0.5 %shard_map.111 = (f32[5,8,32,128]{3,2,1,0:T(8,128)S(1)}, f32[8,32,128]{2,1,0:T(8,128)S(1)}, f32[8,32,128]{2,1,0:T(8,128)S(1)}, f32[8,32,128]{2,1,0:T(8,128)S(1)}...) custom-call(f32[4,8,32,128]{3,2,1,0:T(8,128)S(1)} %get-tuple-element.36.own, ...), custom_call_target="tpu_custom_call" | custom-call | bytes 4456448 | tf_op jit(solution)/shard_map/pallas_call | solution.py:465
  26.7 0.4 %collective-permute-start.14 = (f32[8,32,128]{2,1,0:T(8,128)S(1)}, f32[8,32,128]{2,1,0:T(8,128)S(1)}, u32[]{:S(2)}, u32[]{:S(2)}) collective-permute-start(f32[8,32,128]{2,1,0:T(8,128)S(1)} %get-tuple-element.59), channel_id=1, source_target_pairs={{0,1},{1,0},{2,3},{3,2},{4,5},{5,4},{6,7},{7,6},{8,9},{9,8},{10,11... | collective-permute-start | bytes 393224 | tf_op jit(solution)/shard_map/ppermute | solution.py:559
  27.1 0.2 collective-permute-start.15
  27.2 0.3 %collective-permute-start.16 = (f32[8,32,128]{2,1,0:T(8,128)S(1)}, f32[8,32,128]{2,1,0:T(8,128)S(1)}, u32[]{:S(2)}, u32[]{:S(2)}) collective-permute-start(f32[8,32,128]{2,1,0:T(8,128)S(1)} %get-tuple-element.61), channel_id=1, source_target_pairs={{0,1},{1,0},{2,3},{3,2},{4,5},{5,4},{6,7},{7,6},{8,9},{9,8},{10,11... | collective-permute-start | bytes 393224 | tf_op jit(solution)/shard_map/ppermute | solution.py:559
  27.6 0.2 collective-permute-start.17
  27.8 2.5 %collective-permute-done.13.before = f32[5,2,32,128]{3,2,1,0:T(8,128)S(1)} collective-permute-done((f32[5,2,32,128]{3,2,1,0:T(8,128)S(1)}, f32[5,2,32,128]{3,2,1,0:T(8,128)S(1)}, u32[]{:S(2)}, u32[]{:S(2)}) %collective-permute-start.13) | collective-permute-done | bytes 163872 | tf_op jit(solution)/shard_map/ppermute | solution.py:533
  30.2 0.4 %shard_map.112.total = f32[5,8,32,128]{3,2,1,0:T(8,128)S(1)} custom-call(f32[5,8,32,128]{3,2,1,0:T(8,128)S(1)} %get-tuple-element.56.total, f32[5,8,32,128]{3,2,1,0:T(8,128)S(1)} %get-tuple-element.49.flux, f32[5,2,32,128]{3,2,1,0:T(8,128)S(1)} %collective-permute-done.12.after, f32[5,2,32,128]{3,2,1,0:T(8,128)S(1)} %collective-permute-done.13.before), custom_call_target="tpu_custom_call" | custom-call | bytes 2293760 | tf_op jit(solution)/shard_map/pallas_call | solution.py:465
  30.6 0.9 %collective-permute-done.18.mate_4 = f32[8,32,128]{2,1,0:T(8,128)S(1)} collective-permute-done((f32[8,32,128]{2,1,0:T(8,128)S(1)}, f32[8,32,128]{2,1,0:T(8,128)S(1)}, u32[]{:S(2)}, u32[]{:S(2)}) %collective-permute-start.18) | collective-permute-done | bytes 131104 | tf_op jit(solution)/shard_map/ppermute | solution.py:559
  31.6 1.2 %shard_map.113 = (f32[5,8,32,128]{3,2,1,0:T(8,128)}, f32[5,8,32,128]{3,2,1,0:T(8,128)}) custom-call(f32[5,8,32,128]{3,2,1,0:T(8,128)S(1)} %get-tuple-element.34.conserved, f32[5,8,32,128]{3,2,1,0:T(8,128)S(1)} %shard_map.112.total, f32[8,32,128]{2,1,0:T(8,128)S(1)} %collective-permute-done.14.mate_0, f32[8,32,128]{2,1,0:T(8,128)S(1)} %collective-permute-done.15.mate_1, ...), custom_call_target="tpu_custom_call" | custom-call | bytes 3276800 | tf_op jit(solution)/shard_map/pallas_call | solution.py:465
  (28 shorter events, 0.1 us)
Async XLA Ops:
  1.8 12.7 %collective-permute-start = (f32[2,8,32,128]{3,2,1,0:T(8,128)S(1)}, f32[2,8,32,128]{3,2,1,0:T(8,128)S(1)}, u32[]{:S(2)}, u32[]{:S(2)}) collective-permute-start(f32[2,8,32,128]{3,2,1,0:T(8,128)S(1)} %get-tuple-element.35.first), channel_id=1, source_target_pairs={{0,2},{1,3},{2,0},{3,1},{4,6},{5,7},{6,4},{7,5},{8,10},{9,11},{10,... | collective-permute-start | bytes 786440 | tf_op jit(solution)/shard_map/ppermute | solution.py:506
  4.8 5.4 %copy-start.2 = (bf16[256,256]{1,0:T(8,128)(2,1)S(1)}, bf16[256,256]{1,0:T(8,128)(2,1)}, u32[]{:S(2)}) copy-start(bf16[256,256]{1,0:T(8,128)(2,1)} %constant.16.clone.y_high) | copy-start | bytes 393220
  4.8 5.4 %copy-start.3 = (bf16[256,256]{1,0:T(8,128)(2,1)S(1)}, bf16[256,256]{1,0:T(8,128)(2,1)}, u32[]{:S(2)}) copy-start(bf16[256,256]{1,0:T(8,128)(2,1)} %constant.17.clone.y_low) | copy-start | bytes 393220
  5.0 16.8 %collective-permute-start.4 = (f32[3,8,32,128]{3,2,1,0:T(8,128)S(1)}, f32[3,8,32,128]{3,2,1,0:T(8,128)S(1)}, u32[]{:S(2)}, u32[]{:S(2)}) collective-permute-start(f32[3,8,32,128]{3,2,1,0:T(8,128)S(1)} %get-tuple-element.41.second), channel_id=1, source_target_pairs={{0,2},{1,3},{2,0},{3,1},{4,6},{5,7},{6,4},{7,5},{8,10},{9,11},{10,... | collective-permute-start | bytes 1179656 | tf_op jit(solution)/shard_map/ppermute | solution.py:516
  5.1 8.1 %collective-permute-start.1 = (f32[4,2,32,128]{3,2,1,0:T(8,128)S(1)}, f32[4,2,32,128]{3,2,1,0:T(8,128)S(1)}, u32[]{:S(2)}, u32[]{:S(2)}) collective-permute-start(f32[4,2,32,128]{3,2,1,0:T(8,128)S(1)} %get-tuple-element.37), channel_id=1, source_target_pairs={{0,4},{4,8},{8,12},{12,16},{16,20},{20,24},{24,28},{28,0},{1,5},{5... | collective-permute-start | bytes 393224 | tf_op jit(solution)/shard_map/ppermute | solution.py:507
  7.1 7.4 %collective-permute-start.2 = (f32[4,2,32,128]{3,2,1,0:T(8,128)S(1)}, f32[4,2,32,128]{3,2,1,0:T(8,128)S(1)}, u32[]{:S(2)}, u32[]{:S(2)}) collective-permute-start(f32[4,2,32,128]{3,2,1,0:T(8,128)S(1)} %get-tuple-element.38), channel_id=1, source_target_pairs={{4,0},{8,4},{12,8},{16,12},{20,16},{24,20},{28,24},{0,28},{5,1},{9... | collective-permute-start | bytes 393224 | tf_op jit(solution)/shard_map/ppermute | solution.py:508
  10.9 4.5 %collective-permute-start.6 = (f32[8,32,128]{2,1,0:T(8,128)S(1)}, f32[8,32,128]{2,1,0:T(8,128)S(1)}, u32[]{:S(2)}, u32[]{:S(2)}) collective-permute-start(f32[8,32,128]{2,1,0:T(8,128)S(1)} %get-tuple-element.43), channel_id=1, source_target_pairs={{0,1},{1,0},{2,3},{3,2},{4,5},{5,4},{6,7},{7,6},{8,9},{9,8},{10,11... | collective-permute-start | bytes 393224 | tf_op jit(solution)/shard_map/ppermute | solution.py:514
  13.2 9.1 %collective-permute-start.5 = (f32[2,8,32,128]{3,2,1,0:T(8,128)S(1)}, f32[2,8,32,128]{3,2,1,0:T(8,128)S(1)}, u32[]{:S(2)}, u32[]{:S(2)}) collective-permute-start(f32[2,8,32,128]{3,2,1,0:T(8,128)S(1)} %get-tuple-element.42), channel_id=1, source_target_pairs={{0,1},{1,0},{2,3},{3,2},{4,5},{5,4},{6,7},{7,6},{8,9},{9,8},{10,11... | collective-permute-start | bytes 786440 | tf_op jit(solution)/shard_map/ppermute | solution.py:515
  14.5 1.3 %collective-permute-start.7 = (f32[8,32,128]{2,1,0:T(8,128)S(1)}, f32[8,32,128]{2,1,0:T(8,128)S(1)}, u32[]{:S(2)}, u32[]{:S(2)}) collective-permute-start(f32[8,32,128]{2,1,0:T(8,128)S(1)} %get-tuple-element.44), channel_id=1, source_target_pairs={{0,1},{1,0},{2,3},{3,2},{4,5},{5,4},{6,7},{7,6},{8,9},{9,8},{10,11... | collective-permute-start | bytes 393224 | tf_op jit(solution)/shard_map/ppermute | solution.py:514
  14.5 2.8 %copy-start = (bf16[2,512,256]{2,1,0:T(8,128)(2,1)S(1)}, bf16[2,512,256]{2,1,0:T(8,128)(2,1)}, u32[]{:S(2)}) copy-start(bf16[2,512,256]{2,1,0:T(8,128)(2,1)} %constant.12.clone.z_high) | copy-start | bytes 1572868
  14.5 2.8 %copy-start.1 = (bf16[2,512,256]{2,1,0:T(8,128)(2,1)S(1)}, bf16[2,512,256]{2,1,0:T(8,128)(2,1)}, u32[]{:S(2)}) copy-start(bf16[2,512,256]{2,1,0:T(8,128)(2,1)} %constant.13.clone.z_low) | copy-start | bytes 1572868
  14.9 2.5 %collective-permute-start.8 = (f32[8,32,128]{2,1,0:T(8,128)S(1)}, f32[8,32,128]{2,1,0:T(8,128)S(1)}, u32[]{:S(2)}, u32[]{:S(2)}) collective-permute-start(f32[8,32,128]{2,1,0:T(8,128)S(1)} %get-tuple-element.45), channel_id=1, source_target_pairs={{0,1},{1,0},{2,3},{3,2},{4,5},{5,4},{6,7},{7,6},{8,9},{9,8},{10,11... | collective-permute-start | bytes 393224 | tf_op jit(solution)/shard_map/ppermute | solution.py:522
  15.4 1.9 %collective-permute-start.9 = (f32[8,32,128]{2,1,0:T(8,128)S(1)}, f32[8,32,128]{2,1,0:T(8,128)S(1)}, u32[]{:S(2)}, u32[]{:S(2)}) collective-permute-start(f32[8,32,128]{2,1,0:T(8,128)S(1)} %get-tuple-element.46), channel_id=1, source_target_pairs={{0,1},{1,0},{2,3},{3,2},{4,5},{5,4},{6,7},{7,6},{8,9},{9,8},{10,11... | collective-permute-start | bytes 393224 | tf_op jit(solution)/shard_map/ppermute | solution.py:522
  15.8 10.3 %collective-permute-start.3 = (f32[2,8,32,128]{3,2,1,0:T(8,128)S(1)}, f32[2,8,32,128]{3,2,1,0:T(8,128)S(1)}, u32[]{:S(2)}, u32[]{:S(2)}) collective-permute-start(f32[2,8,32,128]{3,2,1,0:T(8,128)S(1)} %get-tuple-element.40.third), channel_id=1, source_target_pairs={{0,2},{1,3},{2,0},{3,1},{4,6},{5,7},{6,4},{7,5},{8,10},{9,11},{10,... | collective-permute-start | bytes 786440 | tf_op jit(solution)/shard_map/ppermute | solution.py:523
  18.3 9.3 %collective-permute-start.12 = (f32[5,2,32,128]{3,2,1,0:T(8,128)S(1)}, f32[5,2,32,128]{3,2,1,0:T(8,128)S(1)}, u32[]{:S(2)}, u32[]{:S(2)}) collective-permute-start(f32[5,2,32,128]{3,2,1,0:T(8,128)S(1)} %get-tuple-element.57), channel_id=1, source_target_pairs={{4,0},{8,4},{12,8},{16,12},{20,16},{24,20},{28,24},{0,28},{5,1},{9... | collective-permute-start | bytes 491528 | tf_op jit(solution)/shard_map/ppermute | solution.py:532
  21.8 8.4 %collective-permute-start.13 = (f32[5,2,32,128]{3,2,1,0:T(8,128)S(1)}, f32[5,2,32,128]{3,2,1,0:T(8,128)S(1)}, u32[]{:S(2)}, u32[]{:S(2)}) collective-permute-start(f32[5,2,32,128]{3,2,1,0:T(8,128)S(1)} %get-tuple-element.58), channel_id=1, source_target_pairs={{0,4},{4,8},{8,12},{12,16},{16,20},{20,24},{24,28},{28,0},{1,5},{5... | collective-permute-start | bytes 491528 | tf_op jit(solution)/shard_map/ppermute | solution.py:533
  21.8 2.0 %copy-start.4 = (bf16[2,256,256]{2,1,0:T(8,128)(2,1)S(1)}, bf16[2,256,256]{2,1,0:T(8,128)(2,1)}, u32[]{:S(2)}) copy-start(bf16[2,256,256]{2,1,0:T(8,128)(2,1)} %constant.14.clone.f_high) | copy-start | bytes 786436
  21.8 2.0 %copy-start.5 = (bf16[2,256,256]{2,1,0:T(8,128)(2,1)S(1)}, bf16[2,256,256]{2,1,0:T(8,128)(2,1)}, u32[]{:S(2)}) copy-start(bf16[2,256,256]{2,1,0:T(8,128)(2,1)} %constant.15.clone.f_low) | copy-start | bytes 786436
  22.2 1.4 %collective-permute-start.10 = (f32[8,32,128]{2,1,0:T(8,128)S(1)}, f32[8,32,128]{2,1,0:T(8,128)S(1)}, u32[]{:S(2)}, u32[]{:S(2)}) collective-permute-start(f32[8,32,128]{2,1,0:T(8,128)S(1)} %get-tuple-element.50), channel_id=1, source_target_pairs={{0,1},{1,0},{2,3},{3,2},{4,5},{5,4},{6,7},{7,6},{8,9},{9,8},{10,11... | collective-permute-start | bytes 393224 | tf_op jit(solution)/shard_map/ppermute | solution.py:539
  22.3 1.5 %collective-permute-start.11 = (f32[8,32,128]{2,1,0:T(8,128)S(1)}, f32[8,32,128]{2,1,0:T(8,128)S(1)}, u32[]{:S(2)}, u32[]{:S(2)}) collective-permute-start(f32[8,32,128]{2,1,0:T(8,128)S(1)} %get-tuple-element.51), channel_id=1, source_target_pairs={{0,1},{1,0},{2,3},{3,2},{4,5},{5,4},{6,7},{7,6},{8,9},{9,8},{10,11... | collective-permute-start | bytes 393224 | tf_op jit(solution)/shard_map/ppermute | solution.py:540
  26.7 3.9 %collective-permute-start.14 = (f32[8,32,128]{2,1,0:T(8,128)S(1)}, f32[8,32,128]{2,1,0:T(8,128)S(1)}, u32[]{:S(2)}, u32[]{:S(2)}) collective-permute-start(f32[8,32,128]{2,1,0:T(8,128)S(1)} %get-tuple-element.59), channel_id=1, source_target_pairs={{0,1},{1,0},{2,3},{3,2},{4,5},{5,4},{6,7},{7,6},{8,9},{9,8},{10,11... | collective-permute-start | bytes 393224 | tf_op jit(solution)/shard_map/ppermute | solution.py:559
  27.1 3.6 %collective-permute-start.15 = (f32[8,32,128]{2,1,0:T(8,128)S(1)}, f32[8,32,128]{2,1,0:T(8,128)S(1)}, u32[]{:S(2)}, u32[]{:S(2)}) collective-permute-start(f32[8,32,128]{2,1,0:T(8,128)S(1)} %get-tuple-element.60), channel_id=1, source_target_pairs={{0,1},{1,0},{2,3},{3,2},{4,5},{5,4},{6,7},{7,6},{8,9},{9,8},{10,11... | collective-permute-start | bytes 393224 | tf_op jit(solution)/shard_map/ppermute | solution.py:559
  27.2 3.4 %collective-permute-start.16 = (f32[8,32,128]{2,1,0:T(8,128)S(1)}, f32[8,32,128]{2,1,0:T(8,128)S(1)}, u32[]{:S(2)}, u32[]{:S(2)}) collective-permute-start(f32[8,32,128]{2,1,0:T(8,128)S(1)} %get-tuple-element.61), channel_id=1, source_target_pairs={{0,1},{1,0},{2,3},{3,2},{4,5},{5,4},{6,7},{7,6},{8,9},{9,8},{10,11... | collective-permute-start | bytes 393224 | tf_op jit(solution)/shard_map/ppermute | solution.py:559
  27.6 3.1 %collective-permute-start.17 = (f32[8,32,128]{2,1,0:T(8,128)S(1)}, f32[8,32,128]{2,1,0:T(8,128)S(1)}, u32[]{:S(2)}, u32[]{:S(2)}) collective-permute-start(f32[8,32,128]{2,1,0:T(8,128)S(1)} %get-tuple-element.62), channel_id=1, source_target_pairs={{0,1},{1,0},{2,3},{3,2},{4,5},{5,4},{6,7},{7,6},{8,9},{9,8},{10,11... | collective-permute-start | bytes 393224 | tf_op jit(solution)/shard_map/ppermute | solution.py:559
  30.2 1.3 %collective-permute-start.18 = (f32[8,32,128]{2,1,0:T(8,128)S(1)}, f32[8,32,128]{2,1,0:T(8,128)S(1)}, u32[]{:S(2)}, u32[]{:S(2)}) collective-permute-start(f32[8,32,128]{2,1,0:T(8,128)S(1)} %get-tuple-element.63), channel_id=1, source_target_pairs={{0,1},{1,0},{2,3},{3,2},{4,5},{5,4},{6,7},{7,6},{8,9},{9,8},{10,11... | collective-permute-start | bytes 393224 | tf_op jit(solution)/shard_map/ppermute | solution.py:559

commit v4 on v3

--- a/solution.py
+++ b/solution.py
@@ -286,7 +286,7 @@
 
 def kernel_flux_x(
     own, second, peer_first, mate_u, mate_w, across_u, across_w, dx, dy, mu,
-    z_high, z_low, dz, flux, down, up,
+    z_high, z_low, dz, flux, far, near,
 ):
     width = own.shape[-1]
     odd = lax.rem(lax.axis_index("gy"), 2)
@@ -317,10 +317,17 @@
         return carry
 
     lax.fori_loop(0, CX, plane, 0)
+    even = lax.rem(lax.axis_index("gx"), 2) == 0
+    basis = halo_basis()[0]
 
     def sums(f, carry):
         for chunk in row_chunks(rows):
-            halo_sums(flux, f, chunk, up, down)
+            planes = [flux[f, x, chunk, :] for x in range(CX)]
+            for k in range(2):
+                top = sum(float(basis[k, l]) * planes[CX - HALO + l] for l in range(HALO))
+                bottom = sum(float(basis[k, l]) * planes[HALO - 1 - l] for l in range(HALO))
+                far[f, k, chunk, :] = jnp.where(even, bottom, top)
+                near[f, k, chunk, :] = jnp.where(even, top, bottom)
         return carry
 
     lax.fori_loop(0, 5, sums, 0)
@@ -426,10 +433,14 @@
         for_mate[f][...] = part_mate[f] + spread[:, width:].reshape(shape)
 
 
-def kernel_add_stream(total, flux, after, before, result):
+def kernel_add_stream(total, flux, far, near, result):
+    even = lax.rem(lax.axis_index("gx"), 2) == 0
+
     def field(f, carry):
         for rows in row_chunks(flux.shape[2]):
-            derived = compact_x(extended(before, flux, after, f, rows))
+            before = [jnp.where(even, far[f, k, rows, :], near[f, k, rows, :]) for k in (0, 1)]
+            after = [jnp.where(even, near[f, k, rows, :], far[f, k, rows, :]) for k in (1, 0)]
+            derived = compact_x(before + [flux[f, l, rows, :] for l in range(CX)] + after)
             for x in range(CX):
                 result[f, x, rows, :] = total[f, x, rows, :] + derived[x]
         return carry
@@ -488,6 +499,8 @@
     devices = lax.axis_size("gx")
     ring_up = [(i, (i + 1) % devices) for i in range(devices)]
     ring_down = [(j, i) for i, j in ring_up]
+    near_pairs = [(i, i ^ 1) for i in range(devices)]
+    far_pairs = [(i, (i - 1 + 2 * (i % 2)) % devices) for i in range(devices)]
     to_mate = [(i, i ^ 1) for i in range(4)]
     to_peer = [(i, i ^ 2) for i in range(4)]
 
@@ -521,7 +534,7 @@
     )
     across_u, across_w = (lax.ppermute(value, "gy", to_mate) for value in (for_u, for_w))
     peer_third = lax.ppermute(third, "gy", to_peer)
-    dz, flux, flux_down, flux_up = call(
+    dz, flux, far, near = call(
         kernel_flux_x,
         [(2, points, 2 * width), (5,) + block, (5,) + sums, (5,) + sums],
         (
@@ -529,8 +542,8 @@
             z_high, z_low,
         ),
     )
-    flux_after = lax.ppermute(flux_down, "gx", ring_down)
-    flux_before = lax.ppermute(flux_up, "gx", ring_up)
+    from_far = lax.ppermute(far, "gx", far_pairs)
+    from_near = lax.ppermute(near, "gx", near_pairs)
     for_v, for_t, dy_peer = call(
         kernel_peer,
         [block, block, (2, points, width)],
@@ -558,7 +571,7 @@
     )
     from_mate = [lax.ppermute(value, "gy", to_mate) for value in for_mate]
     (total,) = call(
-        kernel_add_stream, [(5,) + block], (total, flux, flux_after, flux_before)
+        kernel_add_stream, [(5,) + block], (total, flux, from_far, from_near)
     )
     tendency, advanced = call(
         kernel_finish,
@@ -673,7 +686,7 @@
 def per_device(mass_per_volume, momentum, energy):
     planes, width, rows = mass_per_volume.shape
     fits = planes == CX and width % 128 == 0 and rows <= 32 and rows % CY == 0
-    if fits and lax.axis_size("gy") == 4:
+    if fits and lax.axis_size("gy") == 4 and lax.axis_size("gx") % 2 == 0:
         return fast_device(mass_per_volume, momentum, energy)
     return plain_device(mass_per_volume, momentum, energy)
 

time: 32.9 us -> 33.2 us (level)
  no operation moved by 1% of the time
where the time goes in v4:
time: 33.2 us; the launch traced here: 33 us
  starting transfers between devices  15.6 us (47%)
  waiting for transfers between devices  8.62 us (26%)
  Pallas kernels  7.98 us (24%)
  between operations  0.81 us (2%)
    pallas_call x10, Pallas kernels, call(): pl.pallas_call(kernel, out_shape=[jax.ShapeDtypeStruct(shape, F32) for sh...  7.98 us
    ppermute x1, starting transfers between devices, fast_device(): from_far = lax.ppermute(far, 'gx', far_pairs)  3.56 us
    ppermute x1, starting transfers between devices, fast_device(): after = lax.ppermute(down, 'gx', ring_down)  3.04 us
    ppermute x1, starting transfers between devices, fast_device(): peer_first = lax.ppermute(first, 'gy', to_peer)  3 us
    ppermute x1, waiting for transfers between devices, fast_device(): from_near = lax.ppermute(near, 'gx', near_pairs)  2.78 us
    ppermute x1, waiting for transfers between devices, fast_device(): before = lax.ppermute(up, 'gx', ring_up)  2.24 us
    ppermute x1, starting transfers between devices, fast_device(): before = lax.ppermute(up, 'gx', ring_up)  2.01 us
    ppermute x1, starting transfers between devices, fast_device(): peer_third = lax.ppermute(third, 'gy', to_peer)  1.49 us
  transfers between devices with their start and end apart: 19, of which 7 were waited for; matrix products, arithmetic and copies ran while one was open for 0% of the time, Pallas kernels for 17%

profile of v4, /device:TPU:0, one launch (start us, length us, event | category | flops | bytes accessed | tf_op | source)
XLA Modules:
  0.0 33.0 jit_solution(3466544789290956232)
XLA Ops:
  0.6 1.2 %shard_map.104 = (f32[5,8,32,128]{3,2,1,0:T(8,128)S(1)}, f32[2,8,32,128]{3,2,1,0:T(8,128)S(1)}) custom-call(f32[8,32,128]{2,1,0:T(8,128)} %bitcast.6, f32[3,8,32,128]{3,2,1,0:T(8,128)} %bitcast.5, f32[8,32,128]{2,1,0:T(8,128)} %bitcast.7), custom_call_target="tpu_custom_call" | custom-call | bytes 1572864 | tf_op jit(solution)/shard_map/pallas_call | solution.py:476
  1.8 3.0 %collective-permute-start = (f32[2,8,32,128]{3,2,1,0:T(8,128)S(1)}, f32[2,8,32,128]{3,2,1,0:T(8,128)S(1)}, u32[]{:S(2)}, u32[]{:S(2)}) collective-permute-start(f32[2,8,32,128]{3,2,1,0:T(8,128)S(1)} %get-tuple-element.35.first), channel_id=1, source_target_pairs={{0,2},{1,3},{2,0},{3,1},{4,6},{5,7},{6,4},{7,5},{8,10},{9,11},{10,... | collective-permute-start | bytes 786440 | tf_op jit(solution)/shard_map/ppermute | solution.py:519
  4.8 0.2 shard_map.105
  5.0 0.1 collective-permute-start.4
  5.1 2.0 %collective-permute-start.1 = (f32[4,2,32,128]{3,2,1,0:T(8,128)S(1)}, f32[4,2,32,128]{3,2,1,0:T(8,128)S(1)}, u32[]{:S(2)}, u32[]{:S(2)}) collective-permute-start(f32[4,2,32,128]{3,2,1,0:T(8,128)S(1)} %get-tuple-element.37), channel_id=1, source_target_pairs={{0,4},{4,8},{8,12},{12,16},{16,20},{20,24},{24,28},{28,0},{1,5},{5... | collective-permute-start | bytes 393224 | tf_op jit(solution)/shard_map/ppermute | solution.py:520
  7.1 3.0 %collective-permute-start.2 = (f32[4,2,32,128]{3,2,1,0:T(8,128)S(1)}, f32[4,2,32,128]{3,2,1,0:T(8,128)S(1)}, u32[]{:S(2)}, u32[]{:S(2)}) collective-permute-start(f32[4,2,32,128]{3,2,1,0:T(8,128)S(1)} %get-tuple-element.38), channel_id=1, source_target_pairs={{4,0},{8,4},{12,8},{16,12},{20,16},{24,20},{28,24},{0,28},{5,1},{9... | collective-permute-start | bytes 393224 | tf_op jit(solution)/shard_map/ppermute | solution.py:521
  10.2 0.7 %shard_map.106 = (f32[4,8,32,128]{3,2,1,0:T(8,128)S(1)}, f32[8,32,128]{2,1,0:T(8,128)S(1)}, f32[8,32,128]{2,1,0:T(8,128)S(1)}, f32[8,32,128]{2,1,0:T(8,128)S(1)}, f32[2,8,32,128]{3,2,1,0:T(8,128)S(1)}) custom-call(f32[4,8,32,128]{3,2,1,0:T(8,128)S(1)} %get-tuple-element.36.own, bf16[256,256]{1,0:T(8,128)(2,1)S(1)} %copy-done.2, bf16[256,256]{1,0:T(8,128)(2,1)S(1)} %copy-done.3), custom_call_target="tpu_custom_call" | custom-call | bytes 1966080 | tf_op jit(solution)/shard_map/pallas_call | solution.py:476
  10.9 0.1 collective-permute-start.6
  11.0 2.2 %collective-permute-done.1.before = f32[4,2,32,128]{3,2,1,0:T(8,128)S(1)} collective-permute-done((f32[4,2,32,128]{3,2,1,0:T(8,128)S(1)}, f32[4,2,32,128]{3,2,1,0:T(8,128)S(1)}, u32[]{:S(2)}, u32[]{:S(2)}) %collective-permute-start.1) | collective-permute-done | bytes 131104 | tf_op jit(solution)/shard_map/ppermute | solution.py:520
  13.2 1.3 %collective-permute-done.2.after = f32[4,2,32,128]{3,2,1,0:T(8,128)S(1)} collective-permute-done((f32[4,2,32,128]{3,2,1,0:T(8,128)S(1)}, f32[4,2,32,128]{3,2,1,0:T(8,128)S(1)}, u32[]{:S(2)}, u32[]{:S(2)}) %collective-permute-start.2) | collective-permute-done | bytes 131104 | tf_op jit(solution)/shard_map/ppermute | solution.py:521
  14.5 0.3 %shard_map.107 = (f32[4,8,32,128]{3,2,1,0:T(8,128)S(1)}, f32[2,8,32,128]{3,2,1,0:T(8,128)S(1)}, f32[8,32,128]{2,1,0:T(8,128)S(1)}, f32[8,32,128]{2,1,0:T(8,128)S(1)}) custom-call(f32[4,8,32,128]{3,2,1,0:T(8,128)S(1)} %get-tuple-element.36.own, f32[4,2,32,128]{3,2,1,0:T(8,128)S(1)} %collective-permute-done.1.before, ...), custom_call_target="tpu_custom_call" | custom-call | bytes 2228224 | tf_op jit(solution)/shard_map/pallas_call | solution.py:476
  14.9 0.6 %collective-permute-start.8 = (f32[8,32,128]{2,1,0:T(8,128)S(1)}, f32[8,32,128]{2,1,0:T(8,128)S(1)}, u32[]{:S(2)}, u32[]{:S(2)}) collective-permute-start(f32[8,32,128]{2,1,0:T(8,128)S(1)} %get-tuple-element.45), channel_id=1, source_target_pairs={{0,1},{1,0},{2,3},{3,2},{4,5},{5,4},{6,7},{7,6},{8,9},{9,8},{10,11... | collective-permute-start | bytes 393224 | tf_op jit(solution)/shard_map/ppermute | solution.py:535
  15.4 0.1 collective-permute-start.9
  15.5 0.3 collective-permute-done.7.mate_w
  15.8 1.5 %collective-permute-start.3 = (f32[2,8,32,128]{3,2,1,0:T(8,128)S(1)}, f32[2,8,32,128]{3,2,1,0:T(8,128)S(1)}, u32[]{:S(2)}, u32[]{:S(2)}) collective-permute-start(f32[2,8,32,128]{3,2,1,0:T(8,128)S(1)} %get-tuple-element.40.third), channel_id=1, source_target_pairs={{0,2},{1,3},{2,0},{3,1},{4,6},{5,7},{6,4},{7,5},{8,10},{9,11},{10,... | collective-permute-start | bytes 786440 | tf_op jit(solution)/shard_map/ppermute | solution.py:536
  17.4 0.9 %shard_map.108 = (f32[2,256,256]{2,1,0:T(8,128)S(1)}, f32[5,8,32,128]{3,2,1,0:T(8,128)S(1)}, f32[5,2,32,128]{3,2,1,0:T(8,128)S(1)}, f32[5,2,32,128]{3,2,1,0:T(8,128)S(1)}) custom-call(f32[4,8,32,128]{3,2,1,0:T(8,128)S(1)} %get-tuple-element.36.own, f32[3,8,32,128]{3,2,1,0:T(8,128)S(1)} %get-tuple-element.41.second, ...), custom_call_target="tpu_custom_call" | custom-call | bytes 5439488 | tf_op jit(solution)/shard_map/pallas_call | solution.py:476
  18.3 3.6 %collective-permute-start.12 = (f32[5,2,32,128]{3,2,1,0:T(8,128)S(1)}, f32[5,2,32,128]{3,2,1,0:T(8,128)S(1)}, u32[]{:S(2)}, u32[]{:S(2)}) collective-permute-start(f32[5,2,32,128]{3,2,1,0:T(8,128)S(1)} %get-tuple-element.57), channel_id=1, source_target_pairs={{0,28},{4,8},{8,4},{12,16},{16,12},{20,24},{24,20},{28,0},{1,29},{... | collective-permute-start | bytes 491528 | tf_op jit(solution)/shard_map/ppermute | solution.py:545
  21.9 0.4 %shard_map.109 = (f32[8,32,128]{2,1,0:T(8,128)S(1)}, f32[8,32,128]{2,1,0:T(8,128)S(1)}, f32[2,256,128]{2,1,0:T(8,128)S(1)}) custom-call(f32[2,8,32,128]{3,2,1,0:T(8,128)S(1)} %collective-permute-done.peer_first, f32[3,8,32,128]{3,2,1,0:T(8,128)S(1)} %collective-permute-done.4.peer_second, f32[5,8,32,128]{3,2,1,0:T(8,128)S(1)} %get-tuple-element.49.flux, ...), custom_call_target="tpu_custom_call" | custom-call | bytes 2097152 | tf_op jit(solution)/shard_map/pallas_call | solution.py:476
  22.2 0.1 collective-permute-start.10
  22.3 0.5 %collective-permute-start.11 = (f32[8,32,128]{2,1,0:T(8,128)S(1)}, f32[8,32,128]{2,1,0:T(8,128)S(1)}, u32[]{:S(2)}, u32[]{:S(2)}) collective-permute-start(f32[8,32,128]{2,1,0:T(8,128)S(1)} %get-tuple-element.51), channel_id=1, source_target_pairs={{0,1},{1,0},{2,3},{3,2},{4,5},{5,4},{6,7},{7,6},{8,9},{9,8},{10,11... | collective-permute-start | bytes 393224 | tf_op jit(solution)/shard_map/ppermute | solution.py:553
  22.8 0.8 %collective-permute-done.10.across_v = f32[8,32,128]{2,1,0:T(8,128)S(1)} collective-permute-done((f32[8,32,128]{2,1,0:T(8,128)S(1)}, f32[8,32,128]{2,1,0:T(8,128)S(1)}, u32[]{:S(2)}, u32[]{:S(2)}) %collective-permute-start.10) | collective-permute-done | bytes 131104 | tf_op jit(solution)/shard_map/ppermute | solution.py:552
  23.7 0.2 collective-permute-done.11.across_t
  23.8 2.3 %shard_map.110 = (f32[5,8,32,128]{3,2,1,0:T(8,128)S(1)}, f32[5,8,32,128]{3,2,1,0:T(8,128)S(1)}) custom-call(f32[4,8,32,128]{3,2,1,0:T(8,128)S(1)} %get-tuple-element.36.own, f32[3,8,32,128]{3,2,1,0:T(8,128)S(1)} %get-tuple-element.41.second, f32[2,8,32,128]{3,2,1,0:T(8,128)S(1)} %collective-permute-done.peer_first, ...), custom_call_target="tpu_custom_call" | custom-call | bytes 7208960 | tf_op jit(solution)/shard_map/pallas_call | solution.py:476
  26.1 0.5 %shard_map.111 = (f32[5,8,32,128]{3,2,1,0:T(8,128)S(1)}, f32[8,32,128]{2,1,0:T(8,128)S(1)}, f32[8,32,128]{2,1,0:T(8,128)S(1)}, f32[8,32,128]{2,1,0:T(8,128)S(1)}...) custom-call(f32[4,8,32,128]{3,2,1,0:T(8,128)S(1)} %get-tuple-element.36.own, ...), custom_call_target="tpu_custom_call" | custom-call | bytes 4456448 | tf_op jit(solution)/shard_map/pallas_call | solution.py:476
  26.7 0.4 %collective-permute-start.14 = (f32[8,32,128]{2,1,0:T(8,128)S(1)}, f32[8,32,128]{2,1,0:T(8,128)S(1)}, u32[]{:S(2)}, u32[]{:S(2)}) collective-permute-start(f32[8,32,128]{2,1,0:T(8,128)S(1)} %get-tuple-element.59), channel_id=1, source_target_pairs={{0,1},{1,0},{2,3},{3,2},{4,5},{5,4},{6,7},{7,6},{8,9},{9,8},{10,11... | collective-permute-start | bytes 393224 | tf_op jit(solution)/shard_map/ppermute | solution.py:572
  27.1 0.2 collective-permute-start.15
  27.2 0.3 %collective-permute-start.16 = (f32[8,32,128]{2,1,0:T(8,128)S(1)}, f32[8,32,128]{2,1,0:T(8,128)S(1)}, u32[]{:S(2)}, u32[]{:S(2)}) collective-permute-start(f32[8,32,128]{2,1,0:T(8,128)S(1)} %get-tuple-element.61), channel_id=1, source_target_pairs={{0,1},{1,0},{2,3},{3,2},{4,5},{5,4},{6,7},{7,6},{8,9},{9,8},{10,11... | collective-permute-start | bytes 393224 | tf_op jit(solution)/shard_map/ppermute | solution.py:572
  27.6 0.2 collective-permute-start.17
  27.8 2.8 %collective-permute-done.13.near = f32[5,2,32,128]{3,2,1,0:T(8,128)S(1)} collective-permute-done((f32[5,2,32,128]{3,2,1,0:T(8,128)S(1)}, f32[5,2,32,128]{3,2,1,0:T(8,128)S(1)}, u32[]{:S(2)}, u32[]{:S(2)}) %collective-permute-start.13) | collective-permute-done | bytes 163872 | tf_op jit(solution)/shard_map/ppermute | solution.py:546
  30.6 0.4 %shard_map.112.total = f32[5,8,32,128]{3,2,1,0:T(8,128)S(1)} custom-call(f32[5,8,32,128]{3,2,1,0:T(8,128)S(1)} %get-tuple-element.56.total, f32[5,8,32,128]{3,2,1,0:T(8,128)S(1)} %get-tuple-element.49.flux, f32[5,2,32,128]{3,2,1,0:T(8,128)S(1)} %collective-permute-done.12.far, f32[5,2,32,128]{3,2,1,0:T(8,128)S(1)} %collective-permute-done.13.near), custom_call_target="tpu_custom_call" | custom-call | bytes 2293760 | tf_op jit(solution)/shard_map/pallas_call | solution.py:476
  31.0 0.9 %collective-permute-done.18.mate_4 = f32[8,32,128]{2,1,0:T(8,128)S(1)} collective-permute-done((f32[8,32,128]{2,1,0:T(8,128)S(1)}, f32[8,32,128]{2,1,0:T(8,128)S(1)}, u32[]{:S(2)}, u32[]{:S(2)}) %collective-permute-start.18) | collective-permute-done | bytes 131104 | tf_op jit(solution)/shard_map/ppermute | solution.py:572
  31.9 1.2 %shard_map.113 = (f32[5,8,32,128]{3,2,1,0:T(8,128)}, f32[5,8,32,128]{3,2,1,0:T(8,128)}) custom-call(f32[5,8,32,128]{3,2,1,0:T(8,128)S(1)} %get-tuple-element.34.conserved, f32[5,8,32,128]{3,2,1,0:T(8,128)S(1)} %shard_map.112.total, f32[8,32,128]{2,1,0:T(8,128)S(1)} %collective-permute-done.14.mate_0, f32[8,32,128]{2,1,0:T(8,128)S(1)} %collective-permute-done.15.mate_1, ...), custom_call_target="tpu_custom_call" | custom-call | bytes 3276800 | tf_op jit(solution)/shard_map/pallas_call | solution.py:476
  (28 shorter events, 0.1 us)
Async XLA Ops:
  1.8 12.7 %collective-permute-start = (f32[2,8,32,128]{3,2,1,0:T(8,128)S(1)}, f32[2,8,32,128]{3,2,1,0:T(8,128)S(1)}, u32[]{:S(2)}, u32[]{:S(2)}) collective-permute-start(f32[2,8,32,128]{3,2,1,0:T(8,128)S(1)} %get-tuple-element.35.first), channel_id=1, source_target_pairs={{0,2},{1,3},{2,0},{3,1},{4,6},{5,7},{6,4},{7,5},{8,10},{9,11},{10,... | collective-permute-start | bytes 786440 | tf_op jit(solution)/shard_map/ppermute | solution.py:519
  4.8 5.4 %copy-start.2 = (bf16[256,256]{1,0:T(8,128)(2,1)S(1)}, bf16[256,256]{1,0:T(8,128)(2,1)}, u32[]{:S(2)}) copy-start(bf16[256,256]{1,0:T(8,128)(2,1)} %constant.16.clone.y_high) | copy-start | bytes 393220
  4.8 5.4 %copy-start.3 = (bf16[256,256]{1,0:T(8,128)(2,1)S(1)}, bf16[256,256]{1,0:T(8,128)(2,1)}, u32[]{:S(2)}) copy-start(bf16[256,256]{1,0:T(8,128)(2,1)} %constant.17.clone.y_low) | copy-start | bytes 393220
  5.0 16.9 %collective-permute-start.4 = (f32[3,8,32,128]{3,2,1,0:T(8,128)S(1)}, f32[3,8,32,128]{3,2,1,0:T(8,128)S(1)}, u32[]{:S(2)}, u32[]{:S(2)}) collective-permute-start(f32[3,8,32,128]{3,2,1,0:T(8,128)S(1)} %get-tuple-element.41.second), channel_id=1, source_target_pairs={{0,2},{1,3},{2,0},{3,1},{4,6},{5,7},{6,4},{7,5},{8,10},{9,11},{10,... | collective-permute-start | bytes 1179656 | tf_op jit(solution)/shard_map/ppermute | solution.py:529
  5.1 8.1 %collective-permute-start.1 = (f32[4,2,32,128]{3,2,1,0:T(8,128)S(1)}, f32[4,2,32,128]{3,2,1,0:T(8,128)S(1)}, u32[]{:S(2)}, u32[]{:S(2)}) collective-permute-start(f32[4,2,32,128]{3,2,1,0:T(8,128)S(1)} %get-tuple-element.37), channel_id=1, source_target_pairs={{0,4},{4,8},{8,12},{12,16},{16,20},{20,24},{24,28},{28,0},{1,5},{5... | collective-permute-start | bytes 393224 | tf_op jit(solution)/shard_map/ppermute | solution.py:520
  7.1 7.4 %collective-permute-start.2 = (f32[4,2,32,128]{3,2,1,0:T(8,128)S(1)}, f32[4,2,32,128]{3,2,1,0:T(8,128)S(1)}, u32[]{:S(2)}, u32[]{:S(2)}) collective-permute-start(f32[4,2,32,128]{3,2,1,0:T(8,128)S(1)} %get-tuple-element.38), channel_id=1, source_target_pairs={{4,0},{8,4},{12,8},{16,12},{20,16},{24,20},{28,24},{0,28},{5,1},{9... | collective-permute-start | bytes 393224 | tf_op jit(solution)/shard_map/ppermute | solution.py:521
  10.9 4.5 %collective-permute-start.6 = (f32[8,32,128]{2,1,0:T(8,128)S(1)}, f32[8,32,128]{2,1,0:T(8,128)S(1)}, u32[]{:S(2)}, u32[]{:S(2)}) collective-permute-start(f32[8,32,128]{2,1,0:T(8,128)S(1)} %get-tuple-element.43), channel_id=1, source_target_pairs={{0,1},{1,0},{2,3},{3,2},{4,5},{5,4},{6,7},{7,6},{8,9},{9,8},{10,11... | collective-permute-start | bytes 393224 | tf_op jit(solution)/shard_map/ppermute | solution.py:527
  13.2 9.1 %collective-permute-start.5 = (f32[2,8,32,128]{3,2,1,0:T(8,128)S(1)}, f32[2,8,32,128]{3,2,1,0:T(8,128)S(1)}, u32[]{:S(2)}, u32[]{:S(2)}) collective-permute-start(f32[2,8,32,128]{3,2,1,0:T(8,128)S(1)} %get-tuple-element.42), channel_id=1, source_target_pairs={{0,1},{1,0},{2,3},{3,2},{4,5},{5,4},{6,7},{7,6},{8,9},{9,8},{10,11... | collective-permute-start | bytes 786440 | tf_op jit(solution)/shard_map/ppermute | solution.py:528
  14.5 1.3 %collective-permute-start.7 = (f32[8,32,128]{2,1,0:T(8,128)S(1)}, f32[8,32,128]{2,1,0:T(8,128)S(1)}, u32[]{:S(2)}, u32[]{:S(2)}) collective-permute-start(f32[8,32,128]{2,1,0:T(8,128)S(1)} %get-tuple-element.44), channel_id=1, source_target_pairs={{0,1},{1,0},{2,3},{3,2},{4,5},{5,4},{6,7},{7,6},{8,9},{9,8},{10,11... | collective-permute-start | bytes 393224 | tf_op jit(solution)/shard_map/ppermute | solution.py:527
  14.5 2.8 %copy-start = (bf16[2,512,256]{2,1,0:T(8,128)(2,1)S(1)}, bf16[2,512,256]{2,1,0:T(8,128)(2,1)}, u32[]{:S(2)}) copy-start(bf16[2,512,256]{2,1,0:T(8,128)(2,1)} %constant.12.clone.z_high) | copy-start | bytes 1572868
  14.5 2.8 %copy-start.1 = (bf16[2,512,256]{2,1,0:T(8,128)(2,1)S(1)}, bf16[2,512,256]{2,1,0:T(8,128)(2,1)}, u32[]{:S(2)}) copy-start(bf16[2,512,256]{2,1,0:T(8,128)(2,1)} %constant.13.clone.z_low) | copy-start | bytes 1572868
  14.9 2.5 %collective-permute-start.8 = (f32[8,32,128]{2,1,0:T(8,128)S(1)}, f32[8,32,128]{2,1,0:T(8,128)S(1)}, u32[]{:S(2)}, u32[]{:S(2)}) collective-permute-start(f32[8,32,128]{2,1,0:T(8,128)S(1)} %get-tuple-element.45), channel_id=1, source_target_pairs={{0,1},{1,0},{2,3},{3,2},{4,5},{5,4},{6,7},{7,6},{8,9},{9,8},{10,11... | collective-permute-start | bytes 393224 | tf_op jit(solution)/shard_map/ppermute | solution.py:535
  15.4 1.9 %collective-permute-start.9 = (f32[8,32,128]{2,1,0:T(8,128)S(1)}, f32[8,32,128]{2,1,0:T(8,128)S(1)}, u32[]{:S(2)}, u32[]{:S(2)}) collective-permute-start(f32[8,32,128]{2,1,0:T(8,128)S(1)} %get-tuple-element.46), channel_id=1, source_target_pairs={{0,1},{1,0},{2,3},{3,2},{4,5},{5,4},{6,7},{7,6},{8,9},{9,8},{10,11... | collective-permute-start | bytes 393224 | tf_op jit(solution)/shard_map/ppermute | solution.py:535
  15.8 10.3 %collective-permute-start.3 = (f32[2,8,32,128]{3,2,1,0:T(8,128)S(1)}, f32[2,8,32,128]{3,2,1,0:T(8,128)S(1)}, u32[]{:S(2)}, u32[]{:S(2)}) collective-permute-start(f32[2,8,32,128]{3,2,1,0:T(8,128)S(1)} %get-tuple-element.40.third), channel_id=1, source_target_pairs={{0,2},{1,3},{2,0},{3,1},{4,6},{5,7},{6,4},{7,5},{8,10},{9,11},{10,... | collective-permute-start | bytes 786440 | tf_op jit(solution)/shard_map/ppermute | solution.py:536
  18.3 9.3 %collective-permute-start.12 = (f32[5,2,32,128]{3,2,1,0:T(8,128)S(1)}, f32[5,2,32,128]{3,2,1,0:T(8,128)S(1)}, u32[]{:S(2)}, u32[]{:S(2)}) collective-permute-start(f32[5,2,32,128]{3,2,1,0:T(8,128)S(1)} %get-tuple-element.57), channel_id=1, source_target_pairs={{0,28},{4,8},{8,4},{12,16},{16,12},{20,24},{24,20},{28,0},{1,29},{... | collective-permute-start | bytes 491528 | tf_op jit(solution)/shard_map/ppermute | solution.py:545
  21.8 8.7 %collective-permute-start.13 = (f32[5,2,32,128]{3,2,1,0:T(8,128)S(1)}, f32[5,2,32,128]{3,2,1,0:T(8,128)S(1)}, u32[]{:S(2)}, u32[]{:S(2)}) collective-permute-start(f32[5,2,32,128]{3,2,1,0:T(8,128)S(1)} %get-tuple-element.58), channel_id=1, source_target_pairs={{0,4},{4,0},{8,12},{12,8},{16,20},{20,16},{24,28},{28,24},{1,5},{5... | collective-permute-start | bytes 491528 | tf_op jit(solution)/shard_map/ppermute | solution.py:546
  21.9 2.0 %copy-start.4 = (bf16[2,256,256]{2,1,0:T(8,128)(2,1)S(1)}, bf16[2,256,256]{2,1,0:T(8,128)(2,1)}, u32[]{:S(2)}) copy-start(bf16[2,256,256]{2,1,0:T(8,128)(2,1)} %constant.14.clone.f_high) | copy-start | bytes 786436
  21.9 2.0 %copy-start.5 = (bf16[2,256,256]{2,1,0:T(8,128)(2,1)S(1)}, bf16[2,256,256]{2,1,0:T(8,128)(2,1)}, u32[]{:S(2)}) copy-start(bf16[2,256,256]{2,1,0:T(8,128)(2,1)} %constant.15.clone.f_low) | copy-start | bytes 786436
  22.2 1.4 %collective-permute-start.10 = (f32[8,32,128]{2,1,0:T(8,128)S(1)}, f32[8,32,128]{2,1,0:T(8,128)S(1)}, u32[]{:S(2)}, u32[]{:S(2)}) collective-permute-start(f32[8,32,128]{2,1,0:T(8,128)S(1)} %get-tuple-element.50), channel_id=1, source_target_pairs={{0,1},{1,0},{2,3},{3,2},{4,5},{5,4},{6,7},{7,6},{8,9},{9,8},{10,11... | collective-permute-start | bytes 393224 | tf_op jit(solution)/shard_map/ppermute | solution.py:552
  22.3 1.5 %collective-permute-start.11 = (f32[8,32,128]{2,1,0:T(8,128)S(1)}, f32[8,32,128]{2,1,0:T(8,128)S(1)}, u32[]{:S(2)}, u32[]{:S(2)}) collective-permute-start(f32[8,32,128]{2,1,0:T(8,128)S(1)} %get-tuple-element.51), channel_id=1, source_target_pairs={{0,1},{1,0},{2,3},{3,2},{4,5},{5,4},{6,7},{7,6},{8,9},{9,8},{10,11... | collective-permute-start | bytes 393224 | tf_op jit(solution)/shard_map/ppermute | solution.py:553
  26.7 4.3 %collective-permute-start.14 = (f32[8,32,128]{2,1,0:T(8,128)S(1)}, f32[8,32,128]{2,1,0:T(8,128)S(1)}, u32[]{:S(2)}, u32[]{:S(2)}) collective-permute-start(f32[8,32,128]{2,1,0:T(8,128)S(1)} %get-tuple-element.59), channel_id=1, source_target_pairs={{0,1},{1,0},{2,3},{3,2},{4,5},{5,4},{6,7},{7,6},{8,9},{9,8},{10,11... | collective-permute-start | bytes 393224 | tf_op jit(solution)/shard_map/ppermute | solution.py:572
  27.1 3.9 %collective-permute-start.15 = (f32[8,32,128]{2,1,0:T(8,128)S(1)}, f32[8,32,128]{2,1,0:T(8,128)S(1)}, u32[]{:S(2)}, u32[]{:S(2)}) collective-permute-start(f32[8,32,128]{2,1,0:T(8,128)S(1)} %get-tuple-element.60), channel_id=1, source_target_pairs={{0,1},{1,0},{2,3},{3,2},{4,5},{5,4},{6,7},{7,6},{8,9},{9,8},{10,11... | collective-permute-start | bytes 393224 | tf_op jit(solution)/shard_map/ppermute | solution.py:572
  27.2 3.7 %collective-permute-start.16 = (f32[8,32,128]{2,1,0:T(8,128)S(1)}, f32[8,32,128]{2,1,0:T(8,128)S(1)}, u32[]{:S(2)}, u32[]{:S(2)}) collective-permute-start(f32[8,32,128]{2,1,0:T(8,128)S(1)} %get-tuple-element.61), channel_id=1, source_target_pairs={{0,1},{1,0},{2,3},{3,2},{4,5},{5,4},{6,7},{7,6},{8,9},{9,8},{10,11... | collective-permute-start | bytes 393224 | tf_op jit(solution)/shard_map/ppermute | solution.py:572
  27.6 3.4 %collective-permute-start.17 = (f32[8,32,128]{2,1,0:T(8,128)S(1)}, f32[8,32,128]{2,1,0:T(8,128)S(1)}, u32[]{:S(2)}, u32[]{:S(2)}) collective-permute-start(f32[8,32,128]{2,1,0:T(8,128)S(1)} %get-tuple-element.62), channel_id=1, source_target_pairs={{0,1},{1,0},{2,3},{3,2},{4,5},{5,4},{6,7},{7,6},{8,9},{9,8},{10,11... | collective-permute-start | bytes 393224 | tf_op jit(solution)/shard_map/ppermute | solution.py:572
  30.5 1.3 %collective-permute-start.18 = (f32[8,32,128]{2,1,0:T(8,128)S(1)}, f32[8,32,128]{2,1,0:T(8,128)S(1)}, u32[]{:S(2)}, u32[]{:S(2)}) collective-permute-start(f32[8,32,128]{2,1,0:T(8,128)S(1)} %get-tuple-element.63), channel_id=1, source_target_pairs={{0,1},{1,0},{2,3},{3,2},{4,5},{5,4},{6,7},{7,6},{8,9},{9,8},{10,11... | collective-permute-start | bytes 393224 | tf_op jit(solution)/shard_map/ppermute | solution.py:572

commit v5 on v2

--- a/solution.py
+++ b/solution.py
@@ -326,17 +326,65 @@
     lax.fori_loop(0, 5, sums, 0)
 
 
-def kernel_peer(peer_first, peer_second, flux, y_high, y_low, for_v, for_t, dy_peer):
+def kernel_peer(peer_second, flux, for_v, for_t):
     for_v[...] = peer_second[0]
     for_t[...] = peer_second[1]
+
+
+def kernel_flux_yz_early(
+    own, second, peer_first, peer_second, for_v, dz, dx, dy, mu, y_high, y_low, f_high, f_low,
+    spread, local, dy_peer, mu_peer, flux, flux_y,
+):
+    rows, width = own.shape[2:]
+    odd = lax.rem(lax.axis_index("gy"), 2)
     dy_peer[0] = left_product(y_high[...], y_low[...], flat(peer_second[0]))
     dy_peer[1] = left_product(y_high[...], y_low[...], flat(peer_first[1]))
 
+    def plane(x, carry):
+        at = pl.ds(pl.multiple_of(x * rows, rows), rows)
+        here = slice(0, width)
+        there = slice(width, 2 * width)
+
+        def span(lanes, u, w, t, density, viscosity, yv):
+            m = density * w
+            flux[0, at, lanes] = m
+            flux[1, at, lanes] = m * u - viscosity * dz[0, at, lanes]
+            flux[2, at, lanes] = (
+                m * w
+                + density * t
+                - viscosity * ((4.0 / 3.0) * dz[1, at, lanes] - (2.0 / 3.0) * yv)
+            )
+
+        u, w, v, t = (own[f, x] for f in range(4))
+        density = second[2, x]
+        viscosity = mu[x]
+        span(here, u, w, t, density, viscosity, dy[V, x])
+        dil = dx[U, x] + dy[V, x] + dz[1, at, here]
+        m = density * v
+        flux_y[0, at, :] = m
+        flux_y[1, at, :] = m * u - viscosity * (dy[U, x] + dx[V, x])
+        flux_y[2, at, :] = (
+            m * v + density * t - viscosity * (2.0 * dy[V, x] - (2.0 / 3.0) * dil)
+        )
+        t = peer_second[1, x]
+        viscosity = shear_resistance_reference * jnp.exp(sutherland_power_law * jnp.log(t))
+        mu_peer[at, :] = viscosity
+        span(
+            there, peer_first[0, x], peer_first[1, x], t, peer_second[2, x], viscosity,
+            dy_peer[0, at, :],
+        )
+        return carry
+
+    lax.fori_loop(0, CX, plane, 0)
+    for k in range(3):
+        spread[k] = right_product(flux[k], f_high[odd], f_low[odd])
+        local[k] = left_product(y_high[...], y_low[...], flux_y[k])
+
 
 def kernel_flux_yz(
-    own, second, peer_first, peer_second, second_mate, across_v, across_t, dy_peer,
-    dz, dx, dy, mu, y_high, y_low, z_high, z_low, f_high, f_low, part, part_mate,
-    dz_more, flux, flux_y,
+    own, second, peer_first, peer_second, second_mate, across_v, across_t, dy_peer, mu_peer,
+    spread_early, local_early, dz, dx, dy, mu, y_high, y_low, z_high, z_low, f_high, f_low,
+    part, part_mate, dz_more, flux, flux_y,
 ):
     rows, width = own.shape[2:]
     odd = lax.rem(lax.axis_index("gy"), 2)
@@ -347,58 +395,52 @@
         )
         dz_more[f] = right_product(values, z_high[odd], z_low[odd])
 
-    def span_flux(at, lanes, u, w, v, t, density, viscosity, yv, yw):
-        s1 = viscosity * dz[0, at, lanes]
-        s2 = viscosity * (dz_more[0, at, lanes] + yw)
-        s3 = viscosity * ((4.0 / 3.0) * dz[1, at, lanes] - (2.0 / 3.0) * yv)
-        m = density * w
-        total = m * (enthalpy * t + 0.5 * (u * u + v * v + w * w))
-        flux[0, at, lanes] = m
-        flux[1, at, lanes] = m * u - s1
-        flux[2, at, lanes] = m * v - s2
-        flux[3, at, lanes] = m * w + density * t - s3
-        flux[4, at, lanes] = (
-            total
-            - (s1 * u + s2 * v + s3 * w)
-            - conduction * viscosity * dz_more[1, at, lanes]
-        )
-
     def plane(x, carry):
         at = pl.ds(pl.multiple_of(x * rows, rows), rows)
         here = slice(0, width)
+        there = slice(width, 2 * width)
+
+        def span(lanes, u, w, v, t, density, viscosity, yv, yw):
+            s1 = viscosity * dz[0, at, lanes]
+            s2 = viscosity * (dz_more[0, at, lanes] + yw)
+            s3 = viscosity * ((4.0 / 3.0) * dz[1, at, lanes] - (2.0 / 3.0) * yv)
+            energy = density * (enthalpy * t + 0.5 * (u * u + v * v + w * w))
+            flux[0, at, lanes] = density * w * v - s2
+            flux[1, at, lanes] = (
+                energy * w
+                - (s1 * u + s2 * v + s3 * w)
+                - conduction * viscosity * dz_more[1, at, lanes]
+            )
+            return energy
+
         u, w, v, t = (own[f, x] for f in range(4))
         density = second[2, x]
         viscosity = mu[x]
-        span_flux(at, here, u, w, v, t, density, viscosity, dy[V, x], dy[W, x])
+        energy = span(here, u, w, v, t, density, viscosity, dy[V, x], dy[W, x])
         dil = dx[U, x] + dy[V, x] + dz[1, at, here]
         s1 = viscosity * (dy[U, x] + dx[V, x])
         s2 = viscosity * (2.0 * dy[V, x] - (2.0 / 3.0) * dil)
         s3 = viscosity * (dy[W, x] + dz_more[0, at, here])
-        m = density * v
-        total = m * (enthalpy * t + 0.5 * (u * u + v * v + w * w))
-        flux_y[0, at, :] = m
-        flux_y[1, at, :] = m * u - s1
-        flux_y[2, at, :] = m * v + density * t - s2
-        flux_y[3, at, :] = m * w - s3
-        flux_y[4, at, :] = (
-            total - (s1 * u + s2 * v + s3 * w) - conduction * viscosity * dy[T, x]
-        )
-        t = peer_second[1, x]
-        viscosity = shear_resistance_reference * jnp.exp(sutherland_power_law * jnp.log(t))
-        span_flux(
-            at, slice(width, 2 * width), peer_first[0, x], peer_first[1, x],
-            peer_second[0, x], t, peer_second[2, x], viscosity,
-            dy_peer[0, at, :], dy_peer[1, at, :],
+        flux_y[0, at, :] = density * v * w - s3
+        flux_y[1, at, :] = (
+            energy * v - (s1 * u + s2 * v + s3 * w) - conduction * viscosity * dy[T, x]
+        )
+        span(
+            there, peer_first[0, x], peer_first[1, x], peer_second[0, x], peer_second[1, x],
+            peer_second[2, x], mu_peer[at, :], dy_peer[0, at, :], dy_peer[1, at, :],
         )
         return carry
 
     lax.fori_loop(0, CX, plane, 0)
     shape = own.shape[1:]
+    spreads = {0: spread_early[0], 1: spread_early[1], 3: spread_early[2]}
+    locals_y = {0: local_early[0], 1: local_early[1], 2: local_early[2]}
+    for k in range(2):
+        spreads[2 + 2 * k] = right_product(flux[k], f_high[odd], f_low[odd])
+        locals_y[3 + k] = left_product(y_high[...], y_low[...], flux_y[k])
     for f in range(5):
-        spread = right_product(flux[f], f_high[odd], f_low[odd])
-        local = left_product(y_high[...], y_low[...], flux_y[f])
-        part[f] = (spread[:, :width] + local).reshape(shape)
-        part_mate[f] = spread[:, width:].reshape(shape)
+        part[f] = (spreads[f][:, :width] + locals_y[f]).reshape(shape)
+        part_mate[f] = spreads[f][:, width:].reshape(shape)
 
 
 def kernel_corrections(
@@ -531,24 +573,33 @@
     )
     flux_before = lax.ppermute(flux_up, "gx", ring_up)
     flux_after = lax.ppermute(flux_down, "gx", ring_down)
-    for_v, for_t, dy_peer = call(
-        kernel_peer,
-        [block, block, (2, points, width)],
-        (peer_first, peer_second, flux, y_high, y_low),
-    )
+    for_v, for_t = call(kernel_peer, [block, block], (peer_second, flux))
     across_v = lax.ppermute(for_v, "gy", to_mate)
     across_t = lax.ppermute(for_t, "gy", to_mate)
+    spread, local, dy_peer, mu_peer = call(
+        kernel_flux_yz_early,
+        [(3, points, 2 * width), (3, points, width), (2, points, width), (points, width)],
+        (
+            own, second, peer_first, peer_second, for_v, dz, dx, dy, mu,
+            y_high, y_low, f_high, f_low,
+        ),
+        scratch=(
+            pltpu.VMEM((3, points, 2 * width), F32),
+            pltpu.VMEM((3, points, width), F32),
+        ),
+    )
     part, part_mate = call(
         kernel_flux_yz,
         [(5,) + block, (5,) + block],
         (
-            own, second, peer_first, peer_second, second_mate, across_v, across_t, dy_peer,
-            dz, dx, dy, mu, y_high, y_low, z_high, z_low, f_high, f_low,
+            own, second, peer_first, peer_second, second_mate, across_v, across_t,
+            dy_peer, mu_peer, spread, local, dz, dx, dy, mu,
+            y_high, y_low, z_high, z_low, f_high, f_low,
         ),
         scratch=(
             pltpu.VMEM((2, points, 2 * width), F32),
-            pltpu.VMEM((5, points, 2 * width), F32),
-            pltpu.VMEM((5, points, width), F32),
+            pltpu.VMEM((2, points, 2 * width), F32),
+            pltpu.VMEM((2, points, width), F32),
         ),
     )
     total, *for_mate = call(
@@ -673,7 +724,7 @@
 def per_device(mass_per_volume, momentum, energy):
     planes, width, rows = mass_per_volume.shape
     fits = planes == CX and width % 128 == 0 and rows <= 32 and rows % CY == 0
-    if fits and lax.axis_size("gy") == 4:
+    if fits and lax.axis_size("gy") == 4 and lax.axis_size("gx") % 2 == 0:
         return fast_device(mass_per_volume, momentum, energy)
     return plain_device(mass_per_volume, momentum, energy)
 

time: 31.6 us -> 31.4 us (level)
  waiting for transfers between devices: 5.56 us -> 4.79 us
  local copies, waits for them, and re-layouts: 0.03 us -> 0.44 us
  Pallas kernels: 7.99 us -> 8.36 us
    ppermute x1, waiting for transfers between devices: 0.83 us -> 0.01 us  [fast_device(): across_v = lax.ppermute(for_v, 'gy', to_mate)]
    unnamed x12, local copies, waits for them, and re-layouts: 0.03 us -> 0.44 us
    pallas_call x10 -> x11, Pallas kernels: 7.99 us -> 8.36 us  [call(): pl.pallas_call(kernel, out_shape=[jax.ShapeDtypeStruct(shape, F32) for sh...]
  transfers between devices with their start and end apart: 19 -> 19, of which waited for: 8 -> 7; matrix products, arithmetic and copies ran while one was open for 0% -> 0% of each run, Pallas kernels for 18% -> 19%
where the time goes in v5:
time: 31.4 us; the launch traced here: 31.3 us
  starting transfers between devices  16.9 us (54%)
  Pallas kernels  8.36 us (27%)
  waiting for transfers between devices  4.79 us (15%)
  between operations  0.8 us (3%)
  local copies, waits for them, and re-layouts  0.44 us (1%)
    pallas_call x11, Pallas kernels, call(): pl.pallas_call(kernel, out_shape=[jax.ShapeDtypeStruct(shape, F32) for sh...  8.36 us
    ppermute x1, starting transfers between devices, fast_device(): flux_after = lax.ppermute(flux_down, 'gx', ring_down)  3.94 us
    ppermute x1, starting transfers between devices, fast_device(): after = lax.ppermute(down, 'gx', ring_down)  3.04 us
    ppermute x1, starting transfers between devices, fast_device(): peer_first = lax.ppermute(first, 'gy', to_peer)  3 us
    ppermute x1, waiting for transfers between devices, fast_device(): before = lax.ppermute(up, 'gx', ring_up)  2.24 us
    ppermute x1, starting transfers between devices, fast_device(): before = lax.ppermute(up, 'gx', ring_up)  2.01 us
    ppermute x1, starting transfers between devices, fast_device(): peer_third = lax.ppermute(third, 'gy', to_peer)  1.49 us
    ppermute x1, waiting for transfers between devices, fast_device(): after = lax.ppermute(down, 'gx', ring_down)  1.3 us
  transfers between devices with their start and end apart: 19, of which 7 were waited for; matrix products, arithmetic and copies ran while one was open for 0% of the time, Pallas kernels for 19%

profile of v5, /device:TPU:0, one launch (start us, length us, event | category | flops | bytes accessed | tf_op | source)
XLA Modules:
  0.0 31.3 jit_solution(9108580153365141835)
XLA Ops:
  0.6 1.2 %shard_map.104 = (f32[5,8,32,128]{3,2,1,0:T(8,128)S(1)}, f32[2,8,32,128]{3,2,1,0:T(8,128)S(1)}) custom-call(f32[8,32,128]{2,1,0:T(8,128)} %bitcast.6, f32[3,8,32,128]{3,2,1,0:T(8,128)} %bitcast.5, f32[8,32,128]{2,1,0:T(8,128)} %bitcast.7), custom_call_target="tpu_custom_call" | custom-call | bytes 1572864 | tf_op jit(solution)/shard_map/pallas_call | solution.py:507
  1.8 3.0 %collective-permute-start = (f32[2,8,32,128]{3,2,1,0:T(8,128)S(1)}, f32[2,8,32,128]{3,2,1,0:T(8,128)S(1)}, u32[]{:S(2)}, u32[]{:S(2)}) collective-permute-start(f32[2,8,32,128]{3,2,1,0:T(8,128)S(1)} %get-tuple-element.38.first), channel_id=1, source_target_pairs={{0,2},{1,3},{2,0},{3,1},{4,6},{5,7},{6,4},{7,5},{8,10},{9,11},{10,... | collective-permute-start | bytes 786440 | tf_op jit(solution)/shard_map/ppermute | solution.py:548
  4.8 0.2 shard_map.105
  5.0 0.1 collective-permute-start.4
  5.1 2.0 %collective-permute-start.1 = (f32[4,2,32,128]{3,2,1,0:T(8,128)S(1)}, f32[4,2,32,128]{3,2,1,0:T(8,128)S(1)}, u32[]{:S(2)}, u32[]{:S(2)}) collective-permute-start(f32[4,2,32,128]{3,2,1,0:T(8,128)S(1)} %get-tuple-element.40), channel_id=1, source_target_pairs={{0,4},{4,8},{8,12},{12,16},{16,20},{20,24},{24,28},{28,0},{1,5},{5... | collective-permute-start | bytes 393224 | tf_op jit(solution)/shard_map/ppermute | solution.py:549
  7.1 3.0 %collective-permute-start.2 = (f32[4,2,32,128]{3,2,1,0:T(8,128)S(1)}, f32[4,2,32,128]{3,2,1,0:T(8,128)S(1)}, u32[]{:S(2)}, u32[]{:S(2)}) collective-permute-start(f32[4,2,32,128]{3,2,1,0:T(8,128)S(1)} %get-tuple-element.41), channel_id=1, source_target_pairs={{4,0},{8,4},{12,8},{16,12},{20,16},{24,20},{28,24},{0,28},{5,1},{9... | collective-permute-start | bytes 393224 | tf_op jit(solution)/shard_map/ppermute | solution.py:550
  10.2 0.7 %shard_map.106 = (f32[4,8,32,128]{3,2,1,0:T(8,128)S(1)}, f32[8,32,128]{2,1,0:T(8,128)S(1)}, f32[8,32,128]{2,1,0:T(8,128)S(1)}, f32[8,32,128]{2,1,0:T(8,128)S(1)}, f32[2,8,32,128]{3,2,1,0:T(8,128)S(1)}) custom-call(f32[4,8,32,128]{3,2,1,0:T(8,128)S(1)} %get-tuple-element.39.own, bf16[256,256]{1,0:T(8,128)(2,1)S(1)} %copy-done.4, bf16[256,256]{1,0:T(8,128)(2,1)S(1)} %copy-done.5), custom_call_target="tpu_custom_call" | custom-call | bytes 1966080 | tf_op jit(solution)/shard_map/pallas_call | solution.py:507
  11.0 2.2 %collective-permute-done.1.before = f32[4,2,32,128]{3,2,1,0:T(8,128)S(1)} collective-permute-done((f32[4,2,32,128]{3,2,1,0:T(8,128)S(1)}, f32[4,2,32,128]{3,2,1,0:T(8,128)S(1)}, u32[]{:S(2)}, u32[]{:S(2)}) %collective-permute-start.1) | collective-permute-done | bytes 131104 | tf_op jit(solution)/shard_map/ppermute | solution.py:549
  13.2 1.3 %collective-permute-done.2.after = f32[4,2,32,128]{3,2,1,0:T(8,128)S(1)} collective-permute-done((f32[4,2,32,128]{3,2,1,0:T(8,128)S(1)}, f32[4,2,32,128]{3,2,1,0:T(8,128)S(1)}, u32[]{:S(2)}, u32[]{:S(2)}) %collective-permute-start.2) | collective-permute-done | bytes 131104 | tf_op jit(solution)/shard_map/ppermute | solution.py:550
  14.5 0.3 %shard_map.107 = (f32[4,8,32,128]{3,2,1,0:T(8,128)S(1)}, f32[2,8,32,128]{3,2,1,0:T(8,128)S(1)}, f32[8,32,128]{2,1,0:T(8,128)S(1)}, f32[8,32,128]{2,1,0:T(8,128)S(1)}) custom-call(f32[4,8,32,128]{3,2,1,0:T(8,128)S(1)} %get-tuple-element.39.own, f32[4,2,32,128]{3,2,1,0:T(8,128)S(1)} %collective-permute-done.1.before, ...), custom_call_target="tpu_custom_call" | custom-call | bytes 2228224 | tf_op jit(solution)/shard_map/pallas_call | solution.py:507
  14.9 0.6 %collective-permute-start.8 = (f32[8,32,128]{2,1,0:T(8,128)S(1)}, f32[8,32,128]{2,1,0:T(8,128)S(1)}, u32[]{:S(2)}, u32[]{:S(2)}) collective-permute-start(f32[8,32,128]{2,1,0:T(8,128)S(1)} %get-tuple-element.48), channel_id=1, source_target_pairs={{0,1},{1,0},{2,3},{3,2},{4,5},{5,4},{6,7},{7,6},{8,9},{9,8},{10,11... | collective-permute-start | bytes 393224 | tf_op jit(solution)/shard_map/ppermute | solution.py:564
  15.4 0.1 collective-permute-start.9
  15.5 0.3 %collective-permute-done.7.mate_w = f32[8,32,128]{2,1,0:T(8,128)S(1)} collective-permute-done((f32[8,32,128]{2,1,0:T(8,128)S(1)}, f32[8,32,128]{2,1,0:T(8,128)S(1)}, u32[]{:S(2)}, u32[]{:S(2)}) %collective-permute-start.7) | collective-permute-done | bytes 131104 | tf_op jit(solution)/shard_map/ppermute | solution.py:556
  15.8 1.5 %collective-permute-start.3 = (f32[2,8,32,128]{3,2,1,0:T(8,128)S(1)}, f32[2,8,32,128]{3,2,1,0:T(8,128)S(1)}, u32[]{:S(2)}, u32[]{:S(2)}) collective-permute-start(f32[2,8,32,128]{3,2,1,0:T(8,128)S(1)} %get-tuple-element.43.third), channel_id=1, source_target_pairs={{0,2},{1,3},{2,0},{3,1},{4,6},{5,7},{6,4},{7,5},{8,10},{9,11},{10,... | collective-permute-start | bytes 786440 | tf_op jit(solution)/shard_map/ppermute | solution.py:565
  17.4 0.9 %shard_map.108 = (f32[2,256,256]{2,1,0:T(8,128)S(1)}, f32[5,8,32,128]{3,2,1,0:T(8,128)S(1)}, f32[5,2,32,128]{3,2,1,0:T(8,128)S(1)}, f32[5,2,32,128]{3,2,1,0:T(8,128)S(1)}) custom-call(f32[4,8,32,128]{3,2,1,0:T(8,128)S(1)} %get-tuple-element.39.own, f32[3,8,32,128]{3,2,1,0:T(8,128)S(1)} %get-tuple-element.44.second, ...), custom_call_target="tpu_custom_call" | custom-call | bytes 5439488 | tf_op jit(solution)/shard_map/pallas_call | solution.py:507
  18.3 0.8 %collective-permute-start.12 = (f32[5,2,32,128]{3,2,1,0:T(8,128)S(1)}, f32[5,2,32,128]{3,2,1,0:T(8,128)S(1)}, u32[]{:S(2)}, u32[]{:S(2)}) collective-permute-start(f32[5,2,32,128]{3,2,1,0:T(8,128)S(1)} %get-tuple-element.63), channel_id=1, source_target_pairs={{0,4},{4,8},{8,12},{12,16},{16,20},{20,24},{24,28},{28,0},{1,5},{5... | collective-permute-start | bytes 491528 | tf_op jit(solution)/shard_map/ppermute | solution.py:574
  19.1 3.9 %collective-permute-start.13 = (f32[5,2,32,128]{3,2,1,0:T(8,128)S(1)}, f32[5,2,32,128]{3,2,1,0:T(8,128)S(1)}, u32[]{:S(2)}, u32[]{:S(2)}) collective-permute-start(f32[5,2,32,128]{3,2,1,0:T(8,128)S(1)} %get-tuple-element.64), channel_id=1, source_target_pairs={{4,0},{8,4},{12,8},{16,12},{20,16},{24,20},{28,24},{0,28},{5,1},{9... | collective-permute-start | bytes 491528 | tf_op jit(solution)/shard_map/ppermute | solution.py:575
  23.2 0.5 %collective-permute-start.11 = (f32[8,32,128]{2,1,0:T(8,128)S(1)}, f32[8,32,128]{2,1,0:T(8,128)S(1)}, u32[]{:S(2)}, u32[]{:S(2)}) collective-permute-start(f32[8,32,128]{2,1,0:T(8,128)S(1)} %get-tuple-element.54), channel_id=1, source_target_pairs={{0,1},{1,0},{2,3},{3,2},{4,5},{5,4},{6,7},{7,6},{8,9},{9,8},{10,11... | collective-permute-start | bytes 393224 | tf_op jit(solution)/shard_map/ppermute | solution.py:578
  23.7 0.3 %copy-done = bf16[2,256,256]{2,1,0:T(8,128)(2,1)S(1)} copy-done((bf16[2,256,256]{2,1,0:T(8,128)(2,1)S(1)}, bf16[2,256,256]{2,1,0:T(8,128)(2,1)}, u32[]{:S(2)}) %copy-start) | copy-done | bytes 262168
  24.0 0.1 copy-done.1
  24.1 1.4 %shard_map.110 = (f32[3,256,256]{2,1,0:T(8,128)S(1)}, f32[3,256,128]{2,1,0:T(8,128)S(1)}, f32[2,256,128]{2,1,0:T(8,128)S(1)}, f32[256,128]{1,0:T(8,128)S(1)}) custom-call(f32[4,8,32,128]{3,2,1,0:T(8,128)S(1)} %get-tuple-element.39.own, f32[3,8,32,128]{3,2,1,0:T(8,128)S(1)} %get-tuple-element.44.second, ...), custom_call_target="tpu_custom_call" | custom-call | bytes 5767168 | tf_op jit(solution)/shard_map/pallas_call | solution.py:507
  25.5 1.6 %shard_map.111 = (f32[5,8,32,128]{3,2,1,0:T(8,128)S(1)}, f32[5,8,32,128]{3,2,1,0:T(8,128)S(1)}) custom-call(f32[4,8,32,128]{3,2,1,0:T(8,128)S(1)} %get-tuple-element.39.own, f32[3,8,32,128]{3,2,1,0:T(8,128)S(1)} %get-tuple-element.44.second, f32[2,8,32,128]{3,2,1,0:T(8,128)S(1)} %collective-permute-done.peer_first, ...), custom_call_target="tpu_custom_call" | custom-call | bytes 8519680 | tf_op jit(solution)/shard_map/pallas_call | solution.py:507
  27.1 0.5 %shard_map.112 = (f32[5,8,32,128]{3,2,1,0:T(8,128)S(1)}, f32[8,32,128]{2,1,0:T(8,128)S(1)}, f32[8,32,128]{2,1,0:T(8,128)S(1)}, f32[8,32,128]{2,1,0:T(8,128)S(1)}...) custom-call(f32[4,8,32,128]{3,2,1,0:T(8,128)S(1)} %get-tuple-element.39.own, ...), custom_call_target="tpu_custom_call" | custom-call | bytes 4456448 | tf_op jit(solution)/shard_map/pallas_call | solution.py:507
  27.7 0.5 %collective-permute-start.15 = (f32[8,32,128]{2,1,0:T(8,128)S(1)}, f32[8,32,128]{2,1,0:T(8,128)S(1)}, u32[]{:S(2)}, u32[]{:S(2)}) collective-permute-start(f32[8,32,128]{2,1,0:T(8,128)S(1)} %get-tuple-element.66), channel_id=1, source_target_pairs={{0,1},{1,0},{2,3},{3,2},{4,5},{5,4},{6,7},{7,6},{8,9},{9,8},{10,11... | collective-permute-start | bytes 393224 | tf_op jit(solution)/shard_map/ppermute | solution.py:610
  28.2 0.1 collective-permute-start.16
  28.3 0.4 %collective-permute-start.17 = (f32[8,32,128]{2,1,0:T(8,128)S(1)}, f32[8,32,128]{2,1,0:T(8,128)S(1)}, u32[]{:S(2)}, u32[]{:S(2)}) collective-permute-start(f32[8,32,128]{2,1,0:T(8,128)S(1)} %get-tuple-element.68), channel_id=1, source_target_pairs={{0,1},{1,0},{2,3},{3,2},{4,5},{5,4},{6,7},{7,6},{8,9},{9,8},{10,11... | collective-permute-start | bytes 393224 | tf_op jit(solution)/shard_map/ppermute | solution.py:610
  28.8 0.1 collective-permute-start.18
  28.8 0.4 %shard_map.113.total = f32[5,8,32,128]{3,2,1,0:T(8,128)S(1)} custom-call(f32[5,8,32,128]{3,2,1,0:T(8,128)S(1)} %get-tuple-element.62.total, f32[5,8,32,128]{3,2,1,0:T(8,128)S(1)} %get-tuple-element.52.flux, f32[5,2,32,128]{3,2,1,0:T(8,128)S(1)} %collective-permute-done.12.before, f32[5,2,32,128]{3,2,1,0:T(8,128)S(1)} %collective-permute-done.13.after), custom_call_target="tpu_custom_call" | custom-call | bytes 2293760 | tf_op jit(solution)/shard_map/pallas_call | solution.py:507
  29.3 0.3 %collective-permute-done.16.mate_2 = f32[8,32,128]{2,1,0:T(8,128)S(1)} collective-permute-done((f32[8,32,128]{2,1,0:T(8,128)S(1)}, f32[8,32,128]{2,1,0:T(8,128)S(1)}, u32[]{:S(2)}, u32[]{:S(2)}) %collective-permute-start.16) | collective-permute-done | bytes 131104 | tf_op jit(solution)/shard_map/ppermute | solution.py:610
  29.6 0.2 collective-permute-done.17.mate_3
  29.8 0.3 %collective-permute-done.18.mate_4 = f32[8,32,128]{2,1,0:T(8,128)S(1)} collective-permute-done((f32[8,32,128]{2,1,0:T(8,128)S(1)}, f32[8,32,128]{2,1,0:T(8,128)S(1)}, u32[]{:S(2)}, u32[]{:S(2)}) %collective-permute-start.18) | collective-permute-done | bytes 131104 | tf_op jit(solution)/shard_map/ppermute | solution.py:610
  30.1 1.2 %shard_map.114 = (f32[5,8,32,128]{3,2,1,0:T(8,128)}, f32[5,8,32,128]{3,2,1,0:T(8,128)}) custom-call(f32[5,8,32,128]{3,2,1,0:T(8,128)S(1)} %get-tuple-element.37.conserved, f32[5,8,32,128]{3,2,1,0:T(8,128)S(1)} %shard_map.113.total, f32[8,32,128]{2,1,0:T(8,128)S(1)} %collective-permute-done.14.mate_0, f32[8,32,128]{2,1,0:T(8,128)S(1)} %collective-permute-done.15.mate_1, ...), custom_call_target="tpu_custom_call" | custom-call | bytes 3276800 | tf_op jit(solution)/shard_map/pallas_call | solution.py:507
  (29 shorter events, 0.3 us)
Async XLA Ops:
  1.8 12.7 %collective-permute-start = (f32[2,8,32,128]{3,2,1,0:T(8,128)S(1)}, f32[2,8,32,128]{3,2,1,0:T(8,128)S(1)}, u32[]{:S(2)}, u32[]{:S(2)}) collective-permute-start(f32[2,8,32,128]{3,2,1,0:T(8,128)S(1)} %get-tuple-element.38.first), channel_id=1, source_target_pairs={{0,2},{1,3},{2,0},{3,1},{4,6},{5,7},{6,4},{7,5},{8,10},{9,11},{10,... | collective-permute-start | bytes 786440 | tf_op jit(solution)/shard_map/ppermute | solution.py:548
  4.8 5.4 %copy-start.4 = (bf16[256,256]{1,0:T(8,128)(2,1)S(1)}, bf16[256,256]{1,0:T(8,128)(2,1)}, u32[]{:S(2)}) copy-start(bf16[256,256]{1,0:T(8,128)(2,1)} %constant.16.clone.y_high) | copy-start | bytes 393220
  4.8 5.4 %copy-start.5 = (bf16[256,256]{1,0:T(8,128)(2,1)S(1)}, bf16[256,256]{1,0:T(8,128)(2,1)}, u32[]{:S(2)}) copy-start(bf16[256,256]{1,0:T(8,128)(2,1)} %constant.17.clone.y_low) | copy-start | bytes 393220
  5.0 18.1 %collective-permute-start.4 = (f32[3,8,32,128]{3,2,1,0:T(8,128)S(1)}, f32[3,8,32,128]{3,2,1,0:T(8,128)S(1)}, u32[]{:S(2)}, u32[]{:S(2)}) collective-permute-start(f32[3,8,32,128]{3,2,1,0:T(8,128)S(1)} %get-tuple-element.44.second), channel_id=1, source_target_pairs={{0,2},{1,3},{2,0},{3,1},{4,6},{5,7},{6,4},{7,5},{8,10},{9,11},{10,... | collective-permute-start | bytes 1179656 | tf_op jit(solution)/shard_map/ppermute | solution.py:558
  5.1 8.1 %collective-permute-start.1 = (f32[4,2,32,128]{3,2,1,0:T(8,128)S(1)}, f32[4,2,32,128]{3,2,1,0:T(8,128)S(1)}, u32[]{:S(2)}, u32[]{:S(2)}) collective-permute-start(f32[4,2,32,128]{3,2,1,0:T(8,128)S(1)} %get-tuple-element.40), channel_id=1, source_target_pairs={{0,4},{4,8},{8,12},{12,16},{16,20},{20,24},{24,28},{28,0},{1,5},{5... | collective-permute-start | bytes 393224 | tf_op jit(solution)/shard_map/ppermute | solution.py:549
  7.1 7.4 %collective-permute-start.2 = (f32[4,2,32,128]{3,2,1,0:T(8,128)S(1)}, f32[4,2,32,128]{3,2,1,0:T(8,128)S(1)}, u32[]{:S(2)}, u32[]{:S(2)}) collective-permute-start(f32[4,2,32,128]{3,2,1,0:T(8,128)S(1)} %get-tuple-element.41), channel_id=1, source_target_pairs={{4,0},{8,4},{12,8},{16,12},{20,16},{24,20},{28,24},{0,28},{5,1},{9... | collective-permute-start | bytes 393224 | tf_op jit(solution)/shard_map/ppermute | solution.py:550
  10.9 4.5 %collective-permute-start.6 = (f32[8,32,128]{2,1,0:T(8,128)S(1)}, f32[8,32,128]{2,1,0:T(8,128)S(1)}, u32[]{:S(2)}, u32[]{:S(2)}) collective-permute-start(f32[8,32,128]{2,1,0:T(8,128)S(1)} %get-tuple-element.46), channel_id=1, source_target_pairs={{0,1},{1,0},{2,3},{3,2},{4,5},{5,4},{6,7},{7,6},{8,9},{9,8},{10,11... | collective-permute-start | bytes 393224 | tf_op jit(solution)/shard_map/ppermute | solution.py:556
  13.2 10.0 %collective-permute-start.5 = (f32[2,8,32,128]{3,2,1,0:T(8,128)S(1)}, f32[2,8,32,128]{3,2,1,0:T(8,128)S(1)}, u32[]{:S(2)}, u32[]{:S(2)}) collective-permute-start(f32[2,8,32,128]{3,2,1,0:T(8,128)S(1)} %get-tuple-element.45), channel_id=1, source_target_pairs={{0,1},{1,0},{2,3},{3,2},{4,5},{5,4},{6,7},{7,6},{8,9},{9,8},{10,11... | collective-permute-start | bytes 786440 | tf_op jit(solution)/shard_map/ppermute | solution.py:557
  14.5 1.3 %collective-permute-start.7 = (f32[8,32,128]{2,1,0:T(8,128)S(1)}, f32[8,32,128]{2,1,0:T(8,128)S(1)}, u32[]{:S(2)}, u32[]{:S(2)}) collective-permute-start(f32[8,32,128]{2,1,0:T(8,128)S(1)} %get-tuple-element.47), channel_id=1, source_target_pairs={{0,1},{1,0},{2,3},{3,2},{4,5},{5,4},{6,7},{7,6},{8,9},{9,8},{10,11... | collective-permute-start | bytes 393224 | tf_op jit(solution)/shard_map/ppermute | solution.py:556
  14.5 2.8 %copy-start.2 = (bf16[2,512,256]{2,1,0:T(8,128)(2,1)S(1)}, bf16[2,512,256]{2,1,0:T(8,128)(2,1)}, u32[]{:S(2)}) copy-start(bf16[2,512,256]{2,1,0:T(8,128)(2,1)} %constant.12.clone.z_high) | copy-start | bytes 1572868
  14.5 2.8 %copy-start.3 = (bf16[2,512,256]{2,1,0:T(8,128)(2,1)S(1)}, bf16[2,512,256]{2,1,0:T(8,128)(2,1)}, u32[]{:S(2)}) copy-start(bf16[2,512,256]{2,1,0:T(8,128)(2,1)} %constant.13.clone.z_low) | copy-start | bytes 1572868
  14.9 2.5 %collective-permute-start.8 = (f32[8,32,128]{2,1,0:T(8,128)S(1)}, f32[8,32,128]{2,1,0:T(8,128)S(1)}, u32[]{:S(2)}, u32[]{:S(2)}) collective-permute-start(f32[8,32,128]{2,1,0:T(8,128)S(1)} %get-tuple-element.48), channel_id=1, source_target_pairs={{0,1},{1,0},{2,3},{3,2},{4,5},{5,4},{6,7},{7,6},{8,9},{9,8},{10,11... | collective-permute-start | bytes 393224 | tf_op jit(solution)/shard_map/ppermute | solution.py:564
  15.4 1.9 %collective-permute-start.9 = (f32[8,32,128]{2,1,0:T(8,128)S(1)}, f32[8,32,128]{2,1,0:T(8,128)S(1)}, u32[]{:S(2)}, u32[]{:S(2)}) collective-permute-start(f32[8,32,128]{2,1,0:T(8,128)S(1)} %get-tuple-element.49), channel_id=1, source_target_pairs={{0,1},{1,0},{2,3},{3,2},{4,5},{5,4},{6,7},{7,6},{8,9},{9,8},{10,11... | collective-permute-start | bytes 393224 | tf_op jit(solution)/shard_map/ppermute | solution.py:564
  15.8 11.3 %collective-permute-start.3 = (f32[2,8,32,128]{3,2,1,0:T(8,128)S(1)}, f32[2,8,32,128]{3,2,1,0:T(8,128)S(1)}, u32[]{:S(2)}, u32[]{:S(2)}) collective-permute-start(f32[2,8,32,128]{3,2,1,0:T(8,128)S(1)} %get-tuple-element.43.third), channel_id=1, source_target_pairs={{0,2},{1,3},{2,0},{3,1},{4,6},{5,7},{6,4},{7,5},{8,10},{9,11},{10,... | collective-permute-start | bytes 786440 | tf_op jit(solution)/shard_map/ppermute | solution.py:565
  18.3 10.0 %collective-permute-start.12 = (f32[5,2,32,128]{3,2,1,0:T(8,128)S(1)}, f32[5,2,32,128]{3,2,1,0:T(8,128)S(1)}, u32[]{:S(2)}, u32[]{:S(2)}) collective-permute-start(f32[5,2,32,128]{3,2,1,0:T(8,128)S(1)} %get-tuple-element.63), channel_id=1, source_target_pairs={{0,4},{4,8},{8,12},{12,16},{16,20},{20,24},{24,28},{28,0},{1,5},{5... | collective-permute-start | bytes 491528 | tf_op jit(solution)/shard_map/ppermute | solution.py:574
  19.1 9.6 %collective-permute-start.13 = (f32[5,2,32,128]{3,2,1,0:T(8,128)S(1)}, f32[5,2,32,128]{3,2,1,0:T(8,128)S(1)}, u32[]{:S(2)}, u32[]{:S(2)}) collective-permute-start(f32[5,2,32,128]{3,2,1,0:T(8,128)S(1)} %get-tuple-element.64), channel_id=1, source_target_pairs={{4,0},{8,4},{12,8},{16,12},{20,16},{24,20},{28,24},{0,28},{5,1},{9... | collective-permute-start | bytes 491528 | tf_op jit(solution)/shard_map/ppermute | solution.py:575
  23.1 1.0 %copy-start = (bf16[2,256,256]{2,1,0:T(8,128)(2,1)S(1)}, bf16[2,256,256]{2,1,0:T(8,128)(2,1)}, u32[]{:S(2)}) copy-start(bf16[2,256,256]{2,1,0:T(8,128)(2,1)} %constant.14.clone.f_high) | copy-start | bytes 786436
  23.1 1.0 %copy-start.1 = (bf16[2,256,256]{2,1,0:T(8,128)(2,1)S(1)}, bf16[2,256,256]{2,1,0:T(8,128)(2,1)}, u32[]{:S(2)}) copy-start(bf16[2,256,256]{2,1,0:T(8,128)(2,1)} %constant.15.clone.f_low) | copy-start | bytes 786436
  23.1 2.4 %collective-permute-start.10 = (f32[8,32,128]{2,1,0:T(8,128)S(1)}, f32[8,32,128]{2,1,0:T(8,128)S(1)}, u32[]{:S(2)}, u32[]{:S(2)}) collective-permute-start(f32[8,32,128]{2,1,0:T(8,128)S(1)} %get-tuple-element.53.for_v), channel_id=1, source_target_pairs={{0,1},{1,0},{2,3},{3,2},{4,5},{5,4},{6,7},{7,6},{8,9},{9,8},{10,11... | collective-permute-start | bytes 393224 | tf_op jit(solution)/shard_map/ppermute | solution.py:577
  23.2 2.3 %collective-permute-start.11 = (f32[8,32,128]{2,1,0:T(8,128)S(1)}, f32[8,32,128]{2,1,0:T(8,128)S(1)}, u32[]{:S(2)}, u32[]{:S(2)}) collective-permute-start(f32[8,32,128]{2,1,0:T(8,128)S(1)} %get-tuple-element.54), channel_id=1, source_target_pairs={{0,1},{1,0},{2,3},{3,2},{4,5},{5,4},{6,7},{7,6},{8,9},{9,8},{10,11... | collective-permute-start | bytes 393224 | tf_op jit(solution)/shard_map/ppermute | solution.py:578
  27.7 1.5 %collective-permute-start.14 = (f32[8,32,128]{2,1,0:T(8,128)S(1)}, f32[8,32,128]{2,1,0:T(8,128)S(1)}, u32[]{:S(2)}, u32[]{:S(2)}) collective-permute-start(f32[8,32,128]{2,1,0:T(8,128)S(1)} %get-tuple-element.65), channel_id=1, source_target_pairs={{0,1},{1,0},{2,3},{3,2},{4,5},{5,4},{6,7},{7,6},{8,9},{9,8},{10,11... | collective-permute-start | bytes 393224 | tf_op jit(solution)/shard_map/ppermute | solution.py:610
  27.7 1.5 %collective-permute-start.15 = (f32[8,32,128]{2,1,0:T(8,128)S(1)}, f32[8,32,128]{2,1,0:T(8,128)S(1)}, u32[]{:S(2)}, u32[]{:S(2)}) collective-permute-start(f32[8,32,128]{2,1,0:T(8,128)S(1)} %get-tuple-element.66), channel_id=1, source_target_pairs={{0,1},{1,0},{2,3},{3,2},{4,5},{5,4},{6,7},{7,6},{8,9},{9,8},{10,11... | collective-permute-start | bytes 393224 | tf_op jit(solution)/shard_map/ppermute | solution.py:610
  28.2 1.3 %collective-permute-start.16 = (f32[8,32,128]{2,1,0:T(8,128)S(1)}, f32[8,32,128]{2,1,0:T(8,128)S(1)}, u32[]{:S(2)}, u32[]{:S(2)}) collective-permute-start(f32[8,32,128]{2,1,0:T(8,128)S(1)} %get-tuple-element.67), channel_id=1, source_target_pairs={{0,1},{1,0},{2,3},{3,2},{4,5},{5,4},{6,7},{7,6},{8,9},{9,8},{10,11... | collective-permute-start | bytes 393224 | tf_op jit(solution)/shard_map/ppermute | solution.py:610
  28.3 1.5 %collective-permute-start.17 = (f32[8,32,128]{2,1,0:T(8,128)S(1)}, f32[8,32,128]{2,1,0:T(8,128)S(1)}, u32[]{:S(2)}, u32[]{:S(2)}) collective-permute-start(f32[8,32,128]{2,1,0:T(8,128)S(1)} %get-tuple-element.68), channel_id=1, source_target_pairs={{0,1},{1,0},{2,3},{3,2},{4,5},{5,4},{6,7},{7,6},{8,9},{9,8},{10,11... | collective-permute-start | bytes 393224 | tf_op jit(solution)/shard_map/ppermute | solution.py:610
  28.8 1.3 %collective-permute-start.18 = (f32[8,32,128]{2,1,0:T(8,128)S(1)}, f32[8,32,128]{2,1,0:T(8,128)S(1)}, u32[]{:S(2)}, u32[]{:S(2)}) collective-permute-start(f32[8,32,128]{2,1,0:T(8,128)S(1)} %get-tuple-element.69), channel_id=1, source_target_pairs={{0,1},{1,0},{2,3},{3,2},{4,5},{5,4},{6,7},{7,6},{8,9},{9,8},{10,11... | collective-permute-start | bytes 393224 | tf_op jit(solution)/shard_map/ppermute | solution.py:610

commit v6 on v5

--- a/solution.py
+++ b/solution.py
@@ -286,7 +286,7 @@
 
 def kernel_flux_x(
     own, second, peer_first, mate_u, mate_w, across_u, across_w, dx, dy, mu,
-    z_high, z_low, dz, flux, up, down,
+    z_high, z_low, f_high, f_low, dz, flux, up, down,
 ):
     width = own.shape[-1]
     odd = lax.rem(lax.axis_index("gy"), 2)
@@ -568,7 +568,7 @@
         [(2, points, 2 * width), (5,) + block, (5,) + sums, (5,) + sums],
         (
             own, second, peer_first, mate_u, mate_w, across_u, across_w, dx, dy, mu,
-            z_high, z_low,
+            z_high, z_low, f_high, f_low,
         ),
     )
     flux_before = lax.ppermute(flux_up, "gx", ring_up)

time: 31.4 us -> 31 us (0.987)
  local copies, waits for them, and re-layouts: 0.44 us -> 0.03 us
    unnamed x12, local copies, waits for them, and re-layouts: 0.44 us -> 0.03 us
  transfers between devices with their start and end apart: 19 -> 19, of which waited for: 7 -> 6; matrix products, arithmetic and copies ran while one was open for 0% -> 0% of each run, Pallas kernels for 19% -> 20%
where the time goes in v6:
time: 31 us; the launch traced here: 30.9 us
  starting transfers between devices  16.9 us (55%)
  Pallas kernels  8.37 us (27%)
  waiting for transfers between devices  4.76 us (15%)
  between operations  0.82 us (3%)
    pallas_call x11, Pallas kernels, call(): pl.pallas_call(kernel, out_shape=[jax.ShapeDtypeStruct(shape, F32) for sh...  8.37 us
    ppermute x1, starting transfers between devices, fast_device(): flux_after = lax.ppermute(flux_down, 'gx', ring_down)  3.95 us
    ppermute x1, starting transfers between devices, fast_device(): after = lax.ppermute(down, 'gx', ring_down)  3.04 us
    ppermute x1, starting transfers between devices, fast_device(): peer_first = lax.ppermute(first, 'gy', to_peer)  3 us
    ppermute x1, waiting for transfers between devices, fast_device(): before = lax.ppermute(up, 'gx', ring_up)  2.23 us
    ppermute x1, starting transfers between devices, fast_device(): before = lax.ppermute(up, 'gx', ring_up)  2.01 us
    ppermute x1, starting transfers between devices, fast_device(): peer_third = lax.ppermute(third, 'gy', to_peer)  1.49 us
    ppermute x1, waiting for transfers between devices, fast_device(): after = lax.ppermute(down, 'gx', ring_down)  1.3 us
  transfers between devices with their start and end apart: 19, of which 6 were waited for; matrix products, arithmetic and copies ran while one was open for 0% of the time, Pallas kernels for 20%

profile of v6, /device:TPU:0, one launch (start us, length us, event | category | flops | bytes accessed | tf_op | source)
XLA Modules:
  0.0 30.9 jit_solution(13229390832030406992)
XLA Ops:
  0.6 1.2 %shard_map.104 = (f32[5,8,32,128]{3,2,1,0:T(8,128)S(1)}, f32[2,8,32,128]{3,2,1,0:T(8,128)S(1)}) custom-call(f32[8,32,128]{2,1,0:T(8,128)} %bitcast.6, f32[3,8,32,128]{3,2,1,0:T(8,128)} %bitcast.5, f32[8,32,128]{2,1,0:T(8,128)} %bitcast.7), custom_call_target="tpu_custom_call" | custom-call | bytes 1572864 | tf_op jit(solution)/shard_map/pallas_call | solution.py:507
  1.8 3.0 %collective-permute-start = (f32[2,8,32,128]{3,2,1,0:T(8,128)S(1)}, f32[2,8,32,128]{3,2,1,0:T(8,128)S(1)}, u32[]{:S(2)}, u32[]{:S(2)}) collective-permute-start(f32[2,8,32,128]{3,2,1,0:T(8,128)S(1)} %get-tuple-element.38.first), channel_id=1, source_target_pairs={{0,2},{1,3},{2,0},{3,1},{4,6},{5,7},{6,4},{7,5},{8,10},{9,11},{10,... | collective-permute-start | bytes 786440 | tf_op jit(solution)/shard_map/ppermute | solution.py:548
  4.8 0.2 shard_map.105
  5.0 0.1 collective-permute-start.4
  5.1 2.0 %collective-permute-start.1 = (f32[4,2,32,128]{3,2,1,0:T(8,128)S(1)}, f32[4,2,32,128]{3,2,1,0:T(8,128)S(1)}, u32[]{:S(2)}, u32[]{:S(2)}) collective-permute-start(f32[4,2,32,128]{3,2,1,0:T(8,128)S(1)} %get-tuple-element.40), channel_id=1, source_target_pairs={{0,4},{4,8},{8,12},{12,16},{16,20},{20,24},{24,28},{28,0},{1,5},{5... | collective-permute-start | bytes 393224 | tf_op jit(solution)/shard_map/ppermute | solution.py:549
  7.1 3.0 %collective-permute-start.2 = (f32[4,2,32,128]{3,2,1,0:T(8,128)S(1)}, f32[4,2,32,128]{3,2,1,0:T(8,128)S(1)}, u32[]{:S(2)}, u32[]{:S(2)}) collective-permute-start(f32[4,2,32,128]{3,2,1,0:T(8,128)S(1)} %get-tuple-element.41), channel_id=1, source_target_pairs={{4,0},{8,4},{12,8},{16,12},{20,16},{24,20},{28,24},{0,28},{5,1},{9... | collective-permute-start | bytes 393224 | tf_op jit(solution)/shard_map/ppermute | solution.py:550
  10.2 0.7 %shard_map.106 = (f32[4,8,32,128]{3,2,1,0:T(8,128)S(1)}, f32[8,32,128]{2,1,0:T(8,128)S(1)}, f32[8,32,128]{2,1,0:T(8,128)S(1)}, f32[8,32,128]{2,1,0:T(8,128)S(1)}, f32[2,8,32,128]{3,2,1,0:T(8,128)S(1)}) custom-call(f32[4,8,32,128]{3,2,1,0:T(8,128)S(1)} %get-tuple-element.39.own, bf16[256,256]{1,0:T(8,128)(2,1)S(1)} %copy-done.4, bf16[256,256]{1,0:T(8,128)(2,1)S(1)} %copy-done.5), custom_call_target="tpu_custom_call" | custom-call | bytes 1966080 | tf_op jit(solution)/shard_map/pallas_call | solution.py:507
  11.0 2.2 %collective-permute-done.1.before = f32[4,2,32,128]{3,2,1,0:T(8,128)S(1)} collective-permute-done((f32[4,2,32,128]{3,2,1,0:T(8,128)S(1)}, f32[4,2,32,128]{3,2,1,0:T(8,128)S(1)}, u32[]{:S(2)}, u32[]{:S(2)}) %collective-permute-start.1) | collective-permute-done | bytes 131104 | tf_op jit(solution)/shard_map/ppermute | solution.py:549
  13.2 1.3 %collective-permute-done.2.after = f32[4,2,32,128]{3,2,1,0:T(8,128)S(1)} collective-permute-done((f32[4,2,32,128]{3,2,1,0:T(8,128)S(1)}, f32[4,2,32,128]{3,2,1,0:T(8,128)S(1)}, u32[]{:S(2)}, u32[]{:S(2)}) %collective-permute-start.2) | collective-permute-done | bytes 131104 | tf_op jit(solution)/shard_map/ppermute | solution.py:550
  14.5 0.3 %shard_map.107 = (f32[4,8,32,128]{3,2,1,0:T(8,128)S(1)}, f32[2,8,32,128]{3,2,1,0:T(8,128)S(1)}, f32[8,32,128]{2,1,0:T(8,128)S(1)}, f32[8,32,128]{2,1,0:T(8,128)S(1)}) custom-call(f32[4,8,32,128]{3,2,1,0:T(8,128)S(1)} %get-tuple-element.39.own, f32[4,2,32,128]{3,2,1,0:T(8,128)S(1)} %collective-permute-done.1.before, ...), custom_call_target="tpu_custom_call" | custom-call | bytes 2228224 | tf_op jit(solution)/shard_map/pallas_call | solution.py:507
  14.9 0.6 %collective-permute-start.8 = (f32[8,32,128]{2,1,0:T(8,128)S(1)}, f32[8,32,128]{2,1,0:T(8,128)S(1)}, u32[]{:S(2)}, u32[]{:S(2)}) collective-permute-start(f32[8,32,128]{2,1,0:T(8,128)S(1)} %get-tuple-element.48), channel_id=1, source_target_pairs={{0,1},{1,0},{2,3},{3,2},{4,5},{5,4},{6,7},{7,6},{8,9},{9,8},{10,11... | collective-permute-start | bytes 393224 | tf_op jit(solution)/shard_map/ppermute | solution.py:564
  15.4 0.1 collective-permute-start.9
  15.5 0.3 %collective-permute-done.7.mate_w = f32[8,32,128]{2,1,0:T(8,128)S(1)} collective-permute-done((f32[8,32,128]{2,1,0:T(8,128)S(1)}, f32[8,32,128]{2,1,0:T(8,128)S(1)}, u32[]{:S(2)}, u32[]{:S(2)}) %collective-permute-start.7) | collective-permute-done | bytes 131104 | tf_op jit(solution)/shard_map/ppermute | solution.py:556
  15.8 1.5 %collective-permute-start.3 = (f32[2,8,32,128]{3,2,1,0:T(8,128)S(1)}, f32[2,8,32,128]{3,2,1,0:T(8,128)S(1)}, u32[]{:S(2)}, u32[]{:S(2)}) collective-permute-start(f32[2,8,32,128]{3,2,1,0:T(8,128)S(1)} %get-tuple-element.43.third), channel_id=1, source_target_pairs={{0,2},{1,3},{2,0},{3,1},{4,6},{5,7},{6,4},{7,5},{8,10},{9,11},{10,... | collective-permute-start | bytes 786440 | tf_op jit(solution)/shard_map/ppermute | solution.py:565
  17.4 0.9 %shard_map.108 = (f32[2,256,256]{2,1,0:T(8,128)S(1)}, f32[5,8,32,128]{3,2,1,0:T(8,128)S(1)}, f32[5,2,32,128]{3,2,1,0:T(8,128)S(1)}, f32[5,2,32,128]{3,2,1,0:T(8,128)S(1)}) custom-call(f32[4,8,32,128]{3,2,1,0:T(8,128)S(1)} %get-tuple-element.39.own, f32[3,8,32,128]{3,2,1,0:T(8,128)S(1)} %get-tuple-element.44.second, ...), custom_call_target="tpu_custom_call" | custom-call | bytes 5963776 | tf_op jit(solution)/shard_map/pallas_call | solution.py:507
  18.3 0.8 %collective-permute-start.12 = (f32[5,2,32,128]{3,2,1,0:T(8,128)S(1)}, f32[5,2,32,128]{3,2,1,0:T(8,128)S(1)}, u32[]{:S(2)}, u32[]{:S(2)}) collective-permute-start(f32[5,2,32,128]{3,2,1,0:T(8,128)S(1)} %get-tuple-element.63), channel_id=1, source_target_pairs={{0,4},{4,8},{8,12},{12,16},{16,20},{20,24},{24,28},{28,0},{1,5},{5... | collective-permute-start | bytes 491528 | tf_op jit(solution)/shard_map/ppermute | solution.py:574
  19.1 4.0 %collective-permute-start.13 = (f32[5,2,32,128]{3,2,1,0:T(8,128)S(1)}, f32[5,2,32,128]{3,2,1,0:T(8,128)S(1)}, u32[]{:S(2)}, u32[]{:S(2)}) collective-permute-start(f32[5,2,32,128]{3,2,1,0:T(8,128)S(1)} %get-tuple-element.64), channel_id=1, source_target_pairs={{4,0},{8,4},{12,8},{16,12},{20,16},{24,20},{28,24},{0,28},{5,1},{9... | collective-permute-start | bytes 491528 | tf_op jit(solution)/shard_map/ppermute | solution.py:575
  23.1 0.1 collective-permute-start.10
  23.2 0.5 %collective-permute-start.11 = (f32[8,32,128]{2,1,0:T(8,128)S(1)}, f32[8,32,128]{2,1,0:T(8,128)S(1)}, u32[]{:S(2)}, u32[]{:S(2)}) collective-permute-start(f32[8,32,128]{2,1,0:T(8,128)S(1)} %get-tuple-element.54), channel_id=1, source_target_pairs={{0,1},{1,0},{2,3},{3,2},{4,5},{5,4},{6,7},{7,6},{8,9},{9,8},{10,11... | collective-permute-start | bytes 393224 | tf_op jit(solution)/shard_map/ppermute | solution.py:578
  23.7 1.4 %shard_map.110 = (f32[3,256,256]{2,1,0:T(8,128)S(1)}, f32[3,256,128]{2,1,0:T(8,128)S(1)}, f32[2,256,128]{2,1,0:T(8,128)S(1)}, f32[256,128]{1,0:T(8,128)S(1)}) custom-call(f32[4,8,32,128]{3,2,1,0:T(8,128)S(1)} %get-tuple-element.39.own, f32[3,8,32,128]{3,2,1,0:T(8,128)S(1)} %get-tuple-element.44.second, ...), custom_call_target="tpu_custom_call" | custom-call | bytes 5767168 | tf_op jit(solution)/shard_map/pallas_call | solution.py:507
  25.1 1.6 %shard_map.111 = (f32[5,8,32,128]{3,2,1,0:T(8,128)S(1)}, f32[5,8,32,128]{3,2,1,0:T(8,128)S(1)}) custom-call(f32[4,8,32,128]{3,2,1,0:T(8,128)S(1)} %get-tuple-element.39.own, f32[3,8,32,128]{3,2,1,0:T(8,128)S(1)} %get-tuple-element.44.second, f32[2,8,32,128]{3,2,1,0:T(8,128)S(1)} %collective-permute-done.peer_first, ...), custom_call_target="tpu_custom_call" | custom-call | bytes 8519680 | tf_op jit(solution)/shard_map/pallas_call | solution.py:507
  26.7 0.5 %shard_map.112 = (f32[5,8,32,128]{3,2,1,0:T(8,128)S(1)}, f32[8,32,128]{2,1,0:T(8,128)S(1)}, f32[8,32,128]{2,1,0:T(8,128)S(1)}, f32[8,32,128]{2,1,0:T(8,128)S(1)}...) custom-call(f32[4,8,32,128]{3,2,1,0:T(8,128)S(1)} %get-tuple-element.39.own, ...), custom_call_target="tpu_custom_call" | custom-call | bytes 4456448 | tf_op jit(solution)/shard_map/pallas_call | solution.py:507
  27.3 0.2 collective-permute-start.14
  27.4 0.4 %collective-permute-start.15 = (f32[8,32,128]{2,1,0:T(8,128)S(1)}, f32[8,32,128]{2,1,0:T(8,128)S(1)}, u32[]{:S(2)}, u32[]{:S(2)}) collective-permute-start(f32[8,32,128]{2,1,0:T(8,128)S(1)} %get-tuple-element.66), channel_id=1, source_target_pairs={{0,1},{1,0},{2,3},{3,2},{4,5},{5,4},{6,7},{7,6},{8,9},{9,8},{10,11... | collective-permute-start | bytes 393224 | tf_op jit(solution)/shard_map/ppermute | solution.py:610
  27.8 0.1 collective-permute-start.16
  27.9 0.4 %collective-permute-start.17 = (f32[8,32,128]{2,1,0:T(8,128)S(1)}, f32[8,32,128]{2,1,0:T(8,128)S(1)}, u32[]{:S(2)}, u32[]{:S(2)}) collective-permute-start(f32[8,32,128]{2,1,0:T(8,128)S(1)} %get-tuple-element.68), channel_id=1, source_target_pairs={{0,1},{1,0},{2,3},{3,2},{4,5},{5,4},{6,7},{7,6},{8,9},{9,8},{10,11... | collective-permute-start | bytes 393224 | tf_op jit(solution)/shard_map/ppermute | solution.py:610
  28.4 0.1 collective-permute-start.18
  28.4 0.4 %shard_map.113.total = f32[5,8,32,128]{3,2,1,0:T(8,128)S(1)} custom-call(f32[5,8,32,128]{3,2,1,0:T(8,128)S(1)} %get-tuple-element.62.total, f32[5,8,32,128]{3,2,1,0:T(8,128)S(1)} %get-tuple-element.52.flux, f32[5,2,32,128]{3,2,1,0:T(8,128)S(1)} %collective-permute-done.12.before, f32[5,2,32,128]{3,2,1,0:T(8,128)S(1)} %collective-permute-done.13.after), custom_call_target="tpu_custom_call" | custom-call | bytes 2293760 | tf_op jit(solution)/shard_map/pallas_call | solution.py:507
  28.9 0.3 %collective-permute-done.16.mate_2 = f32[8,32,128]{2,1,0:T(8,128)S(1)} collective-permute-done((f32[8,32,128]{2,1,0:T(8,128)S(1)}, f32[8,32,128]{2,1,0:T(8,128)S(1)}, u32[]{:S(2)}, u32[]{:S(2)}) %collective-permute-start.16) | collective-permute-done | bytes 131104 | tf_op jit(solution)/shard_map/ppermute | solution.py:610
  29.2 0.2 collective-permute-done.17.mate_3
  29.4 0.3 %collective-permute-done.18.mate_4 = f32[8,32,128]{2,1,0:T(8,128)S(1)} collective-permute-done((f32[8,32,128]{2,1,0:T(8,128)S(1)}, f32[8,32,128]{2,1,0:T(8,128)S(1)}, u32[]{:S(2)}, u32[]{:S(2)}) %collective-permute-start.18) | collective-permute-done | bytes 131104 | tf_op jit(solution)/shard_map/ppermute | solution.py:610
  29.7 1.2 %shard_map.114 = (f32[5,8,32,128]{3,2,1,0:T(8,128)}, f32[5,8,32,128]{3,2,1,0:T(8,128)}) custom-call(f32[5,8,32,128]{3,2,1,0:T(8,128)S(1)} %get-tuple-element.37.conserved, f32[5,8,32,128]{3,2,1,0:T(8,128)S(1)} %shard_map.113.total, f32[8,32,128]{2,1,0:T(8,128)S(1)} %collective-permute-done.14.mate_0, f32[8,32,128]{2,1,0:T(8,128)S(1)} %collective-permute-done.15.mate_1, ...), custom_call_target="tpu_custom_call" | custom-call | bytes 3276800 | tf_op jit(solution)/shard_map/pallas_call | solution.py:507
  (29 shorter events, 0.2 us)
Async XLA Ops:
  1.8 12.7 %collective-permute-start = (f32[2,8,32,128]{3,2,1,0:T(8,128)S(1)}, f32[2,8,32,128]{3,2,1,0:T(8,128)S(1)}, u32[]{:S(2)}, u32[]{:S(2)}) collective-permute-start(f32[2,8,32,128]{3,2,1,0:T(8,128)S(1)} %get-tuple-element.38.first), channel_id=1, source_target_pairs={{0,2},{1,3},{2,0},{3,1},{4,6},{5,7},{6,4},{7,5},{8,10},{9,11},{10,... | collective-permute-start | bytes 786440 | tf_op jit(solution)/shard_map/ppermute | solution.py:548
  4.8 5.4 %copy-start.4 = (bf16[256,256]{1,0:T(8,128)(2,1)S(1)}, bf16[256,256]{1,0:T(8,128)(2,1)}, u32[]{:S(2)}) copy-start(bf16[256,256]{1,0:T(8,128)(2,1)} %constant.16.clone.y_high) | copy-start | bytes 393220
  4.8 5.4 %copy-start.5 = (bf16[256,256]{1,0:T(8,128)(2,1)S(1)}, bf16[256,256]{1,0:T(8,128)(2,1)}, u32[]{:S(2)}) copy-start(bf16[256,256]{1,0:T(8,128)(2,1)} %constant.17.clone.y_low) | copy-start | bytes 393220
  5.0 18.1 %collective-permute-start.4 = (f32[3,8,32,128]{3,2,1,0:T(8,128)S(1)}, f32[3,8,32,128]{3,2,1,0:T(8,128)S(1)}, u32[]{:S(2)}, u32[]{:S(2)}) collective-permute-start(f32[3,8,32,128]{3,2,1,0:T(8,128)S(1)} %get-tuple-element.44.second), channel_id=1, source_target_pairs={{0,2},{1,3},{2,0},{3,1},{4,6},{5,7},{6,4},{7,5},{8,10},{9,11},{10,... | collective-permute-start | bytes 1179656 | tf_op jit(solution)/shard_map/ppermute | solution.py:558
  5.1 8.1 %collective-permute-start.1 = (f32[4,2,32,128]{3,2,1,0:T(8,128)S(1)}, f32[4,2,32,128]{3,2,1,0:T(8,128)S(1)}, u32[]{:S(2)}, u32[]{:S(2)}) collective-permute-start(f32[4,2,32,128]{3,2,1,0:T(8,128)S(1)} %get-tuple-element.40), channel_id=1, source_target_pairs={{0,4},{4,8},{8,12},{12,16},{16,20},{20,24},{24,28},{28,0},{1,5},{5... | collective-permute-start | bytes 393224 | tf_op jit(solution)/shard_map/ppermute | solution.py:549
  7.1 7.4 %collective-permute-start.2 = (f32[4,2,32,128]{3,2,1,0:T(8,128)S(1)}, f32[4,2,32,128]{3,2,1,0:T(8,128)S(1)}, u32[]{:S(2)}, u32[]{:S(2)}) collective-permute-start(f32[4,2,32,128]{3,2,1,0:T(8,128)S(1)} %get-tuple-element.41), channel_id=1, source_target_pairs={{4,0},{8,4},{12,8},{16,12},{20,16},{24,20},{28,24},{0,28},{5,1},{9... | collective-permute-start | bytes 393224 | tf_op jit(solution)/shard_map/ppermute | solution.py:550
  10.2 7.2 %copy-start.3 = (bf16[2,512,256]{2,1,0:T(8,128)(2,1)S(1)}, bf16[2,512,256]{2,1,0:T(8,128)(2,1)}, u32[]{:S(2)}) copy-start(bf16[2,512,256]{2,1,0:T(8,128)(2,1)} %constant.13.clone.z_low) | copy-start | bytes 1572868
  10.9 4.6 %collective-permute-start.6 = (f32[8,32,128]{2,1,0:T(8,128)S(1)}, f32[8,32,128]{2,1,0:T(8,128)S(1)}, u32[]{:S(2)}, u32[]{:S(2)}) collective-permute-start(f32[8,32,128]{2,1,0:T(8,128)S(1)} %get-tuple-element.46), channel_id=1, source_target_pairs={{0,1},{1,0},{2,3},{3,2},{4,5},{5,4},{6,7},{7,6},{8,9},{9,8},{10,11... | collective-permute-start | bytes 393224 | tf_op jit(solution)/shard_map/ppermute | solution.py:556
  13.2 10.0 %collective-permute-start.5 = (f32[2,8,32,128]{3,2,1,0:T(8,128)S(1)}, f32[2,8,32,128]{3,2,1,0:T(8,128)S(1)}, u32[]{:S(2)}, u32[]{:S(2)}) collective-permute-start(f32[2,8,32,128]{3,2,1,0:T(8,128)S(1)} %get-tuple-element.45), channel_id=1, source_target_pairs={{0,1},{1,0},{2,3},{3,2},{4,5},{5,4},{6,7},{7,6},{8,9},{9,8},{10,11... | collective-permute-start | bytes 786440 | tf_op jit(solution)/shard_map/ppermute | solution.py:557
  14.5 1.3 %collective-permute-start.7 = (f32[8,32,128]{2,1,0:T(8,128)S(1)}, f32[8,32,128]{2,1,0:T(8,128)S(1)}, u32[]{:S(2)}, u32[]{:S(2)}) collective-permute-start(f32[8,32,128]{2,1,0:T(8,128)S(1)} %get-tuple-element.47), channel_id=1, source_target_pairs={{0,1},{1,0},{2,3},{3,2},{4,5},{5,4},{6,7},{7,6},{8,9},{9,8},{10,11... | collective-permute-start | bytes 393224 | tf_op jit(solution)/shard_map/ppermute | solution.py:556
  14.5 2.8 %copy-start = (bf16[2,256,256]{2,1,0:T(8,128)(2,1)S(1)}, bf16[2,256,256]{2,1,0:T(8,128)(2,1)}, u32[]{:S(2)}) copy-start(bf16[2,256,256]{2,1,0:T(8,128)(2,1)} %constant.14.clone.f_high) | copy-start | bytes 786436
  14.5 2.9 %copy-start.1 = (bf16[2,256,256]{2,1,0:T(8,128)(2,1)S(1)}, bf16[2,256,256]{2,1,0:T(8,128)(2,1)}, u32[]{:S(2)}) copy-start(bf16[2,256,256]{2,1,0:T(8,128)(2,1)} %constant.15.clone.f_low) | copy-start | bytes 786436
  14.5 2.9 %copy-start.2 = (bf16[2,512,256]{2,1,0:T(8,128)(2,1)S(1)}, bf16[2,512,256]{2,1,0:T(8,128)(2,1)}, u32[]{:S(2)}) copy-start(bf16[2,512,256]{2,1,0:T(8,128)(2,1)} %constant.12.clone.z_high) | copy-start | bytes 1572868
  14.9 2.5 %collective-permute-start.8 = (f32[8,32,128]{2,1,0:T(8,128)S(1)}, f32[8,32,128]{2,1,0:T(8,128)S(1)}, u32[]{:S(2)}, u32[]{:S(2)}) collective-permute-start(f32[8,32,128]{2,1,0:T(8,128)S(1)} %get-tuple-element.48), channel_id=1, source_target_pairs={{0,1},{1,0},{2,3},{3,2},{4,5},{5,4},{6,7},{7,6},{8,9},{9,8},{10,11... | collective-permute-start | bytes 393224 | tf_op jit(solution)/shard_map/ppermute | solution.py:564
  15.4 1.9 %collective-permute-start.9 = (f32[8,32,128]{2,1,0:T(8,128)S(1)}, f32[8,32,128]{2,1,0:T(8,128)S(1)}, u32[]{:S(2)}, u32[]{:S(2)}) collective-permute-start(f32[8,32,128]{2,1,0:T(8,128)S(1)} %get-tuple-element.49), channel_id=1, source_target_pairs={{0,1},{1,0},{2,3},{3,2},{4,5},{5,4},{6,7},{7,6},{8,9},{9,8},{10,11... | collective-permute-start | bytes 393224 | tf_op jit(solution)/shard_map/ppermute | solution.py:564
  15.8 10.9 %collective-permute-start.3 = (f32[2,8,32,128]{3,2,1,0:T(8,128)S(1)}, f32[2,8,32,128]{3,2,1,0:T(8,128)S(1)}, u32[]{:S(2)}, u32[]{:S(2)}) collective-permute-start(f32[2,8,32,128]{3,2,1,0:T(8,128)S(1)} %get-tuple-element.43.third), channel_id=1, source_target_pairs={{0,2},{1,3},{2,0},{3,1},{4,6},{5,7},{6,4},{7,5},{8,10},{9,11},{10,... | collective-permute-start | bytes 786440 | tf_op jit(solution)/shard_map/ppermute | solution.py:565
  18.3 9.6 %collective-permute-start.12 = (f32[5,2,32,128]{3,2,1,0:T(8,128)S(1)}, f32[5,2,32,128]{3,2,1,0:T(8,128)S(1)}, u32[]{:S(2)}, u32[]{:S(2)}) collective-permute-start(f32[5,2,32,128]{3,2,1,0:T(8,128)S(1)} %get-tuple-element.63), channel_id=1, source_target_pairs={{0,4},{4,8},{8,12},{12,16},{16,20},{20,24},{24,28},{28,0},{1,5},{5... | collective-permute-start | bytes 491528 | tf_op jit(solution)/shard_map/ppermute | solution.py:574
  19.1 9.2 %collective-permute-start.13 = (f32[5,2,32,128]{3,2,1,0:T(8,128)S(1)}, f32[5,2,32,128]{3,2,1,0:T(8,128)S(1)}, u32[]{:S(2)}, u32[]{:S(2)}) collective-permute-start(f32[5,2,32,128]{3,2,1,0:T(8,128)S(1)} %get-tuple-element.64), channel_id=1, source_target_pairs={{4,0},{8,4},{12,8},{16,12},{20,16},{24,20},{28,24},{0,28},{5,1},{9... | collective-permute-start | bytes 491528 | tf_op jit(solution)/shard_map/ppermute | solution.py:575
  23.1 2.0 %collective-permute-start.10 = (f32[8,32,128]{2,1,0:T(8,128)S(1)}, f32[8,32,128]{2,1,0:T(8,128)S(1)}, u32[]{:S(2)}, u32[]{:S(2)}) collective-permute-start(f32[8,32,128]{2,1,0:T(8,128)S(1)} %get-tuple-element.53.for_v), channel_id=1, source_target_pairs={{0,1},{1,0},{2,3},{3,2},{4,5},{5,4},{6,7},{7,6},{8,9},{9,8},{10,11... | collective-permute-start | bytes 393224 | tf_op jit(solution)/shard_map/ppermute | solution.py:577
  23.2 1.9 %collective-permute-start.11 = (f32[8,32,128]{2,1,0:T(8,128)S(1)}, f32[8,32,128]{2,1,0:T(8,128)S(1)}, u32[]{:S(2)}, u32[]{:S(2)}) collective-permute-start(f32[8,32,128]{2,1,0:T(8,128)S(1)} %get-tuple-element.54), channel_id=1, source_target_pairs={{0,1},{1,0},{2,3},{3,2},{4,5},{5,4},{6,7},{7,6},{8,9},{9,8},{10,11... | collective-permute-start | bytes 393224 | tf_op jit(solution)/shard_map/ppermute | solution.py:578
  27.3 1.6 %collective-permute-start.14 = (f32[8,32,128]{2,1,0:T(8,128)S(1)}, f32[8,32,128]{2,1,0:T(8,128)S(1)}, u32[]{:S(2)}, u32[]{:S(2)}) collective-permute-start(f32[8,32,128]{2,1,0:T(8,128)S(1)} %get-tuple-element.65), channel_id=1, source_target_pairs={{0,1},{1,0},{2,3},{3,2},{4,5},{5,4},{6,7},{7,6},{8,9},{9,8},{10,11... | collective-permute-start | bytes 393224 | tf_op jit(solution)/shard_map/ppermute | solution.py:610
  27.4 1.4 %collective-permute-start.15 = (f32[8,32,128]{2,1,0:T(8,128)S(1)}, f32[8,32,128]{2,1,0:T(8,128)S(1)}, u32[]{:S(2)}, u32[]{:S(2)}) collective-permute-start(f32[8,32,128]{2,1,0:T(8,128)S(1)} %get-tuple-element.66), channel_id=1, source_target_pairs={{0,1},{1,0},{2,3},{3,2},{4,5},{5,4},{6,7},{7,6},{8,9},{9,8},{10,11... | collective-permute-start | bytes 393224 | tf_op jit(solution)/shard_map/ppermute | solution.py:610
  27.8 1.3 %collective-permute-start.16 = (f32[8,32,128]{2,1,0:T(8,128)S(1)}, f32[8,32,128]{2,1,0:T(8,128)S(1)}, u32[]{:S(2)}, u32[]{:S(2)}) collective-permute-start(f32[8,32,128]{2,1,0:T(8,128)S(1)} %get-tuple-element.67), channel_id=1, source_target_pairs={{0,1},{1,0},{2,3},{3,2},{4,5},{5,4},{6,7},{7,6},{8,9},{9,8},{10,11... | collective-permute-start | bytes 393224 | tf_op jit(solution)/shard_map/ppermute | solution.py:610
  27.9 1.4 %collective-permute-start.17 = (f32[8,32,128]{2,1,0:T(8,128)S(1)}, f32[8,32,128]{2,1,0:T(8,128)S(1)}, u32[]{:S(2)}, u32[]{:S(2)}) collective-permute-start(f32[8,32,128]{2,1,0:T(8,128)S(1)} %get-tuple-element.68), channel_id=1, source_target_pairs={{0,1},{1,0},{2,3},{3,2},{4,5},{5,4},{6,7},{7,6},{8,9},{9,8},{10,11... | collective-permute-start | bytes 393224 | tf_op jit(solution)/shard_map/ppermute | solution.py:610
  28.4 1.3 %collective-permute-start.18 = (f32[8,32,128]{2,1,0:T(8,128)S(1)}, f32[8,32,128]{2,1,0:T(8,128)S(1)}, u32[]{:S(2)}, u32[]{:S(2)}) collective-permute-start(f32[8,32,128]{2,1,0:T(8,128)S(1)} %get-tuple-element.69), channel_id=1, source_target_pairs={{0,1},{1,0},{2,3},{3,2},{4,5},{5,4},{6,7},{7,6},{8,9},{9,8},{10,11... | collective-permute-start | bytes 393224 | tf_op jit(solution)/shard_map/ppermute | solution.py:610
